TPU v7x, 32 devices: a whole 2x2x4 slice. The times are simulated.
32 devices in a mesh: leaf: 8 (over z, y), sub: 4 (over x, core).
Axes of the slice: x: 2, y: 2, z: 4, core: 2. Of those that a mesh axis runs over, the one named last changes fastest.
Arguments:
- start_vec: float32 [128, 256], P(('leaf', 'sub')), as said below
- near_blocks: bfloat16 [128, 2, 256, 256], P(('leaf', 'sub')), may hold values from -0.25 to 0.25
- near_ids: int32 [128, 1], P(('leaf', 'sub')), may hold values from 0 to 47
- far_ids: int32 [128, 2], P(('leaf', 'sub')), may hold values from 0 to 15
- leaf_basis: bfloat16 [128, 64, 256], P(('leaf', 'sub')), may hold values from -0.375 to 0.375
- leaf_coupling: bfloat16 [128, 64, 128], P(('leaf', 'sub')), may hold values from -0.5 to 0.5
- node_transfer: bfloat16 [32, 64, 256], P(('leaf', 'sub')), may hold values from -0.375 to 0.375
- branch_transfer: bfloat16 [32, 64, 64], P(('leaf', 'sub')), may hold values from -0.75 to 0.75
- top_ids: int32 [8, 4], P('leaf'), may hold values from 0 to 7
- top_coupling: bfloat16 [8, 64, 256], P('leaf'), may hold values from -0.375 to 0.375
Outputs:
- basis: float32 [4, 128, 256], P(None, ('leaf', 'sub'))
- hessen: float32 [4, 3], replicated
Inputs may be any that keep to these rules, and one draw needn't show every extreme that they name: start_vec is real-valued with entries of order one.
All inputs are finite; a program needn't handle non-finite values.
Results may differ from a plain program's by a relative error of at most 0.02.
Values may be sent and summed in bfloat16 or wider, within the bound.
No kernel may reach another device: no remote copies, remote signals or barrier semaphores. Data moves between devices by JAX's collectives and lax.ppermute only.
A program may use at most 64 MiB of HBM per device.

v0:
```python
import jax
import jax.numpy as jnp
from jax import lax
from jax.sharding import PartitionSpec as P

MATVECS = 3


def with_halo(cells, sides, width):
    for axis, dim in sides:
        count = lax.axis_size(axis)
        ends = count - 1
        head = lax.slice_in_dim(cells, 0, width, axis=dim)
        tail = lax.slice_in_dim(cells, cells.shape[dim] - width, cells.shape[dim], axis=dim)
        cells = jnp.concatenate(
            [
                lax.ppermute(tail, axis, [(i, (i + 1) % count) for i in range(ends)]),
                cells,
                lax.ppermute(head, axis, [((i + 1) % count, i) for i in range(ends)]),
            ],
            axis=dim,
        )
    return cells


def apply_matrix(
    vector,
    near_blocks,
    near_ids,
    far_ids,
    leaf_basis,
    leaf_coupling,
    node_transfer,
    branch_transfer,
    top_ids,
    top_coupling,
):
    highest = lax.Precision.HIGHEST
    leaves = vector.shape[0]
    branches = lax.axis_size("leaf")
    rank = leaf_basis.shape[1]
    vec_bf = vector.astype(jnp.bfloat16)
    coef_bf = jnp.einsum(
        "lrk,lk->lr", leaf_basis, vec_bf, preferred_element_type=jnp.float32
    ).astype(jnp.bfloat16)
    node_coef = jnp.dot(node_transfer[0], coef_bf.reshape(-1), preferred_element_type=jnp.float32)
    upper_f = branch_transfer[0].astype(jnp.float32)
    node_term = jnp.dot(upper_f, node_coef, precision=highest).astype(jnp.bfloat16)[None, :]
    branch_leafc, branch_terms = (
        lax.all_gather(coef_bf, "sub", axis=0, tiled=True),
        lax.all_gather(node_term, "sub", axis=0, tiled=True),
    )
    own_coef = jnp.sum(branch_terms.astype(jnp.float32), axis=0).astype(jnp.bfloat16)
    branch_table = lax.all_gather(own_coef[None, :], "leaf", axis=0, tiled=True)
    branch_vec = lax.all_gather(vec_bf, "sub", axis=0, tiled=True)
    neighbours = with_halo(branch_vec, (("leaf", 0),), branch_vec.shape[0])
    picked = neighbours[near_ids]
    near_input = jnp.concatenate([vec_bf[:, None, :], picked], axis=1)
    near_out = jnp.einsum(
        "lsij,lsj->li", near_blocks, near_input, preferred_element_type=jnp.float32
    )
    far_coef = branch_leafc[far_ids].reshape(leaves, -1)
    leaf_far = jnp.einsum("lrk,lk->lr", leaf_coupling, far_coef, preferred_element_type=jnp.float32)
    selector = (top_ids[0][:, None] == jnp.arange(branches, dtype=jnp.int32)[None, :]).astype(
        jnp.bfloat16
    )
    partners = jnp.dot(selector, branch_table, preferred_element_type=jnp.float32).astype(
        jnp.bfloat16
    )
    branch_local = jnp.dot(
        top_coupling[0], partners.reshape(-1), preferred_element_type=jnp.float32
    )
    node_local = jnp.dot(branch_local, upper_f, precision=highest)
    leaf_down = jnp.dot(
        node_local, node_transfer[0].astype(jnp.float32), precision=highest
    ).reshape(leaves, rank)
    local_coef = (leaf_down + leaf_far).astype(jnp.bfloat16)
    far_out = jnp.einsum("lrk,lr->lk", leaf_basis, local_coef, preferred_element_type=jnp.float32)
    return 0.5 * vector + near_out + far_out


def per_device(
    start_vec,
    near_blocks,
    near_ids,
    far_ids,
    leaf_basis,
    leaf_coupling,
    node_transfer,
    branch_transfer,
    top_ids,
    top_coupling,
):
    total = float(
        start_vec.shape[0] * start_vec.shape[1] * lax.axis_size("leaf") * lax.axis_size("sub")
    )
    start_sum = lax.psum(jnp.sum(start_vec * start_vec), ("leaf", "sub"))
    first = start_vec * lax.rsqrt(start_sum / total + 1e-06)
    vectors = [first]
    hessen = jnp.zeros((MATVECS + 1, MATVECS), jnp.float32)
    for column in range(MATVECS):
        image = apply_matrix(
            vectors[column],
            near_blocks,
            near_ids,
            far_ids,
            leaf_basis,
            leaf_coupling,
            node_transfer,
            branch_transfer,
            top_ids,
            top_coupling,
        )
        partial_dots = jnp.stack([jnp.sum(earlier * image) for earlier in vectors])
        dot_sums, square_sum = lax.psum((partial_dots, jnp.sum(image * image)), ("leaf", "sub"))
        dots = dot_sums / total
        square = square_sum / total
        remain = square - jnp.sum(dots * dots)
        scale = jnp.sqrt(jnp.maximum(remain, 0.01 * square))
        update = image
        for index_i in range(column + 1):
            update = update - dots[index_i] * vectors[index_i]
        vectors.append(update / scale)
        hessen = hessen.at[: column + 1, column].set(dots)
        hessen = hessen.at[column + 1, column].set(scale)
    return (jnp.stack(vectors), hessen)


def solution(mesh):
    placed = (
        P(("leaf", "sub"), None),
        P(("leaf", "sub"), None, None, None),
        P(("leaf", "sub"), None),
        P(("leaf", "sub"), None),
        P(("leaf", "sub"), None, None),
        P(("leaf", "sub"), None, None),
        P(("leaf", "sub"), None, None),
        P(("leaf", "sub"), None, None),
        P("leaf", None),
        P("leaf", None, None),
    )
    return jax.shard_map(
        per_device,
        mesh=mesh,
        in_specs=placed,
        out_specs=(P(None, ("leaf", "sub"), None), P()),
        check_vma=False,
    )
```

profile of v0, /device:TPU:0, one launch (start us, length us, event | category | flops | bytes accessed | tf_op | source)
XLA Modules:
  0.0 332.2 jit_solution(8254820614206892239)
XLA Ops:
  0.6 1.4 multiply_reduce_fusion.9
  2.0 42.2 %psum.49 = f32[]{:T(128)} all-reduce(f32[]{:T(128)} %multiply_reduce_fusion.9), channel_id=1, replica_groups=mesh['leaf'=8,'sub'=4] {'leaf','sub'}, use_global_device_ids=true, to_apply=%region_1.0 | all-reduce | flops 1 | bytes 8 | tf_op jit(solution)/shard_map/psum | solution.py:97
  44.9 5.4 %all-gather.6 = bf16[4,4,256]{2,1,0:T(4,128)(2,1)S(1)} all-gather(bf16[1,4,256]{2,1,0:T(4,128)(2,1)S(1)} %get-tuple-element.107), channel_id=1, replica_groups=mesh['leaf'=8,'sub'=4] {'sub'}, dimensions={0}, use_global_device_ids=true | all-gather | bytes 10240 | tf_op jit(solution)/shard_map/all_gather | solution.py:55
  50.4 1.3 collective-permute-start.1
  51.7 4.7 %collective-permute-start = (bf16[16,256]{1,0:T(8,128)(2,1)S(1)}, bf16[16,256]{1,0:T(8,128)(2,1)S(1)}, u32[]{:S(2)}, u32[]{:S(2)}) collective-permute-start(bf16[16,256]{1,0:T(8,128)(2,1)S(1)} %reshape.327), channel_id=1, source_target_pairs={{0,4},{4,8},{8,12},{12,16},{16,20},{20,24},{24,28},{1,5},{5,9},{9,... | collective-permute-start | bytes 24584 | tf_op jit(solution)/shard_map/ppermute | solution.py:17
  56.4 1.0 fusion.31
  57.7 0.6 copy-done.7
  58.4 0.7 copy-done.11
  59.1 0.6 dynamic-slice.49
  60.6 6.8 %all-reduce.1 = bf16[256]{0:T(256)(128)(2,1)S(1)} all-reduce(bf16[256]{0:T(256)(128)(2,1)S(1)} %dynamic-update-slice.12), channel_id=2, replica_groups=mesh['leaf'=8,'sub'=4] {'sub'}, use_global_device_ids=true, to_apply=%add.1 | all-reduce | flops 256 | bytes 1024
  68.1 0.6 dynamic-slice.50
  69.6 19.1 %all-reduce.2 = bf16[512]{0:T(512)(128)(2,1)S(1)} all-reduce(bf16[512]{0:T(512)(128)(2,1)S(1)} %dynamic-update-slice.13), channel_id=3, replica_groups=mesh['leaf'=8,'sub'=4] {'leaf'}, use_global_device_ids=true, to_apply=%add.2 | all-reduce | flops 512 | bytes 2048
  90.0 5.2 %all-gather.7 = bf16[4,4,64]{2,1,0:T(4,128)(2,1)S(1)} all-gather(bf16[1,4,64]{2,1,0:T(4,128)(2,1)S(1)} %convert_bitcast_fusion.11), channel_id=1, replica_groups=mesh['leaf'=8,'sub'=4] {'sub'}, dimensions={0}, use_global_device_ids=true | all-gather | bytes 2560 | tf_op jit(solution)/shard_map/all_gather | solution.py:50
  97.0 0.6 fusion.48
  97.7 0.7 and_reduce_fusion
  99.0 0.6 compare_reduce_fusion
  100.6 0.7 multiply_reduce_fusion.8
  101.3 37.1 %all-reduce.9 = (f32[]{:T(128)}, f32[1]{0:T(128)}) all-reduce(f32[]{:T(128)} %get-tuple-element.90, f32[1]{0:T(128)} %bitcast.32), channel_id=1, replica_groups=mesh['leaf'=8,'sub'=4] {'leaf','sub'}, use_global_device_ids=true, to_apply=%region_6.0 | all-reduce | flops 2 | bytes 16 | tf_op jit(solution)/shard_map/psum | solution.py:115
  141.7 5.5 %all-gather.8 = bf16[4,4,256]{2,1,0:T(4,128)(2,1)S(1)} all-gather(bf16[1,4,256]{2,1,0:T(4,128)(2,1)S(1)} %get-tuple-element.110), channel_id=1, replica_groups=mesh['leaf'=8,'sub'=4] {'sub'}, dimensions={0}, use_global_device_ids=true | all-gather | bytes 10240 | tf_op jit(solution)/shard_map/all_gather | solution.py:55
  147.2 1.3 collective-permute-start.3
  148.4 4.8 %collective-permute-start.2 = (bf16[16,256]{1,0:T(8,128)(2,1)S(1)}, bf16[16,256]{1,0:T(8,128)(2,1)S(1)}, u32[]{:S(2)}, u32[]{:S(2)}) collective-permute-start(bf16[16,256]{1,0:T(8,128)(2,1)S(1)} %reshape.331), channel_id=1, source_target_pairs={{0,4},{4,8},{8,12},{12,16},{16,20},{20,24},{24,28},{1,5},{5,9},{9,... | collective-permute-start | bytes 24584 | tf_op jit(solution)/shard_map/ppermute | solution.py:17
  153.8 6.7 %all-reduce.3 = bf16[256]{0:T(256)(128)(2,1)S(1)} all-reduce(bf16[256]{0:T(256)(128)(2,1)S(1)} %dynamic-update-slice.14), channel_id=4, replica_groups=mesh['leaf'=8,'sub'=4] {'sub'}, use_global_device_ids=true, to_apply=%add.3 | all-reduce | flops 256 | bytes 1024
  160.9 20.0 %all-reduce.4 = bf16[512]{0:T(512)(128)(2,1)S(1)} all-reduce(bf16[512]{0:T(512)(128)(2,1)S(1)} %dynamic-update-slice.15), channel_id=5, replica_groups=mesh['leaf'=8,'sub'=4] {'leaf'}, use_global_device_ids=true, to_apply=%add.4 | all-reduce | flops 512 | bytes 2048
  181.7 5.1 %all-gather.9 = bf16[4,4,64]{2,1,0:T(4,128)(2,1)S(1)} all-gather(bf16[1,4,64]{2,1,0:T(4,128)(2,1)S(1)} %convert_bitcast_fusion.10), channel_id=1, replica_groups=mesh['leaf'=8,'sub'=4] {'sub'}, dimensions={0}, use_global_device_ids=true | all-gather | bytes 2560 | tf_op jit(solution)/shard_map/all_gather | solution.py:50
  188.8 0.7 multiply_reduce_fusion.6
  189.5 1.3 pad_maximum_fusion.4
  190.8 37.0 %all-reduce.8 = (f32[]{:T(128)}, f32[2]{0:T(128)S(1)}) all-reduce(f32[]{:T(128)} %get-tuple-element.87, f32[2]{0:T(128)S(1)} %pad_maximum_fusion.4), channel_id=1, replica_groups=mesh['leaf'=8,'sub'=4] {'leaf','sub'}, use_global_device_ids=true, to_apply=%region_12.0 | all-reduce | flops 3 | bytes 24 | tf_op jit(solution)/shard_map/psum | solution.py:115
  229.2 0.6 broadcast_multiply_fusion.2
  230.4 0.6 fusion.50
  231.0 1.3 convert_bitcast_fusion.2
  232.5 5.5 %all-gather.10 = bf16[4,4,256]{2,1,0:T(4,128)(2,1)S(1)} all-gather(bf16[1,4,256]{2,1,0:T(4,128)(2,1)S(1)} %get-tuple-element.108), channel_id=1, replica_groups=mesh['leaf'=8,'sub'=4] {'sub'}, dimensions={0}, use_global_device_ids=true | all-gather | bytes 10240 | tf_op jit(solution)/shard_map/all_gather | solution.py:55
  237.9 1.3 collective-permute-start.5
  239.2 4.8 %collective-permute-start.4 = (bf16[16,256]{1,0:T(8,128)(2,1)S(1)}, bf16[16,256]{1,0:T(8,128)(2,1)S(1)}, u32[]{:S(2)}, u32[]{:S(2)}) collective-permute-start(bf16[16,256]{1,0:T(8,128)(2,1)S(1)} %reshape.335), channel_id=1, source_target_pairs={{0,4},{4,8},{8,12},{12,16},{16,20},{20,24},{24,28},{1,5},{5,9},{9,... | collective-permute-start | bytes 24584 | tf_op jit(solution)/shard_map/ppermute | solution.py:17
  244.6 6.7 %all-reduce.5 = bf16[256]{0:T(256)(128)(2,1)S(1)} all-reduce(bf16[256]{0:T(256)(128)(2,1)S(1)} %dynamic-update-slice.16), channel_id=6, replica_groups=mesh['leaf'=8,'sub'=4] {'sub'}, use_global_device_ids=true, to_apply=%add.5 | all-reduce | flops 256 | bytes 1024
  251.7 19.8 %all-reduce.6 = bf16[512]{0:T(512)(128)(2,1)S(1)} all-reduce(bf16[512]{0:T(512)(128)(2,1)S(1)} %dynamic-update-slice.17), channel_id=7, replica_groups=mesh['leaf'=8,'sub'=4] {'leaf'}, use_global_device_ids=true, to_apply=%add.6 | all-reduce | flops 512 | bytes 2048
  272.2 5.1 %all-gather.11 = bf16[4,4,64]{2,1,0:T(4,128)(2,1)S(1)} all-gather(bf16[1,4,64]{2,1,0:T(4,128)(2,1)S(1)} %convert_bitcast_fusion.9), channel_id=1, replica_groups=mesh['leaf'=8,'sub'=4] {'sub'}, dimensions={0}, use_global_device_ids=true | all-gather | bytes 2560 | tf_op jit(solution)/shard_map/all_gather | solution.py:50
  278.2 1.9 broadcast_select_fusion.1
  280.2 1.4 scatter.24
  282.7 0.7 multiply_reduce_fusion.3
  283.4 2.0 pad_maximum_fusion.5
  285.3 37.1 %all-reduce.7 = (f32[]{:T(128)}, f32[3]{0:T(128)S(1)}) all-reduce(f32[]{:T(128)} %get-tuple-element.83, f32[3]{0:T(128)S(1)} %pad_maximum_fusion.5), channel_id=1, replica_groups=mesh['leaf'=8,'sub'=4] {'leaf','sub'}, use_global_device_ids=true, to_apply=%region_20.0 | all-reduce | flops 4 | bytes 32 | tf_op jit(solution)/shard_map/psum | solution.py:115
  323.7 0.6 broadcast_multiply_fusion.1
  325.0 0.6 fusion.49
  325.6 2.0 broadcast_select_fusion
  327.6 1.3 scatter.26
  329.1 0.7 copy.19
  329.7 1.9 divide_bitcast_fusion
  331.6 0.6 pad_maximum_fusion.3
  (131 shorter events, 14.0 us)
Async XLA Ops:
  0.6 99.6 %copy-start = (bf16[4,2,256,256]{3,2,1,0:T(8,128)(2,1)S(1)}, bf16[4,2,256,256]{3,2,1,0:T(8,128)(2,1)}, u32[]{:S(2)}) copy-start(bf16[4,2,256,256]{3,2,1,0:T(8,128)(2,1)} %param.23) | copy-start | bytes 3145732
  2.0 42.9 %copy-start.2 = (f32[4,256]{1,0:T(4,128)S(1)}, f32[4,256]{1,0:T(4,128)}, u32[]{:S(2)}) copy-start(f32[4,256]{1,0:T(4,128)} %param.22) | copy-start | bytes 12292
  50.4 49.3 %collective-permute-start.1 = (bf16[16,256]{1,0:T(8,128)(2,1)S(1)}, bf16[16,256]{1,0:T(8,128)(2,1)S(1)}, u32[]{:S(2)}, u32[]{:S(2)}) collective-permute-start(bf16[16,256]{1,0:T(8,128)(2,1)S(1)} %reshape.327), channel_id=1, source_target_pairs={{4,0},{8,4},{12,8},{16,12},{20,16},{24,20},{28,24},{5,1},{9,5},{13... | collective-permute-start | bytes 24584 | tf_op jit(solution)/shard_map/ppermute | solution.py:19
  51.7 48.0 %collective-permute-start = (bf16[16,256]{1,0:T(8,128)(2,1)S(1)}, bf16[16,256]{1,0:T(8,128)(2,1)S(1)}, u32[]{:S(2)}, u32[]{:S(2)}) collective-permute-start(bf16[16,256]{1,0:T(8,128)(2,1)S(1)} %reshape.327), channel_id=1, source_target_pairs={{0,4},{4,8},{8,12},{12,16},{16,20},{20,24},{24,28},{1,5},{5,9},{9,... | collective-permute-start | bytes 24584 | tf_op jit(solution)/shard_map/ppermute | solution.py:17
  56.4 1.2 copy-start.3
  57.6 0.7 copy-start.7
  58.4 0.7 copy-start.11
  67.4 0.7 copy-start.10
  88.7 0.7 copy-start.9
  88.8 0.8 copy-start.6
  89.7 5.5 %copy-start.4 = (s32[4,2]{0,1:T(2,128)S(1)}, s32[4,2]{0,1:T(2,128)}, u32[]{:S(2)}) copy-start(s32[4,2]{0,1:T(2,128)} %param.25) | copy-start | bytes 100
  89.9 6.5 %copy-start.1 = (bf16[4,64,256]{2,1,0:T(8,128)(2,1)S(1)}, bf16[4,64,256]{2,1,0:T(8,128)(2,1)}, u32[]{:S(2)}) copy-start(bf16[4,64,256]{2,1,0:T(8,128)(2,1)} %param.26) | copy-start | bytes 393220
  90.0 6.2 %copy-start.5 = (bf16[4,64,128]{2,1,0:T(8,128)(2,1)S(1)}, bf16[4,64,128]{2,1,0:T(8,128)(2,1)}, u32[]{:S(2)}) copy-start(bf16[4,64,128]{2,1,0:T(8,128)(2,1)} %param.27) | copy-start | bytes 196612
  96.4 0.7 copy-start.8
  97.0 0.7 copy-start.12
  147.2 40.7 %collective-permute-start.3 = (bf16[16,256]{1,0:T(8,128)(2,1)S(1)}, bf16[16,256]{1,0:T(8,128)(2,1)S(1)}, u32[]{:S(2)}, u32[]{:S(2)}) collective-permute-start(bf16[16,256]{1,0:T(8,128)(2,1)S(1)} %reshape.331), channel_id=1, source_target_pairs={{4,0},{8,4},{12,8},{16,12},{20,16},{24,20},{28,24},{5,1},{9,5},{13... | collective-permute-start | bytes 24584 | tf_op jit(solution)/shard_map/ppermute | solution.py:19
  148.4 39.4 %collective-permute-start.2 = (bf16[16,256]{1,0:T(8,128)(2,1)S(1)}, bf16[16,256]{1,0:T(8,128)(2,1)S(1)}, u32[]{:S(2)}, u32[]{:S(2)}) collective-permute-start(bf16[16,256]{1,0:T(8,128)(2,1)S(1)} %reshape.331), channel_id=1, source_target_pairs={{0,4},{4,8},{8,12},{12,16},{16,20},{20,24},{24,28},{1,5},{5,9},{9,... | collective-permute-start | bytes 24584 | tf_op jit(solution)/shard_map/ppermute | solution.py:17
  237.9 43.8 %collective-permute-start.5 = (bf16[16,256]{1,0:T(8,128)(2,1)S(1)}, bf16[16,256]{1,0:T(8,128)(2,1)S(1)}, u32[]{:S(2)}, u32[]{:S(2)}) collective-permute-start(bf16[16,256]{1,0:T(8,128)(2,1)S(1)} %reshape.335), channel_id=1, source_target_pairs={{4,0},{8,4},{12,8},{16,12},{20,16},{24,20},{28,24},{5,1},{9,5},{13... | collective-permute-start | bytes 24584 | tf_op jit(solution)/shard_map/ppermute | solution.py:19
  239.2 42.5 %collective-permute-start.4 = (bf16[16,256]{1,0:T(8,128)(2,1)S(1)}, bf16[16,256]{1,0:T(8,128)(2,1)S(1)}, u32[]{:S(2)}, u32[]{:S(2)}) collective-permute-start(bf16[16,256]{1,0:T(8,128)(2,1)S(1)} %reshape.335), channel_id=1, source_target_pairs={{0,4},{4,8},{8,12},{12,16},{16,20},{20,24},{24,28},{1,5},{5,9},{9,... | collective-permute-start | bytes 24584 | tf_op jit(solution)/shard_map/ppermute | solution.py:17
where the time goes:
time: 335 us; the launch traced here: 332 us
  blocking collectives  264 us (79%)
  starting transfers between devices  18.1 us (5%)
  other arithmetic  17.2 us (5%)
  local copies, waits for them, and re-layouts  16.9 us (5%)
  between operations  10 us (3%)
  matrix products  5.72 us (2%)
    psum x3, blocking collectives, per_device(): lax.psum((partial_dots, jnp.sum(image * image)), ('leaf', 'sub'))  111 us
    unnamed x6, blocking collectives  79.2 us
    psum x1, blocking collectives, per_device(): start_sum = lax.psum(jnp.sum(start_vec * start_vec), ('leaf', 'sub'))  42.2 us
    all_gather x3, blocking collectives, apply_matrix(): branch_vec = lax.all_gather(vec_bf, 'sub', axis=0, tiled=True)  16.3 us
    all_gather x3, blocking collectives, apply_matrix(): lax.all_gather(coef_bf, 'sub', axis=0, tiled=True)  15.3 us
    ppermute x3, starting transfers between devices, with_halo(): lax.ppermute(tail, axis, [(i, (i + 1) % count) for i in range(ends)])  14.3 us
  transfers between devices with their start and end apart: 6, of which 0 were waited for; matrix products, arithmetic and copies ran while one was open for 5% of the time, Pallas kernels for 0%

commit v1 on v0

v1 whole, which is shorter than its diff:
```python
import jax
import jax.numpy as jnp
from jax import lax
from jax.experimental import pallas as pl
from jax.experimental.pallas import tpu as pltpu
from jax.sharding import PartitionSpec as P

F32 = jnp.float32
BF16 = jnp.bfloat16
ROWS = 8
VMEM = pl.BlockSpec(memory_space=pltpu.VMEM)
SMEM = pl.BlockSpec(memory_space=pltpu.SMEM)


def dot_nt(a, b):
    return lax.dot_general(a, b, (((1,), (1,)), ((), ())), preferred_element_type=F32)


def dot_nn(a, b):
    return lax.dot_general(a, b, (((1,), (0,)), ((), ())), preferred_element_type=F32)


def dot_tn(a, b):
    return lax.dot_general(a, b, (((0,), (0,)), ((), ())), preferred_element_type=F32)


def iota(shape, dim):
    return lax.broadcasted_iota(jnp.int32, shape, dim)


def twice(rows):
    return jnp.concatenate([rows, rows], axis=0)


def by_leaf(parts):
    row = iota(parts[0].shape, 0) % len(parts)
    total = parts[-1]
    for leaf in range(len(parts) - 1):
        total = jnp.where(row == leaf, parts[leaf], total)
    return total


def in_lanes(values):
    group = iota((ROWS, 128), 1) // 32
    out = jnp.zeros((ROWS, 128), F32)
    for index, value in enumerate(values):
        out = jnp.where(group == index, value, out)
    return out


def inner(a, b):
    prod = a * b
    prod = prod[:, :128] + prod[:, 128:]
    return 0.5 * jnp.sum(jnp.sum(prod, axis=0, keepdims=True), axis=1, keepdims=True)


def write_block(vec, dots, basis2_ref, down_ref, out_ref):
    leaves = basis2_ref.shape[0]
    vec_bf = vec.astype(BF16)
    coef = by_leaf([dot_nt(vec_bf, basis2_ref[l]) for l in range(leaves)])
    term = jnp.zeros((ROWS, 128), F32)
    for l in range(leaves):
        one = jnp.broadcast_to(vec[l : l + 1, :], vec.shape).astype(BF16)
        term = term + dot_nt(one, down_ref[l])
    val = in_lanes(dots)
    rest = val - val.astype(BF16).astype(F32)
    last = rest - rest.astype(BF16).astype(F32)
    row = iota((ROWS, 128), 0)
    left = jnp.where(row < 4, vec[:, :128], coef)
    right = jnp.where(row == 4, term, jnp.where(row == 5, val, jnp.where(row == 6, rest, last)))
    right = jnp.where(row < 4, vec[:, 128:], right)
    block = twice(jnp.concatenate([left, right], axis=1)).astype(BF16)
    pairs = out_ref.shape[0] // 16
    if pairs <= 32:
        for p in range(pairs):
            out_ref[16 * p : 16 * p + 16, :] = block
    else:

        def store(p, carry):
            out_ref[pl.ds(pl.multiple_of(16 * p, 16), 16), :] = block
            return carry

        lax.fori_loop(0, pairs, store, 0)


def first_kernel(
    subs,
    near_ids,
    far_ids,
    top_ids,
    place,
    start_ref,
    basis_ref,
    node_ref,
    upper_ref,
    top_ref,
    block_ref,
    pick_ref,
    down_ref,
    top_down_ref,
    basis2_ref,
):
    leaves, rank, _ = basis_ref.shape
    node = node_ref[0]
    reach = dot_nn(upper_ref[0], node).astype(BF16)
    top_down_ref[...] = dot_tn(reach, top_ref[0]).astype(BF16)
    for l in range(leaves):
        own = basis_ref[l]
        basis2_ref[l] = twice(own)
        part = dot_nn(reach[:, l * rank : (l + 1) * rank], own).astype(BF16)
        down_ref[l] = twice(part)
    branch = place[0]
    width = pick_ref.shape[1]
    col = iota((ROWS, width), 1)
    row4 = iota((ROWS, width), 0) % leaves

    def leaf_column(leaf_index, offset):
        return (leaf_index // leaves) * ROWS + leaf_index % leaves + offset

    def pick(columns):
        want = columns[leaves - 1]
        for l in range(leaves - 1):
            want = jnp.where(row4 == l, columns[l], want)
        return (col == want).astype(F32)

    branch_leaves = subs * leaves
    count = (width // ROWS) * leaves
    near = []
    for l in range(leaves):
        index = (branch - 1) * branch_leaves + near_ids[l, 0]
        inside = (index >= 0) & (index < count)
        near.append(jnp.where(inside, leaf_column(jnp.maximum(index, 0), 0), -1))
    groups = [pick(near)]
    for s in range(2):
        groups.append(
            pick([leaf_column(branch * branch_leaves + far_ids[l, s], leaves) for l in range(leaves)])
        )
    for s in range(4):
        groups.append(((col % ROWS == 4) & (col // (ROWS * subs) == top_ids[0, s])).astype(F32))
    groups.append((col % ROWS >= 5).astype(F32))
    pick_ref[...] = jnp.concatenate(groups, axis=0).astype(BF16)
    start = twice(start_ref[...])
    write_block(start, [inner(start, start)], basis2_ref, down_ref, block_ref)


def multiply(own, got_ref, pick_ref, near_ref, top_down_ref, coupling_ref, basis_ref):
    leaves, rank, size = basis_ref.shape
    got = dot_nn(pick_ref[...], got_ref[...])
    group = [got[ROWS * g : ROWS * g + ROWS, :] for g in range(8)]
    low = iota((ROWS, 128), 1) < rank
    far_in = jnp.where(low, group[1][:, :128], group[2][:, :128]).astype(BF16)
    top_a = jnp.where(low, group[3][:, 128:], group[4][:, 128:]).astype(BF16)
    top_b = jnp.where(low, group[5][:, 128:], group[6][:, 128:]).astype(BF16)
    top_in = jnp.concatenate([top_a, top_b], axis=1)
    local = dot_nt(far_in, coupling_ref[...].reshape(leaves * rank, -1))
    local = local + dot_nt(top_in, top_down_ref[...])
    mine = iota((ROWS, leaves * rank), 1) // rank == iota((ROWS, leaves * rank), 0) % leaves
    local = jnp.where(mine, local, 0.0).astype(BF16)
    far_out = dot_nn(local, basis_ref[...].reshape(leaves * rank, size))
    own_bf = own.astype(BF16)
    other = group[0].astype(BF16)
    near_out = by_leaf(
        [dot_nt(own_bf, near_ref[l, 0]) + dot_nt(other, near_ref[l, 1]) for l in range(leaves)]
    )
    dots = [group[7][:, 128 + 32 * i : 129 + 32 * i] for i in range(4)]
    return near_out + far_out, dots


def entry(table, i, j, value):
    row, lane = iota(table.shape, 0), iota(table.shape, 1)
    return jnp.where((row == i) & (lane == j), value, table)


def norm_of(square, heads):
    remain = square
    for head in heads:
        remain = remain - head * head
    return jnp.sqrt(jnp.maximum(remain, 0.01 * square))


def second_kernel(
    total,
    start_ref,
    got_ref,
    pick_ref,
    near_ref,
    top_down_ref,
    coupling_ref,
    basis_ref,
    basis2_ref,
    down_ref,
    block_ref,
    b0_ref,
    k1_ref,
):
    start = twice(start_ref[...])
    image, dots = multiply(
        start, got_ref, pick_ref, near_ref, top_down_ref, coupling_ref, basis_ref
    )
    scale = lax.rsqrt(dots[0] / total + 1e-06)
    b0 = scale * start
    k1 = scale * image
    w0 = 0.5 * b0 + k1
    b0_ref[...] = b0
    k1_ref[...] = k1
    write_block(k1, [inner(b0, w0), inner(w0, w0)], basis2_ref, down_ref, block_ref)


def third_kernel(
    total,
    b0_ref,
    k1_ref,
    got_ref,
    pick_ref,
    near_ref,
    top_down_ref,
    coupling_ref,
    basis_ref,
    basis2_ref,
    down_ref,
    block_ref,
    b1_ref,
    k2_ref,
    table_ref,
):
    k1 = k1_ref[...]
    image, dots = multiply(k1, got_ref, pick_ref, near_ref, top_down_ref, coupling_ref, basis_ref)
    b0 = b0_ref[...]
    h00 = dots[0] / total
    h10 = norm_of(dots[1] / total, [h00])
    inv = 1.0 / h10
    shift = 0.5 - h00
    b1 = (shift * b0 + k1) * inv
    k2 = (shift * k1 + image) * inv
    w1 = 0.5 * b1 + k2
    b1_ref[...] = b1
    k2_ref[...] = k2
    table = jnp.zeros((ROWS, 128), F32)
    table = entry(table, 0, 0, h00)
    table_ref[...] = entry(table, 1, 0, h10)
    write_block(
        k2, [inner(b0, w1), inner(b1, w1), inner(w1, w1)], basis2_ref, down_ref, block_ref
    )


def fourth_kernel(
    total,
    b0_ref,
    k1_ref,
    b1_ref,
    k2_ref,
    table_in_ref,
    got_ref,
    pick_ref,
    near_ref,
    top_down_ref,
    coupling_ref,
    basis_ref,
    dots_ref,
    b2_ref,
    w2_ref,
    table_ref,
):
    k2 = k2_ref[...]
    image, dots = multiply(k2, got_ref, pick_ref, near_ref, top_down_ref, coupling_ref, basis_ref)
    b0, k1, b1 = b0_ref[...], k1_ref[...], b1_ref[...]
    h01 = dots[0] / total
    h11 = dots[1] / total
    h21 = norm_of(dots[2] / total, [h01, h11])
    inv = 1.0 / h21
    shift = 0.5 - h11
    b2 = (shift * b1 + k2 - h01 * b0) * inv
    k3 = (shift * k2 + image - h01 * k1) * inv
    w2 = 0.5 * b2 + k3
    b2_ref[...] = b2
    w2_ref[...] = w2
    table = entry(table_in_ref[...], 0, 1, h01)
    table = entry(table, 1, 1, h11)
    table_ref[...] = entry(table, 2, 1, h21)
    val = in_lanes([inner(b0, w2), inner(b1, w2), inner(b2, w2), inner(w2, w2)])
    dots_ref[...] = jnp.broadcast_to(val[:1, :].reshape(1, 1, 128), dots_ref.shape)


def last_kernel(
    total, b0_ref, b1_ref, b2_ref, w2_ref, table_ref, dots_ref, out_ref, hessen_ref
):
    leaves = out_ref.shape[1]
    sums = jnp.sum(dots_ref[...], axis=0)
    dots = [sums[:, 32 * i : 32 * i + 1] / total for i in range(4)]
    b0, b1, b2 = b0_ref[:leaves, :], b1_ref[:leaves, :], b2_ref[:leaves, :]
    scale = norm_of(dots[3], dots[:3])
    update = w2_ref[:leaves, :] - dots[0] * b0 - dots[1] * b1 - dots[2] * b2
    out_ref[0] = b0
    out_ref[1] = b1
    out_ref[2] = b2
    out_ref[3] = update * (1.0 / scale)
    table = table_ref[...]
    for i in range(3):
        table = entry(table, i, 2, dots[i])
    table = entry(table, 3, 2, scale)
    hessen_ref[...] = table[:4, :3]


def shaped(shape, dtype=F32):
    return jax.ShapeDtypeStruct(shape, dtype)


def call(kernel, ins, outs):
    return pl.pallas_call(
        kernel,
        in_specs=ins,
        out_specs=[VMEM] * len(outs),
        out_shape=outs,
        compiler_params=pltpu.CompilerParams(vmem_limit_bytes=16 * 1024 * 1024),
    )


def per_device(
    start_vec,
    near_blocks,
    near_ids,
    far_ids,
    leaf_basis,
    leaf_coupling,
    node_transfer,
    branch_transfer,
    top_ids,
    top_coupling,
):
    axes = ("leaf", "sub")
    subs = lax.axis_size("sub")
    devices = lax.axis_size("leaf") * subs
    leaves, size = start_vec.shape
    rank = leaf_basis.shape[1]
    total = float(leaves * size * devices)
    block = shaped((devices * ROWS, size), BF16)
    vec = shaped((ROWS, size))
    table = shaped((ROWS, 128))

    def exchange(blocks):
        return lax.all_to_all(blocks, axes, 0, 0, tiled=True)

    place = lax.axis_index("leaf").astype(jnp.int32).reshape(1)
    out, pick, down, top_down, basis2 = call(
        lambda *refs: first_kernel(subs, *refs),
        [SMEM] * 4 + [VMEM] * 5,
        [
            block,
            shaped((8 * ROWS, devices * ROWS), BF16),
            shaped((leaves, 2 * rank, size), BF16),
            shaped((leaves * rank, top_coupling.shape[2]), BF16),
            shaped((leaves, 2 * rank, size), BF16),
        ],
    )(
        near_ids,
        far_ids,
        top_ids,
        place,
        start_vec,
        leaf_basis,
        node_transfer,
        branch_transfer,
        top_coupling,
    )
    fixed = (pick, near_blocks, top_down, leaf_coupling, leaf_basis)
    out, b0, k1 = call(
        lambda *refs: second_kernel(total, *refs), [VMEM] * 9, [block, vec, vec]
    )(start_vec, exchange(out), *fixed, basis2, down)
    out, b1, k2, heads = call(
        lambda *refs: third_kernel(total, *refs), [VMEM] * 10, [block, vec, vec, table]
    )(b0, k1, exchange(out), *fixed, basis2, down)
    dots, b2, w2, heads = call(
        lambda *refs: fourth_kernel(total, *refs),
        [VMEM] * 11,
        [shaped((devices, 1, 128)), vec, vec, table],
    )(b0, k1, b1, k2, heads, exchange(out), *fixed)
    basis, hessen = call(
        lambda *refs: last_kernel(total, *refs),
        [VMEM] * 6,
        [shaped((4, leaves, size)), shaped((4, 3))],
    )(b0, b1, b2, w2, heads, exchange(dots))
    return basis, hessen


def solution(mesh):
    placed = (
        P(("leaf", "sub"), None),
        P(("leaf", "sub"), None, None, None),
        P(("leaf", "sub"), None),
        P(("leaf", "sub"), None),
        P(("leaf", "sub"), None, None),
        P(("leaf", "sub"), None, None),
        P(("leaf", "sub"), None, None),
        P(("leaf", "sub"), None, None),
        P("leaf", None),
        P("leaf", None, None),
    )
    return jax.shard_map(
        per_device,
        mesh=mesh,
        in_specs=placed,
        out_specs=(P(None, ("leaf", "sub"), None), P()),
        check_vma=False,
    )
```

time: 335 us -> 56 us (0.17)
  blocking collectives: 264 us -> 44.3 us
  starting transfers between devices: 18.1 us -> 0 us
  other arithmetic: 17.2 us -> 0 us
  local copies, waits for them, and re-layouts: 16.9 us -> 5.86 us
  between operations: 10 us -> 0.71 us
  matrix products: 5.72 us -> 0 us
  Pallas kernels: 0 us -> 4.72 us
    psum x4 -> x0, blocking collectives: 153 us -> none  [the longest x3 111 us: per_device(): lax.psum((partial_dots, jnp.sum(image * image)), ('leaf', 'sub'))]
    unnamed x6 -> x0, blocking collectives: 79.2 us -> none
    all_to_all x0 -> x4, blocking collectives: none -> 44.3 us  [exchange(): return lax.all_to_all(blocks, axes, 0, 0, tiled=True)]
    all_gather x6 -> x0, blocking collectives: 31.7 us -> none  [the longest x3 16.3 us: apply_matrix(): branch_vec = lax.all_gather(vec_bf, 'sub', axis=0, tiled=True)]
    ppermute x6 -> x0, starting transfers between devices: 18.1 us -> none  [the longest x3 14.3 us: with_halo(): lax.ppermute(tail, axis, [(i, (i + 1) % count) for i in range(ends)])]
    another operation x10 -> x0, other arithmetic: 11 us -> none
    dot_general x30 -> x0, matrix products: 5.72 us -> none  [the longest x3 1.31 us: apply_matrix(): jnp.einsum('lrk,lk->lr', leaf_basis, vec_bf, preferred_element_type=jnp.f...]
    pallas_call x0 -> x5, Pallas kernels: none -> 4.72 us  [the longest x1 1.24 us: per_device(): call(lambda *refs: first_kernel(subs, *refs), [SMEM] * 4 + [VMEM] * 5, [b...]
  transfers between devices with their start and end apart: 6 -> 0, of which waited for: 0 -> 0; matrix products, arithmetic and copies ran while one was open for 5% -> 0% of each run, Pallas kernels for 0% -> 0%
where the time goes in v1:
time: 56 us; the launch traced here: 55.6 us
  blocking collectives  44.3 us (79%)
  local copies, waits for them, and re-layouts  5.86 us (10%)
  Pallas kernels  4.72 us (8%)
  between operations  0.71 us (1%)
    all_to_all x4, blocking collectives, exchange(): return lax.all_to_all(blocks, axes, 0, 0, tiled=True)  44.3 us
    unnamed x26, local copies, waits for them, and re-layouts  5.86 us
    pallas_call x1, Pallas kernels, per_device(): call(lambda *refs: first_kernel(subs, *refs), [SMEM] * 4 + [VMEM] * 5, [b...  1.24 us

profile of v1, /device:TPU:0, one launch (start us, length us, event | category | flops | bytes accessed | tf_op | source)
XLA Modules:
  0.0 55.6 jit_solution(13445229372081427858)
XLA Ops:
  0.6 0.0 copy-start.11
  0.6 0.0 copy-start.10
  0.7 0.6 %copy-done.11 = s32[4,1]{0,1:T(1,128)S(1)} copy-done((s32[4,1]{0,1:T(1,128)S(1)}, s32[4,1]{0,1:T(1,128)}, u32[]{:S(2)}) %copy-start.11) | copy-done | bytes 40
  1.3 0.0 copy-start.7
  1.3 0.1 copy.12.refs_0_
  1.4 0.0 copy-done.10
  1.4 0.1 copy.13.refs_1_
  1.5 0.0 copy-start.9
  1.5 0.5 copy-done.7
  2.0 0.2 copy-done.9
  2.1 0.0 copy-start.2
  2.1 0.9 %copy-done.2 = bf16[4,64,256]{2,1,0:T(8,128)(2,1)S(1)} copy-done((bf16[4,64,256]{2,1,0:T(8,128)(2,1)S(1)}, bf16[4,64,256]{2,1,0:T(8,128)(2,1)}, u32[]{:S(2)}) %copy-start.2) | copy-done | bytes 131096
  3.0 0.0 copy-start.5
  3.0 0.8 %copy-done.5 = bf16[1,64,256]{2,1,0:T(8,128)(2,1)S(1)} copy-done((bf16[1,64,256]{2,1,0:T(8,128)(2,1)S(1)}, bf16[1,64,256]{2,1,0:T(8,128)(2,1)}, u32[]{:S(2)}) %copy-start.5) | copy-done | bytes 32792
  3.8 0.0 copy-start.6
  3.8 0.8 %copy-done.6 = bf16[1,64,256]{2,1,0:T(8,128)(2,1)S(1)} copy-done((bf16[1,64,256]{2,1,0:T(8,128)(2,1)S(1)}, bf16[1,64,256]{2,1,0:T(8,128)(2,1)}, u32[]{:S(2)}) %copy-start.6) | copy-done | bytes 32792
  4.6 0.0 copy-start.8
  4.6 0.7 %copy-done.8 = bf16[1,64,64]{2,1,0:T(8,128)(2,1)S(1)} copy-done((bf16[1,64,64]{2,1,0:T(8,128)(2,1)S(1)}, bf16[1,64,64]{2,1,0:T(8,128)(2,1)}, u32[]{:S(2)}) %copy-start.8) | copy-done | bytes 8216
  5.3 1.2 %shard_map.113 = (bf16[256,256]{1,0:T(8,128)(2,1)S(1)}, bf16[64,256]{1,0:T(8,128)(2,1)S(1)}, bf16[4,128,256]{2,1,0:T(8,128)(2,1)S(1)}, bf16[256,256]{1,0:T(8,128)(2,1)S(1)}, bf16[4,128,256]{2,1,0:T(8,128)(2,1)S(1)}) custom-call(s32[4,1]{1,0:T(4,128)S(1)} %copy.12.refs_0_, s32[4,2]{1,0:T(4,128)S(1)} %copy.13.refs_1_, s32[1,4]{1,0:T(1,128)S(1)} %copy-done.9, ...), custom_call_target="tpu_custom_call" | custom-call | tf_op jit(solution)/shard_map/pallas_call | solution.py:344
  6.5 0.0 copy-start.3
  6.5 0.0 copy-start.4
  6.5 15.3 %all_to_all.38 = bf16[32,8,256]{2,1,0:T(8,128)(2,1)S(1)} all-to-all(bf16[32,8,256]{2,1,0:T(8,128)(2,1)S(1)} %bitcast.10), channel_id=1, replica_groups=mesh['leaf'=8,'sub'=4] {'leaf','sub'}, dimensions={0} | all-to-all | bytes 262144 | tf_op jit(solution)/shard_map/all_to_all | solution.py:341
  21.9 0.0 copy-done.3
  21.9 0.0 copy-done.4
  21.9 0.0 copy-start
  21.9 1.2 %copy-done = bf16[4,2,256,256]{3,2,1,0:T(8,128)(2,1)S(1)} copy-done((bf16[4,2,256,256]{3,2,1,0:T(8,128)(2,1)S(1)}, bf16[4,2,256,256]{3,2,1,0:T(8,128)(2,1)}, u32[]{:S(2)}) %copy-start) | copy-done | bytes 1048600
  23.1 0.0 copy-start.1
  23.1 0.9 %shard_map.114 = (bf16[256,256]{1,0:T(8,128)(2,1)S(1)}, f32[8,256]{1,0:T(8,128)S(1)}, f32[8,256]{1,0:T(8,128)S(1)}) custom-call(f32[4,256]{1,0:T(4,128)S(1)} %copy-done.7, bf16[256,256]{1,0:T(8,128)(2,1)S(1)} %bitcast.9, bf16[64,256]{1,0:T(8,128)(2,1)S(1)} %get-tuple-element.19.refs_2_.refs_3_.refs_6_, bf16[4,2,256,256]{3,2,1,0:T(8,128)(2,1)S(1)} %copy-done, ...), custom_call_target="tpu_custom_call" | custom-call | tf_op jit(solution)/shard_map/pallas_call | solution.py:366
  24.0 10.0 %all_to_all.39 = bf16[32,8,256]{2,1,0:T(8,128)(2,1)S(1)} all-to-all(bf16[32,8,256]{2,1,0:T(8,128)(2,1)S(1)} %bitcast.12), channel_id=1, replica_groups=mesh['leaf'=8,'sub'=4] {'leaf','sub'}, dimensions={0} | all-to-all | bytes 262144 | tf_op jit(solution)/shard_map/all_to_all | solution.py:341
  34.1 0.0 copy-done.1
  34.1 0.9 %shard_map.115 = (bf16[256,256]{1,0:T(8,128)(2,1)S(1)}, f32[8,256]{1,0:T(8,128)S(1)}, f32[8,256]{1,0:T(8,128)S(1)}, f32[8,128]{1,0:T(8,128)S(1)}) custom-call(f32[8,256]{1,0:T(8,128)S(1)} %get-tuple-element.23.refs_0_, f32[8,256]{1,0:T(8,128)S(1)} %get-tuple-element.24.refs_1_, bf16[256,256]{1,0:T(8,128)(2,1)S(1)} %bitcast.8, ...), custom_call_target="tpu_custom_call" | custom-call | tf_op jit(solution)/shard_map/pallas_call | solution.py:369
  35.0 10.0 %all_to_all.40 = bf16[32,8,256]{2,1,0:T(8,128)(2,1)S(1)} all-to-all(bf16[32,8,256]{2,1,0:T(8,128)(2,1)S(1)} %bitcast.11), channel_id=1, replica_groups=mesh['leaf'=8,'sub'=4] {'leaf','sub'}, dimensions={0} | all-to-all | bytes 262144 | tf_op jit(solution)/shard_map/all_to_all | solution.py:341
  45.0 0.8 %shard_map.116 = (f32[32,1,128]{2,1,0:T(1,128)S(1)}, f32[8,256]{1,0:T(8,128)S(1)}, f32[8,256]{1,0:T(8,128)S(1)}, f32[8,128]{1,0:T(8,128)S(1)}) custom-call(f32[8,256]{1,0:T(8,128)S(1)} %get-tuple-element.23.refs_0_, f32[8,256]{1,0:T(8,128)S(1)} %get-tuple-element.24.refs_1_, f32[8,256]{1,0:T(8,128)S(1)} %get-tuple-element.26.refs_2_.refs_1_, ...), custom_call_target="tpu_custom_call" | custom-call | tf_op jit(solution)/shard_map/pallas_call | solution.py:372
  45.8 8.9 %all_to_all.41.refs_5_ = f32[32,1,128]{2,1,0:T(1,128)S(1)} all-to-all(f32[32,1,128]{2,1,0:T(1,128)S(1)} %get-tuple-element.33), channel_id=1, replica_groups=mesh['leaf'=8,'sub'=4] {'leaf','sub'}, dimensions={0} | all-to-all | bytes 32768 | tf_op jit(solution)/shard_map/all_to_all | solution.py:341
  54.7 0.8 %shard_map.117 = (f32[4,4,256]{2,1,0:T(4,128)}, f32[4,3]{1,0:T(4,128)}) custom-call(f32[8,256]{1,0:T(8,128)S(1)} %get-tuple-element.23.refs_0_, f32[8,256]{1,0:T(8,128)S(1)} %get-tuple-element.26.refs_2_.refs_1_, f32[8,256]{1,0:T(8,128)S(1)} %get-tuple-element.30.refs_2_, f32[8,256]{1,0:T(8,128)S(1)} %get-tuple-element.31.refs_3_, ...), custom_call_target="tpu_custom_call" | custom-call | tf_op jit(solution)/shard_map/pallas_call | solution.py:377
Async XLA Ops:
  0.6 0.7 %copy-start.11 = (s32[4,1]{0,1:T(1,128)S(1)}, s32[4,1]{0,1:T(1,128)}, u32[]{:S(2)}) copy-start(s32[4,1]{0,1:T(1,128)} %param.12) | copy-start | bytes 52
  0.6 0.7 %copy-start.10 = (s32[4,2]{0,1:T(2,128)S(1)}, s32[4,2]{0,1:T(2,128)}, u32[]{:S(2)}) copy-start(s32[4,2]{0,1:T(2,128)} %param.13) | copy-start | bytes 100
  1.3 0.7 %copy-start.7 = (f32[4,256]{1,0:T(4,128)S(1)}, f32[4,256]{1,0:T(4,128)}, u32[]{:S(2)}) copy-start(f32[4,256]{1,0:T(4,128)} %refs_0_.2) | copy-start | bytes 12292
  1.5 0.7 %copy-start.9 = (s32[1,4]{1,0:T(1,128)S(1)}, s32[1,4]{1,0:T(1,128)}, u32[]{:S(2)}) copy-start(s32[1,4]{1,0:T(1,128)} %refs_2_.1) | copy-start | bytes 52
  2.1 0.9 %copy-start.2 = (bf16[4,64,256]{2,1,0:T(8,128)(2,1)S(1)}, bf16[4,64,256]{2,1,0:T(8,128)(2,1)}, u32[]{:S(2)}) copy-start(bf16[4,64,256]{2,1,0:T(8,128)(2,1)} %refs_10_.1) | copy-start | bytes 393220
  3.0 0.8 %copy-start.5 = (bf16[1,64,256]{2,1,0:T(8,128)(2,1)S(1)}, bf16[1,64,256]{2,1,0:T(8,128)(2,1)}, u32[]{:S(2)}) copy-start(bf16[1,64,256]{2,1,0:T(8,128)(2,1)} %refs_6_.3) | copy-start | bytes 98308
  3.8 0.8 %copy-start.6 = (bf16[1,64,256]{2,1,0:T(8,128)(2,1)S(1)}, bf16[1,64,256]{2,1,0:T(8,128)(2,1)}, u32[]{:S(2)}) copy-start(bf16[1,64,256]{2,1,0:T(8,128)(2,1)} %refs_8_.1) | copy-start | bytes 98308
  4.6 0.7 %copy-start.8 = (bf16[1,64,64]{2,1,0:T(8,128)(2,1)S(1)}, bf16[1,64,64]{2,1,0:T(8,128)(2,1)}, u32[]{:S(2)}) copy-start(bf16[1,64,64]{2,1,0:T(8,128)(2,1)} %refs_7_.3) | copy-start | bytes 24580
  6.5 15.4 %copy-start.3 = (bf16[4,64,256]{2,1,0:T(8,128)(2,1)S(1)}, bf16[4,64,256]{2,1,0:T(8,128)(2,1)}, u32[]{:S(2)}) copy-start(bf16[4,64,256]{2,1,0:T(8,128)(2,1)} %refs_10_.1) | copy-start | bytes 393220
  6.5 15.4 %copy-start.4 = (bf16[4,64,128]{2,1,0:T(8,128)(2,1)S(1)}, bf16[4,64,128]{2,1,0:T(8,128)(2,1)}, u32[]{:S(2)}) copy-start(bf16[4,64,128]{2,1,0:T(8,128)(2,1)} %refs_9_.1) | copy-start | bytes 196612
  21.9 1.2 %copy-start = (bf16[4,2,256,256]{3,2,1,0:T(8,128)(2,1)S(1)}, bf16[4,2,256,256]{3,2,1,0:T(8,128)(2,1)}, u32[]{:S(2)}) copy-start(bf16[4,2,256,256]{3,2,1,0:T(8,128)(2,1)} %refs_7_.5) | copy-start | bytes 3145732
  23.1 10.9 %copy-start.1 = (bf16[4,2,256,256]{3,2,1,0:T(8,128)(2,1)S(1)}, bf16[4,2,256,256]{3,2,1,0:T(8,128)(2,1)}, u32[]{:S(2)}) copy-start(bf16[4,2,256,256]{3,2,1,0:T(8,128)(2,1)} %refs_7_.5) | copy-start | bytes 3145732

commit v2 on v1

--- a/solution.py
+++ b/solution.py
@@ -9,7 +9,7 @@
 BF16 = jnp.bfloat16
 ROWS = 8
 VMEM = pl.BlockSpec(memory_space=pltpu.VMEM)
-SMEM = pl.BlockSpec(memory_space=pltpu.SMEM)
+HBM = pl.BlockSpec(memory_space=pltpu.HBM)
 
 
 def dot_nt(a, b):
@@ -54,14 +54,17 @@
     return 0.5 * jnp.sum(jnp.sum(prod, axis=0, keepdims=True), axis=1, keepdims=True)
 
 
-def write_block(vec, dots, basis2_ref, down_ref, out_ref):
-    leaves = basis2_ref.shape[0]
-    vec_bf = vec.astype(BF16)
-    coef = by_leaf([dot_nt(vec_bf, basis2_ref[l]) for l in range(leaves)])
-    term = jnp.zeros((ROWS, 128), F32)
-    for l in range(leaves):
-        one = jnp.broadcast_to(vec[l : l + 1, :], vec.shape).astype(BF16)
-        term = term + dot_nt(one, down_ref[l])
+def is_mine(shape, rank, leaves):
+    return iota(shape, 1) // rank == iota(shape, 0) % leaves
+
+
+def make_block(vec, dots, basis, reach2):
+    leaves, rank, size = basis.shape
+    coef = dot_nt(vec.astype(BF16), basis.reshape(leaves * rank, size))
+    coef = jnp.where(is_mine(coef.shape, rank, leaves), coef, 0.0)
+    term = 0.5 * jnp.sum(dot_nt(coef.astype(BF16), reach2), axis=0, keepdims=True)
+    coef = coef[:, :128] + coef[:, 128:]
+    coef = coef + pltpu.roll(coef, rank, 1)
     val = in_lanes(dots)
     rest = val - val.astype(BF16).astype(F32)
     last = rest - rest.astype(BF16).astype(F32)
@@ -69,7 +72,10 @@
     left = jnp.where(row < 4, vec[:, :128], coef)
     right = jnp.where(row == 4, term, jnp.where(row == 5, val, jnp.where(row == 6, rest, last)))
     right = jnp.where(row < 4, vec[:, 128:], right)
-    block = twice(jnp.concatenate([left, right], axis=1)).astype(BF16)
+    return twice(jnp.concatenate([left, right], axis=1)).astype(BF16)
+
+
+def store_all(block, out_ref):
     pairs = out_ref.shape[0] // 16
     if pairs <= 32:
         for p in range(pairs):
@@ -84,66 +90,85 @@
 
 
 def first_kernel(
-    subs,
-    near_ids,
-    far_ids,
-    top_ids,
-    place,
+    start_hbm,
+    basis_hbm,
+    node_hbm,
+    upper_hbm,
+    block_ref,
+    reach2_ref,
     start_ref,
     basis_ref,
     node_ref,
     upper_ref,
+    sems,
+):
+    sources = (basis_hbm, node_hbm, upper_hbm, start_hbm)
+    targets = (basis_ref, node_ref, upper_ref, start_ref)
+    copies = [
+        pltpu.make_async_copy(source, target, sems.at[i])
+        for i, (source, target) in enumerate(zip(sources, targets))
+    ]
+    for copy in copies:
+        copy.start()
+    for copy in copies:
+        copy.wait()
+    reach2 = twice(dot_nn(upper_ref[0], node_ref[0])).astype(BF16)
+    reach2_ref[...] = reach2
+    start = twice(start_ref[...])
+    store_all(make_block(start, [inner(start, start)], basis_ref[...], reach2), block_ref)
+
+
+def own_part(vec, near_ref):
+    vec_bf = vec.astype(BF16)
+    return by_leaf([dot_nt(vec_bf, near_ref[l, 0]) for l in range(near_ref.shape[0])])
+
+
+def setup_kernel(
+    subs,
+    near_ids_ref,
+    far_ids_ref,
+    top_ids_ref,
+    branch_ref,
+    reach2_ref,
     top_ref,
-    block_ref,
+    start_ref,
+    near_ref,
     pick_ref,
-    down_ref,
     top_down_ref,
-    basis2_ref,
-):
-    leaves, rank, _ = basis_ref.shape
-    node = node_ref[0]
-    reach = dot_nn(upper_ref[0], node).astype(BF16)
-    top_down_ref[...] = dot_tn(reach, top_ref[0]).astype(BF16)
-    for l in range(leaves):
-        own = basis_ref[l]
-        basis2_ref[l] = twice(own)
-        part = dot_nn(reach[:, l * rank : (l + 1) * rank], own).astype(BF16)
-        down_ref[l] = twice(part)
-    branch = place[0]
+    own_ref,
+):
+    own_ref[...] = own_part(twice(start_ref[...]), near_ref)
+    near_ids, far_ids, top_ids = near_ids_ref[...], far_ids_ref[...], top_ids_ref[...]
+    branch = branch_ref[...]
+    leaves = near_ids.shape[1]
+    rank = top_ref.shape[1]
+    top_down_ref[...] = dot_tn(reach2_ref[:rank, :], top_ref[0]).astype(BF16)
     width = pick_ref.shape[1]
     col = iota((ROWS, width), 1)
-    row4 = iota((ROWS, width), 0) % leaves
-
-    def leaf_column(leaf_index, offset):
-        return (leaf_index // leaves) * ROWS + leaf_index % leaves + offset
-
-    def pick(columns):
-        want = columns[leaves - 1]
-        for l in range(leaves - 1):
-            want = jnp.where(row4 == l, columns[l], want)
-        return (col == want).astype(F32)
+    lane4, row4 = iota((ROWS, leaves), 1), iota((ROWS, leaves), 0) % leaves
+
+    def by_row(ids):
+        kept = jnp.where(lane4 == row4, ids, 0).astype(F32)
+        return jnp.sum(kept, axis=1, keepdims=True).astype(jnp.int32)
+
+    def leaf_column(index):
+        return 2 * index - index % leaves
 
     branch_leaves = subs * leaves
     count = (width // ROWS) * leaves
-    near = []
-    for l in range(leaves):
-        index = (branch - 1) * branch_leaves + near_ids[l, 0]
-        inside = (index >= 0) & (index < count)
-        near.append(jnp.where(inside, leaf_column(jnp.maximum(index, 0), 0), -1))
-    groups = [pick(near)]
+    index = (branch - 1) * branch_leaves + by_row(near_ids)
+    inside = (index >= 0) & (index < count)
+    groups = [col == jnp.where(inside, leaf_column(jnp.maximum(index, 0)), -1)]
     for s in range(2):
-        groups.append(
-            pick([leaf_column(branch * branch_leaves + far_ids[l, s], leaves) for l in range(leaves)])
-        )
+        index = branch * branch_leaves + by_row(far_ids[s : s + 1, :])
+        groups.append(col == leaf_column(index) + leaves)
     for s in range(4):
-        groups.append(((col % ROWS == 4) & (col // (ROWS * subs) == top_ids[0, s])).astype(F32))
-    groups.append((col % ROWS >= 5).astype(F32))
-    pick_ref[...] = jnp.concatenate(groups, axis=0).astype(BF16)
-    start = twice(start_ref[...])
-    write_block(start, [inner(start, start)], basis2_ref, down_ref, block_ref)
-
-
-def multiply(own, got_ref, pick_ref, near_ref, top_down_ref, coupling_ref, basis_ref):
+        groups.append((col % ROWS == 4) & (col // (ROWS * subs) == top_ids[0:1, s : s + 1]))
+    groups.append(col % ROWS >= 5)
+    pick_ref[...] = jnp.concatenate([g.astype(F32) for g in groups], axis=0).astype(BF16)
+
+
+def multiply(own_out, got_ref, pick_ref, near_ref, top_down_ref, coupling_ref, basis_ref):
     leaves, rank, size = basis_ref.shape
     got = dot_nn(pick_ref[...], got_ref[...])
     group = [got[ROWS * g : ROWS * g + ROWS, :] for g in range(8)]
@@ -154,14 +179,10 @@
     top_in = jnp.concatenate([top_a, top_b], axis=1)
     local = dot_nt(far_in, coupling_ref[...].reshape(leaves * rank, -1))
     local = local + dot_nt(top_in, top_down_ref[...])
-    mine = iota((ROWS, leaves * rank), 1) // rank == iota((ROWS, leaves * rank), 0) % leaves
-    local = jnp.where(mine, local, 0.0).astype(BF16)
+    local = jnp.where(is_mine(local.shape, rank, leaves), local, 0.0).astype(BF16)
     far_out = dot_nn(local, basis_ref[...].reshape(leaves * rank, size))
-    own_bf = own.astype(BF16)
     other = group[0].astype(BF16)
-    near_out = by_leaf(
-        [dot_nt(own_bf, near_ref[l, 0]) + dot_nt(other, near_ref[l, 1]) for l in range(leaves)]
-    )
+    near_out = own_out + by_leaf([dot_nt(other, near_ref[l, 1]) for l in range(leaves)])
     dots = [group[7][:, 128 + 32 * i : 129 + 32 * i] for i in range(4)]
     return near_out + far_out, dots
 
@@ -181,21 +202,21 @@
 def second_kernel(
     total,
     start_ref,
+    own_ref,
     got_ref,
     pick_ref,
     near_ref,
     top_down_ref,
     coupling_ref,
     basis_ref,
-    basis2_ref,
-    down_ref,
+    reach2_ref,
     block_ref,
     b0_ref,
     k1_ref,
 ):
     start = twice(start_ref[...])
     image, dots = multiply(
-        start, got_ref, pick_ref, near_ref, top_down_ref, coupling_ref, basis_ref
+        own_ref[...], got_ref, pick_ref, near_ref, top_down_ref, coupling_ref, basis_ref
     )
     scale = lax.rsqrt(dots[0] / total + 1e-06)
     b0 = scale * start
@@ -203,7 +224,8 @@
     w0 = 0.5 * b0 + k1
     b0_ref[...] = b0
     k1_ref[...] = k1
-    write_block(k1, [inner(b0, w0), inner(w0, w0)], basis2_ref, down_ref, block_ref)
+    dots = [inner(b0, w0), inner(w0, w0)]
+    store_all(make_block(k1, dots, basis_ref[...], reach2_ref[...]), block_ref)
 
 
 def third_kernel(
@@ -216,15 +238,22 @@
     top_down_ref,
     coupling_ref,
     basis_ref,
-    basis2_ref,
-    down_ref,
+    reach2_ref,
     block_ref,
     b1_ref,
     k2_ref,
     table_ref,
 ):
     k1 = k1_ref[...]
-    image, dots = multiply(k1, got_ref, pick_ref, near_ref, top_down_ref, coupling_ref, basis_ref)
+    image, dots = multiply(
+        own_part(k1, near_ref),
+        got_ref,
+        pick_ref,
+        near_ref,
+        top_down_ref,
+        coupling_ref,
+        basis_ref,
+    )
     b0 = b0_ref[...]
     h00 = dots[0] / total
     h10 = norm_of(dots[1] / total, [h00])
@@ -238,9 +267,8 @@
     table = jnp.zeros((ROWS, 128), F32)
     table = entry(table, 0, 0, h00)
     table_ref[...] = entry(table, 1, 0, h10)
-    write_block(
-        k2, [inner(b0, w1), inner(b1, w1), inner(w1, w1)], basis2_ref, down_ref, block_ref
-    )
+    dots = [inner(b0, w1), inner(b1, w1), inner(w1, w1)]
+    store_all(make_block(k2, dots, basis_ref[...], reach2_ref[...]), block_ref)
 
 
 def fourth_kernel(
@@ -262,7 +290,15 @@
     table_ref,
 ):
     k2 = k2_ref[...]
-    image, dots = multiply(k2, got_ref, pick_ref, near_ref, top_down_ref, coupling_ref, basis_ref)
+    image, dots = multiply(
+        own_part(k2, near_ref),
+        got_ref,
+        pick_ref,
+        near_ref,
+        top_down_ref,
+        coupling_ref,
+        basis_ref,
+    )
     b0, k1, b1 = b0_ref[...], k1_ref[...], b1_ref[...]
     h01 = dots[0] / total
     h11 = dots[1] / total
@@ -305,12 +341,13 @@
     return jax.ShapeDtypeStruct(shape, dtype)
 
 
-def call(kernel, ins, outs):
+def call(kernel, ins, outs, scratch=()):
     return pl.pallas_call(
         kernel,
         in_specs=ins,
         out_specs=[VMEM] * len(outs),
         out_shape=outs,
+        scratch_shapes=scratch,
         compiler_params=pltpu.CompilerParams(vmem_limit_bytes=16 * 1024 * 1024),
     )
 
@@ -333,42 +370,38 @@
     leaves, size = start_vec.shape
     rank = leaf_basis.shape[1]
     total = float(leaves * size * devices)
-    block = shaped((devices * ROWS, size), BF16)
+    blocks = shaped((devices * ROWS, size), BF16)
     vec = shaped((ROWS, size))
     table = shaped((ROWS, 128))
 
-    def exchange(blocks):
-        return lax.all_to_all(blocks, axes, 0, 0, tiled=True)
-
-    place = lax.axis_index("leaf").astype(jnp.int32).reshape(1)
-    out, pick, down, top_down, basis2 = call(
-        lambda *refs: first_kernel(subs, *refs),
-        [SMEM] * 4 + [VMEM] * 5,
+    def exchange(out):
+        return lax.all_to_all(out, axes, 0, 0, tiled=True)
+
+    sources = (start_vec, leaf_basis, node_transfer, branch_transfer)
+    out, reach2 = call(
+        first_kernel,
+        [HBM] * 4,
+        [blocks, shaped((2 * rank, leaves * rank), BF16)],
+        [pltpu.VMEM(a.shape, a.dtype) for a in sources] + [pltpu.SemaphoreType.DMA((4,))],
+    )(*[pltpu.with_memory_space_constraint(a, pltpu.HBM) for a in sources])
+    got = exchange(out)
+    branch = lax.axis_index("leaf").astype(jnp.int32).reshape(1, 1)
+    pick, top_down, own = call(
+        lambda *refs: setup_kernel(subs, *refs),
+        [VMEM] * 8,
         [
-            block,
             shaped((8 * ROWS, devices * ROWS), BF16),
-            shaped((leaves, 2 * rank, size), BF16),
             shaped((leaves * rank, top_coupling.shape[2]), BF16),
-            shaped((leaves, 2 * rank, size), BF16),
+            vec,
         ],
-    )(
-        near_ids,
-        far_ids,
-        top_ids,
-        place,
-        start_vec,
-        leaf_basis,
-        node_transfer,
-        branch_transfer,
-        top_coupling,
-    )
+    )(near_ids.T, far_ids.T, top_ids, branch, reach2, top_coupling, start_vec, near_blocks)
     fixed = (pick, near_blocks, top_down, leaf_coupling, leaf_basis)
     out, b0, k1 = call(
-        lambda *refs: second_kernel(total, *refs), [VMEM] * 9, [block, vec, vec]
-    )(start_vec, exchange(out), *fixed, basis2, down)
+        lambda *refs: second_kernel(total, *refs), [VMEM] * 9, [blocks, vec, vec]
+    )(start_vec, own, got, *fixed, reach2)
     out, b1, k2, heads = call(
-        lambda *refs: third_kernel(total, *refs), [VMEM] * 10, [block, vec, vec, table]
-    )(b0, k1, exchange(out), *fixed, basis2, down)
+        lambda *refs: third_kernel(total, *refs), [VMEM] * 9, [blocks, vec, vec, table]
+    )(b0, k1, exchange(out), *fixed, reach2)
     dots, b2, w2, heads = call(
         lambda *refs: fourth_kernel(total, *refs),
         [VMEM] * 11,

time: 56 us -> 50.8 us (0.907)
  blocking collectives: 44.3 us -> 28.9 us
  starting transfers between devices: 0 us -> 7.3 us
  waiting for transfers between devices: 0 us -> 5.96 us
  local copies, waits for them, and re-layouts: 5.86 us -> 1.92 us
  Pallas kernels: 4.72 us -> 5.63 us
    all_to_all x4 -> x3, blocking collectives: 44.3 us -> 28.9 us  [exchange(): return lax.all_to_all(out, axes, 0, 0, tiled=True)]
    all_to_all x0 -> x1, starting transfers between devices: none -> 7.3 us  [exchange(): return lax.all_to_all(out, axes, 0, 0, tiled=True)]
    all_to_all x0 -> x1, waiting for transfers between devices: none -> 5.96 us  [exchange(): return lax.all_to_all(out, axes, 0, 0, tiled=True)]
    unnamed x26 -> x18, local copies, waits for them, and re-layouts: 5.86 us -> 1.92 us
    pallas_call x3 -> x4, Pallas kernels: 3.09 us -> 3.99 us  [the longest x1 1.92 us: per_device(): call(first_kernel, [HBM] * 4, [blocks, shaped((2 * rank, leaves * rank),...]
  transfers between devices with their start and end apart: 0 -> 1, of which waited for: 0 -> 1; matrix products, arithmetic and copies ran while one was open for 0% -> 0% of each run, Pallas kernels for 0% -> 1%
where the time goes in v2:
time: 50.8 us; the launch traced here: 50.5 us
  blocking collectives  28.9 us (57%)
  starting transfers between devices  7.3 us (14%)
  waiting for transfers between devices  5.96 us (12%)
  Pallas kernels  5.63 us (11%)
  local copies, waits for them, and re-layouts  1.92 us (4%)
  between operations  0.75 us (1%)
    all_to_all x3, blocking collectives, exchange(): return lax.all_to_all(out, axes, 0, 0, tiled=True)  28.9 us
    all_to_all x1, starting transfers between devices, exchange(): return lax.all_to_all(out, axes, 0, 0, tiled=True)  7.3 us
    all_to_all x1, waiting for transfers between devices, exchange(): return lax.all_to_all(out, axes, 0, 0, tiled=True)  5.96 us
    pallas_call x1, Pallas kernels, per_device(): call(first_kernel, [HBM] * 4, [blocks, shaped((2 * rank, leaves * rank),...  1.92 us
    unnamed x18, local copies, waits for them, and re-layouts  1.92 us
  transfers between devices with their start and end apart: 1, of which 1 were waited for; matrix products, arithmetic and copies ran while one was open for 0% of the time, Pallas kernels for 1%

profile of v2, /device:TPU:0, one launch (start us, length us, event | category | flops | bytes accessed | tf_op | source)
XLA Modules:
  0.0 50.5 jit_solution(11344737448176095414)
XLA Ops:
  0.6 1.9 %shard_map.113 = (bf16[256,256]{1,0:T(8,128)(2,1)}, bf16[128,256]{1,0:T(8,128)(2,1)S(1)}) custom-call(f32[4,256]{1,0:T(4,128)} %refs_0_.1, bf16[4,64,256]{2,1,0:T(8,128)(2,1)} %refs_10_.1, bf16[1,64,256]{2,1,0:T(8,128)(2,1)} %node_hbm.1, bf16[1,64,64]{2,1,0:T(8,128)(2,1)} %upper_hbm.1), custom_call_target="tpu_custom_call" | custom-call | tf_op jit(solution)/shard_map/pallas_call | solution.py:381
  2.6 0.0 copy-start.5
  2.6 0.0 copy-start.2
  2.6 7.3 %all-to-all-start = ((bf16[32,8,256]{2,1,0:T(8,128)(2,1)}), bf16[32,8,256]{2,1,0:T(8,128)(2,1)S(1)}, u32[]{:S(2)}, u32[]{:S(2)}) async-start(bf16[32,8,256]{2,1,0:T(8,128)(2,1)} %bitcast.3), calls=%async_computation | async-start | bytes 262144 | tf_op jit(solution)/shard_map/all_to_all | solution.py:378
  9.9 0.0 copy-start.4
  9.9 0.0 copy-start.8
  9.9 0.0 copy-start.6
  9.9 0.0 copy-start.7
  9.9 0.0 copy-done.5
  10.0 0.6 %copy-done.4 = f32[4,256]{1,0:T(4,128)S(1)} copy-done((f32[4,256]{1,0:T(4,128)S(1)}, f32[4,256]{1,0:T(4,128)}, u32[]{:S(2)}) %copy-start.4) | copy-done | bytes 4120
  10.6 0.0 copy-done.8
  10.6 0.0 copy-done.6
  10.6 0.0 copy-done.7
  10.6 0.0 copy-start
  10.6 1.2 %copy-done = bf16[4,2,256,256]{3,2,1,0:T(8,128)(2,1)S(1)} copy-done((bf16[4,2,256,256]{3,2,1,0:T(8,128)(2,1)S(1)}, bf16[4,2,256,256]{3,2,1,0:T(8,128)(2,1)}, u32[]{:S(2)}) %copy-start) | copy-done | bytes 1048600
  11.8 0.0 copy-start.1
  11.8 0.0 copy-start.3
  11.8 0.3 shard_map.114
  12.2 6.0 %all-to-all-done = bf16[32,8,256]{2,1,0:T(8,128)(2,1)S(1)} async-done(((bf16[32,8,256]{2,1,0:T(8,128)(2,1)}), bf16[32,8,256]{2,1,0:T(8,128)(2,1)S(1)}, u32[]{:S(2)}, u32[]{:S(2)}) %all-to-all-start) | async-done | bytes 131104 | tf_op jit(solution)/shard_map/all_to_all | solution.py:378
  18.1 0.0 copy-done.2
  18.1 0.0 copy-done.1
  18.1 0.0 copy-done.3
  18.1 0.8 %shard_map.115 = (bf16[256,256]{1,0:T(8,128)(2,1)S(1)}, f32[8,256]{1,0:T(8,128)S(1)}, f32[8,256]{1,0:T(8,128)S(1)}) custom-call(f32[4,256]{1,0:T(4,128)S(1)} %copy-done.4, f32[8,256]{1,0:T(8,128)S(1)} %get-tuple-element.19.refs_1_, bf16[256,256]{1,0:T(8,128)(2,1)S(1)} %bitcast.9, bf16[64,256]{1,0:T(8,128)(2,1)S(1)} %get-tuple-element.21.refs_3_.refs_6_, ...), custom_call_target="tpu_custom_call" | custom-call | tf_op jit(solution)/shard_map/pallas_call | solution.py:399
  19.0 10.0 %all_to_all.38 = bf16[32,8,256]{2,1,0:T(8,128)(2,1)S(1)} all-to-all(bf16[32,8,256]{2,1,0:T(8,128)(2,1)S(1)} %bitcast.13), channel_id=1, replica_groups=mesh['leaf'=8,'sub'=4] {'leaf','sub'}, dimensions={0} | all-to-all | bytes 262144 | tf_op jit(solution)/shard_map/all_to_all | solution.py:378
  29.0 0.9 %shard_map.116 = (bf16[256,256]{1,0:T(8,128)(2,1)S(1)}, f32[8,256]{1,0:T(8,128)S(1)}, f32[8,256]{1,0:T(8,128)S(1)}, f32[8,128]{1,0:T(8,128)S(1)}) custom-call(f32[8,256]{1,0:T(8,128)S(1)} %get-tuple-element.23.refs_0_, f32[8,256]{1,0:T(8,128)S(1)} %get-tuple-element.24.refs_1_, bf16[256,256]{1,0:T(8,128)(2,1)S(1)} %bitcast.11, ...), custom_call_target="tpu_custom_call" | custom-call | tf_op jit(solution)/shard_map/pallas_call | solution.py:402
  29.9 10.0 %all_to_all.39 = bf16[32,8,256]{2,1,0:T(8,128)(2,1)S(1)} all-to-all(bf16[32,8,256]{2,1,0:T(8,128)(2,1)S(1)} %bitcast.12), channel_id=1, replica_groups=mesh['leaf'=8,'sub'=4] {'leaf','sub'}, dimensions={0} | all-to-all | bytes 262144 | tf_op jit(solution)/shard_map/all_to_all | solution.py:378
  39.9 0.8 %shard_map.117 = (f32[32,1,128]{2,1,0:T(1,128)S(1)}, f32[8,256]{1,0:T(8,128)S(1)}, f32[8,256]{1,0:T(8,128)S(1)}, f32[8,128]{1,0:T(8,128)S(1)}) custom-call(f32[8,256]{1,0:T(8,128)S(1)} %get-tuple-element.23.refs_0_, f32[8,256]{1,0:T(8,128)S(1)} %get-tuple-element.24.refs_1_, f32[8,256]{1,0:T(8,128)S(1)} %get-tuple-element.26.refs_2_.refs_1_, ...), custom_call_target="tpu_custom_call" | custom-call | tf_op jit(solution)/shard_map/pallas_call | solution.py:405
  40.7 8.9 %all_to_all.40.refs_5_ = f32[32,1,128]{2,1,0:T(1,128)S(1)} all-to-all(f32[32,1,128]{2,1,0:T(1,128)S(1)} %get-tuple-element.33), channel_id=1, replica_groups=mesh['leaf'=8,'sub'=4] {'leaf','sub'}, dimensions={0} | all-to-all | bytes 32768 | tf_op jit(solution)/shard_map/all_to_all | solution.py:378
  49.6 0.8 %shard_map.118 = (f32[4,4,256]{2,1,0:T(4,128)}, f32[4,3]{1,0:T(4,128)}) custom-call(f32[8,256]{1,0:T(8,128)S(1)} %get-tuple-element.23.refs_0_, f32[8,256]{1,0:T(8,128)S(1)} %get-tuple-element.26.refs_2_.refs_1_, f32[8,256]{1,0:T(8,128)S(1)} %get-tuple-element.30.refs_2_, f32[8,256]{1,0:T(8,128)S(1)} %get-tuple-element.31.refs_3_, ...), custom_call_target="tpu_custom_call" | custom-call | tf_op jit(solution)/shard_map/pallas_call | solution.py:410
Async XLA Ops:
  2.6 7.4 %copy-start.5 = (bf16[1,64,256]{2,1,0:T(8,128)(2,1)S(1)}, bf16[1,64,256]{2,1,0:T(8,128)(2,1)}, u32[]{:S(2)}) copy-start(bf16[1,64,256]{2,1,0:T(8,128)(2,1)} %refs_5_.1) | copy-start | bytes 98308
  2.6 15.6 %copy-start.2 = (bf16[4,64,256]{2,1,0:T(8,128)(2,1)S(1)}, bf16[4,64,256]{2,1,0:T(8,128)(2,1)}, u32[]{:S(2)}) copy-start(bf16[4,64,256]{2,1,0:T(8,128)(2,1)} %refs_10_.1) | copy-start | bytes 393220
  2.6 15.5 %all-to-all-start = ((bf16[32,8,256]{2,1,0:T(8,128)(2,1)}), bf16[32,8,256]{2,1,0:T(8,128)(2,1)S(1)}, u32[]{:S(2)}, u32[]{:S(2)}) async-start(bf16[32,8,256]{2,1,0:T(8,128)(2,1)} %bitcast.3), calls=%async_computation | async-start | bytes 262144 | tf_op jit(solution)/shard_map/all_to_all | solution.py:378
  9.9 0.7 %copy-start.4 = (f32[4,256]{1,0:T(4,128)S(1)}, f32[4,256]{1,0:T(4,128)}, u32[]{:S(2)}) copy-start(f32[4,256]{1,0:T(4,128)} %refs_0_.1) | copy-start | bytes 12292
  9.9 0.7 %copy-start.8 = (s32[1,4]{1,0:T(1,128)S(1)}, s32[1,4]{1,0:T(1,128)}, u32[]{:S(2)}) copy-start(s32[1,4]{1,0:T(1,128)} %refs_2_.1) | copy-start | bytes 52
  9.9 0.7 %copy-start.6 = (s32[4,2]{0,1:T(2,128)S(1)}, s32[4,2]{0,1:T(2,128)}, u32[]{:S(2)}) copy-start(s32[4,2]{0,1:T(2,128)} %param.13) | copy-start | bytes 100
  9.9 0.7 %copy-start.7 = (s32[4,1]{0,1:T(1,128)S(1)}, s32[4,1]{0,1:T(1,128)}, u32[]{:S(2)}) copy-start(s32[4,1]{0,1:T(1,128)} %param.12) | copy-start | bytes 52
  10.6 1.2 %copy-start = (bf16[4,2,256,256]{3,2,1,0:T(8,128)(2,1)S(1)}, bf16[4,2,256,256]{3,2,1,0:T(8,128)(2,1)}, u32[]{:S(2)}) copy-start(bf16[4,2,256,256]{3,2,1,0:T(8,128)(2,1)} %refs_7_.7) | copy-start | bytes 3145732
  11.8 6.3 %copy-start.1 = (bf16[4,2,256,256]{3,2,1,0:T(8,128)(2,1)S(1)}, bf16[4,2,256,256]{3,2,1,0:T(8,128)(2,1)}, u32[]{:S(2)}) copy-start(bf16[4,2,256,256]{3,2,1,0:T(8,128)(2,1)} %refs_7_.7) | copy-start | bytes 3145732
  11.8 6.3 %copy-start.3 = (bf16[4,64,128]{2,1,0:T(8,128)(2,1)S(1)}, bf16[4,64,128]{2,1,0:T(8,128)(2,1)}, u32[]{:S(2)}) copy-start(bf16[4,64,128]{2,1,0:T(8,128)(2,1)} %refs_9_.1) | copy-start | bytes 196612

commit v3 on v2

--- a/solution.py
+++ b/solution.py
@@ -40,8 +40,8 @@
     return total
 
 
-def in_lanes(values):
-    group = iota((ROWS, 128), 1) // 32
+def in_lanes(values, first, width):
+    group = iota((ROWS, 128), 1) // width - first // width
     out = jnp.zeros((ROWS, 128), F32)
     for index, value in enumerate(values):
         out = jnp.where(group == index, value, out)
@@ -65,28 +65,27 @@
     term = 0.5 * jnp.sum(dot_nt(coef.astype(BF16), reach2), axis=0, keepdims=True)
     coef = coef[:, :128] + coef[:, 128:]
     coef = coef + pltpu.roll(coef, rank, 1)
-    val = in_lanes(dots)
+    val = in_lanes(dots, rank, 16)
     rest = val - val.astype(BF16).astype(F32)
     last = rest - rest.astype(BF16).astype(F32)
-    row = iota((ROWS, 128), 0)
-    left = jnp.where(row < 4, vec[:, :128], coef)
-    right = jnp.where(row == 4, term, jnp.where(row == 5, val, jnp.where(row == 6, rest, last)))
-    right = jnp.where(row < 4, vec[:, 128:], right)
-    return twice(jnp.concatenate([left, right], axis=1)).astype(BF16)
+    row, low = iota((ROWS, 128), 0), iota((ROWS, 128), 1) < rank
+    third = jnp.where(row == 0, term, jnp.where(row == 1, val, jnp.where(row == 2, rest, last)))
+    third = jnp.where(low, coef, third)
+    return [part[:leaves, :].astype(BF16) for part in (vec[:, :128], vec[:, 128:], third)]
 
 
 def store_all(block, out_ref):
-    pairs = out_ref.shape[0] // 16
-    if pairs <= 32:
-        for p in range(pairs):
-            out_ref[16 * p : 16 * p + 16, :] = block
+    devices = out_ref.shape[0]
+
+    def store(device):
+        for part in range(3):
+            out_ref[device, part] = block[part]
+
+    if devices <= 32:
+        for device in range(devices):
+            store(device)
     else:
-
-        def store(p, carry):
-            out_ref[pl.ds(pl.multiple_of(16 * p, 16), 16), :] = block
-            return carry
-
-        lax.fori_loop(0, pairs, store, 0)
+        pl.loop(0, devices)(store)
 
 
 def first_kernel(
@@ -151,39 +150,36 @@
         kept = jnp.where(lane4 == row4, ids, 0).astype(F32)
         return jnp.sum(kept, axis=1, keepdims=True).astype(jnp.int32)
 
-    def leaf_column(index):
-        return 2 * index - index % leaves
-
     branch_leaves = subs * leaves
-    count = (width // ROWS) * leaves
     index = (branch - 1) * branch_leaves + by_row(near_ids)
-    inside = (index >= 0) & (index < count)
-    groups = [col == jnp.where(inside, leaf_column(jnp.maximum(index, 0)), -1)]
+    groups = [col == index]
     for s in range(2):
-        index = branch * branch_leaves + by_row(far_ids[s : s + 1, :])
-        groups.append(col == leaf_column(index) + leaves)
+        groups.append(col == branch * branch_leaves + by_row(far_ids[s : s + 1, :]))
     for s in range(4):
-        groups.append((col % ROWS == 4) & (col // (ROWS * subs) == top_ids[0:1, s : s + 1]))
-    groups.append(col % ROWS >= 5)
+        groups.append((col % leaves == 0) & (col // branch_leaves == top_ids[0:1, s : s + 1]))
+    groups.append(col % leaves > 0)
     pick_ref[...] = jnp.concatenate([g.astype(F32) for g in groups], axis=0).astype(BF16)
 
 
 def multiply(own_out, got_ref, pick_ref, near_ref, top_down_ref, coupling_ref, basis_ref):
     leaves, rank, size = basis_ref.shape
-    got = dot_nn(pick_ref[...], got_ref[...])
-    group = [got[ROWS * g : ROWS * g + ROWS, :] for g in range(8)]
+    got = [got_ref[:, part].reshape(-1, 128) for part in range(3)]
+    pick = pick_ref[...]
+    other = jnp.concatenate([dot_nn(pick[:ROWS], got[0]), dot_nn(pick[:ROWS], got[1])], axis=1)
+    rest = dot_nn(pick[ROWS:], got[2])
+    group = [rest[ROWS * g : ROWS * g + ROWS, :] for g in range(7)]
     low = iota((ROWS, 128), 1) < rank
-    far_in = jnp.where(low, group[1][:, :128], group[2][:, :128]).astype(BF16)
-    top_a = jnp.where(low, group[3][:, 128:], group[4][:, 128:]).astype(BF16)
-    top_b = jnp.where(low, group[5][:, 128:], group[6][:, 128:]).astype(BF16)
+    far_in = jnp.where(low, group[0], pltpu.roll(group[1], rank, 1)).astype(BF16)
+    top_a = jnp.where(low, pltpu.roll(group[2], rank, 1), group[3]).astype(BF16)
+    top_b = jnp.where(low, pltpu.roll(group[4], rank, 1), group[5]).astype(BF16)
     top_in = jnp.concatenate([top_a, top_b], axis=1)
     local = dot_nt(far_in, coupling_ref[...].reshape(leaves * rank, -1))
     local = local + dot_nt(top_in, top_down_ref[...])
     local = jnp.where(is_mine(local.shape, rank, leaves), local, 0.0).astype(BF16)
     far_out = dot_nn(local, basis_ref[...].reshape(leaves * rank, size))
-    other = group[0].astype(BF16)
+    other = other.astype(BF16)
     near_out = own_out + by_leaf([dot_nt(other, near_ref[l, 1]) for l in range(leaves)])
-    dots = [group[7][:, 128 + 32 * i : 129 + 32 * i] for i in range(4)]
+    dots = [group[6][:, rank + 16 * i : rank + 16 * i + 1] for i in range(4)]
     return near_out + far_out, dots
 
 
@@ -313,7 +309,7 @@
     table = entry(table_in_ref[...], 0, 1, h01)
     table = entry(table, 1, 1, h11)
     table_ref[...] = entry(table, 2, 1, h21)
-    val = in_lanes([inner(b0, w2), inner(b1, w2), inner(b2, w2), inner(w2, w2)])
+    val = in_lanes([inner(b0, w2), inner(b1, w2), inner(b2, w2), inner(w2, w2)], 0, 32)
     dots_ref[...] = jnp.broadcast_to(val[:1, :].reshape(1, 1, 128), dots_ref.shape)
 
 
@@ -370,7 +366,7 @@
     leaves, size = start_vec.shape
     rank = leaf_basis.shape[1]
     total = float(leaves * size * devices)
-    blocks = shaped((devices * ROWS, size), BF16)
+    blocks = shaped((devices, 3, leaves, size // 2), BF16)
     vec = shaped((ROWS, size))
     table = shaped((ROWS, 128))
 
@@ -390,7 +386,7 @@
         lambda *refs: setup_kernel(subs, *refs),
         [VMEM] * 8,
         [
-            shaped((8 * ROWS, devices * ROWS), BF16),
+            shaped((8 * ROWS, devices * leaves), BF16),
             shaped((leaves * rank, top_coupling.shape[2]), BF16),
             vec,
         ],

time: 50.8 us -> 49.5 us (0.974)
  blocking collectives: 28.9 us -> 27.9 us
    all_to_all x3, blocking collectives: 28.9 us -> 27.9 us  [exchange(): return lax.all_to_all(out, axes, 0, 0, tiled=True)]
where the time goes in v3:
time: 49.5 us; the launch traced here: 49.2 us
  blocking collectives  27.9 us (56%)
  starting transfers between devices  7.3 us (15%)
  Pallas kernels  5.81 us (12%)
  waiting for transfers between devices  5.54 us (11%)
  local copies, waits for them, and re-layouts  1.92 us (4%)
  between operations  0.75 us (2%)
    all_to_all x3, blocking collectives, exchange(): return lax.all_to_all(out, axes, 0, 0, tiled=True)  27.9 us
    all_to_all x1, starting transfers between devices, exchange(): return lax.all_to_all(out, axes, 0, 0, tiled=True)  7.3 us
    all_to_all x1, waiting for transfers between devices, exchange(): return lax.all_to_all(out, axes, 0, 0, tiled=True)  5.54 us
    unnamed x18, local copies, waits for them, and re-layouts  1.92 us
    pallas_call x1, Pallas kernels, per_device(): call(first_kernel, [HBM] * 4, [blocks, shaped((2 * rank, leaves * rank),...  1.9 us
    pallas_call x1, Pallas kernels, per_device(): call(lambda *refs: third_kernel(total, *refs), [VMEM] * 9, [blocks, vec,...  1.01 us
  transfers between devices with their start and end apart: 1, of which 1 were waited for; matrix products, arithmetic and copies ran while one was open for 0% of the time, Pallas kernels for 1%

profile of v3, /device:TPU:0, one launch (start us, length us, event | category | flops | bytes accessed | tf_op | source)
XLA Modules:
  0.0 49.2 jit_solution(3395431213908872362)
XLA Ops:
  0.6 1.9 %shard_map.113 = (bf16[32,3,4,128]{3,2,1,0:T(4,128)(2,1)}, bf16[128,256]{1,0:T(8,128)(2,1)S(1)}) custom-call(f32[4,256]{1,0:T(4,128)} %refs_0_.1, bf16[4,64,256]{2,1,0:T(8,128)(2,1)} %refs_10_.1, bf16[1,64,256]{2,1,0:T(8,128)(2,1)} %node_hbm.1, bf16[1,64,64]{2,1,0:T(8,128)(2,1)} %upper_hbm.1), custom_call_target="tpu_custom_call" | custom-call | tf_op jit(solution)/shard_map/pallas_call | solution.py:377
  2.5 0.0 copy-start.5
  2.6 0.0 copy-start.2
  2.6 7.3 %all-to-all-start = ((bf16[32,3,4,128]{3,2,1,0:T(4,128)(2,1)}), bf16[32,3,4,128]{3,2,1,0:T(4,128)(2,1)S(1)}, u32[]{:S(2)}, u32[]{:S(2)}) async-start(bf16[32,3,4,128]{3,2,1,0:T(4,128)(2,1)} %get-tuple-element.20), calls=%async_computation | async-start | bytes 196608 | tf_op jit(solution)/shard_map/all_to_all | solution.py:374
  9.9 0.0 copy-start.4
  9.9 0.0 copy-start.8
  9.9 0.0 copy-start.6
  9.9 0.0 copy-start.7
  9.9 0.0 copy-done.5
  9.9 0.6 %copy-done.4 = f32[4,256]{1,0:T(4,128)S(1)} copy-done((f32[4,256]{1,0:T(4,128)S(1)}, f32[4,256]{1,0:T(4,128)}, u32[]{:S(2)}) %copy-start.4) | copy-done | bytes 4120
  10.6 0.0 copy-done.8
  10.6 0.0 copy-done.6
  10.6 0.0 copy-done.7
  10.6 0.0 copy-start
  10.6 1.2 %copy-done = bf16[4,2,256,256]{3,2,1,0:T(8,128)(2,1)S(1)} copy-done((bf16[4,2,256,256]{3,2,1,0:T(8,128)(2,1)S(1)}, bf16[4,2,256,256]{3,2,1,0:T(8,128)(2,1)}, u32[]{:S(2)}) %copy-start) | copy-done | bytes 1048600
  11.8 0.0 copy-start.1
  11.8 0.0 copy-start.3
  11.8 0.3 shard_map.114
  12.1 5.5 %all-to-all-done.refs_2_ = bf16[32,3,4,128]{3,2,1,0:T(4,128)(2,1)S(1)} async-done(((bf16[32,3,4,128]{3,2,1,0:T(4,128)(2,1)}), bf16[32,3,4,128]{3,2,1,0:T(4,128)(2,1)S(1)}, u32[]{:S(2)}, u32[]{:S(2)}) %all-to-all-start) | async-done | bytes 98336 | tf_op jit(solution)/shard_map/all_to_all | solution.py:374
  17.7 0.0 copy-done.2
  17.7 0.0 copy-done.1
  17.7 0.0 copy-done.3
  17.7 0.9 %shard_map.115 = (bf16[32,3,4,128]{3,2,1,0:T(4,128)(2,1)S(1)}, f32[8,256]{1,0:T(8,128)S(1)}, f32[8,256]{1,0:T(8,128)S(1)}) custom-call(f32[4,256]{1,0:T(4,128)S(1)} %copy-done.4, f32[8,256]{1,0:T(8,128)S(1)} %get-tuple-element.19.refs_1_, bf16[32,3,4,128]{3,2,1,0:T(4,128)(2,1)S(1)} %all-to-all-done.refs_2_, ...), custom_call_target="tpu_custom_call" | custom-call | tf_op jit(solution)/shard_map/pallas_call | solution.py:395
  18.6 9.5 %all_to_all.20.refs_2_ = bf16[32,3,4,128]{3,2,1,0:T(4,128)(2,1)S(1)} all-to-all(bf16[32,3,4,128]{3,2,1,0:T(4,128)(2,1)S(1)} %get-tuple-element.25), channel_id=1, replica_groups=mesh['leaf'=8,'sub'=4] {'leaf','sub'}, dimensions={0} | all-to-all | bytes 196608 | tf_op jit(solution)/shard_map/all_to_all | solution.py:374
  28.1 1.0 %shard_map.116 = (bf16[32,3,4,128]{3,2,1,0:T(4,128)(2,1)S(1)}, f32[8,256]{1,0:T(8,128)S(1)}, f32[8,256]{1,0:T(8,128)S(1)}, f32[8,128]{1,0:T(8,128)S(1)}) custom-call(f32[8,256]{1,0:T(8,128)S(1)} %get-tuple-element.23.refs_0_, f32[8,256]{1,0:T(8,128)S(1)} %get-tuple-element.24.refs_1_, bf16[32,3,4,128]{3,2,1,0:T(4,128)(2,1)S(1)} %all_to_all.20.refs_2_, ...), custom_call_target="tpu_custom_call" | custom-call | tf_op jit(solution)/shard_map/pallas_call | solution.py:398
  29.1 9.5 %all_to_all.21.refs_5_ = bf16[32,3,4,128]{3,2,1,0:T(4,128)(2,1)S(1)} all-to-all(bf16[32,3,4,128]{3,2,1,0:T(4,128)(2,1)S(1)} %get-tuple-element.29), channel_id=1, replica_groups=mesh['leaf'=8,'sub'=4] {'leaf','sub'}, dimensions={0} | all-to-all | bytes 196608 | tf_op jit(solution)/shard_map/all_to_all | solution.py:374
  38.6 0.9 %shard_map.117 = (f32[32,1,128]{2,1,0:T(1,128)S(1)}, f32[8,256]{1,0:T(8,128)S(1)}, f32[8,256]{1,0:T(8,128)S(1)}, f32[8,128]{1,0:T(8,128)S(1)}) custom-call(f32[8,256]{1,0:T(8,128)S(1)} %get-tuple-element.23.refs_0_, f32[8,256]{1,0:T(8,128)S(1)} %get-tuple-element.24.refs_1_, f32[8,256]{1,0:T(8,128)S(1)} %get-tuple-element.26.refs_2_.refs_1_, ...), custom_call_target="tpu_custom_call" | custom-call | tf_op jit(solution)/shard_map/pallas_call | solution.py:401
  39.5 8.8 %all_to_all.22.refs_5_ = f32[32,1,128]{2,1,0:T(1,128)S(1)} all-to-all(f32[32,1,128]{2,1,0:T(1,128)S(1)} %get-tuple-element.33), channel_id=1, replica_groups=mesh['leaf'=8,'sub'=4] {'leaf','sub'}, dimensions={0} | all-to-all | bytes 32768 | tf_op jit(solution)/shard_map/all_to_all | solution.py:374
  48.3 0.8 %shard_map.118 = (f32[4,4,256]{2,1,0:T(4,128)}, f32[4,3]{1,0:T(4,128)}) custom-call(f32[8,256]{1,0:T(8,128)S(1)} %get-tuple-element.23.refs_0_, f32[8,256]{1,0:T(8,128)S(1)} %get-tuple-element.26.refs_2_.refs_1_, f32[8,256]{1,0:T(8,128)S(1)} %get-tuple-element.30.refs_2_, f32[8,256]{1,0:T(8,128)S(1)} %get-tuple-element.31.refs_3_, ...), custom_call_target="tpu_custom_call" | custom-call | tf_op jit(solution)/shard_map/pallas_call | solution.py:406
Async XLA Ops:
  2.5 7.4 %copy-start.5 = (bf16[1,64,256]{2,1,0:T(8,128)(2,1)S(1)}, bf16[1,64,256]{2,1,0:T(8,128)(2,1)}, u32[]{:S(2)}) copy-start(bf16[1,64,256]{2,1,0:T(8,128)(2,1)} %refs_5_.1) | copy-start | bytes 98308
  2.6 15.1 %copy-start.2 = (bf16[4,64,256]{2,1,0:T(8,128)(2,1)S(1)}, bf16[4,64,256]{2,1,0:T(8,128)(2,1)}, u32[]{:S(2)}) copy-start(bf16[4,64,256]{2,1,0:T(8,128)(2,1)} %refs_10_.1) | copy-start | bytes 393220
  2.6 15.1 %all-to-all-start = ((bf16[32,3,4,128]{3,2,1,0:T(4,128)(2,1)}), bf16[32,3,4,128]{3,2,1,0:T(4,128)(2,1)S(1)}, u32[]{:S(2)}, u32[]{:S(2)}) async-start(bf16[32,3,4,128]{3,2,1,0:T(4,128)(2,1)} %get-tuple-element.20), calls=%async_computation | async-start | bytes 196608 | tf_op jit(solution)/shard_map/all_to_all | solution.py:374
  9.9 0.7 %copy-start.4 = (f32[4,256]{1,0:T(4,128)S(1)}, f32[4,256]{1,0:T(4,128)}, u32[]{:S(2)}) copy-start(f32[4,256]{1,0:T(4,128)} %refs_0_.1) | copy-start | bytes 12292
  9.9 0.7 %copy-start.8 = (s32[1,4]{1,0:T(1,128)S(1)}, s32[1,4]{1,0:T(1,128)}, u32[]{:S(2)}) copy-start(s32[1,4]{1,0:T(1,128)} %refs_2_.1) | copy-start | bytes 52
  9.9 0.7 %copy-start.6 = (s32[4,2]{0,1:T(2,128)S(1)}, s32[4,2]{0,1:T(2,128)}, u32[]{:S(2)}) copy-start(s32[4,2]{0,1:T(2,128)} %param.13) | copy-start | bytes 100
  9.9 0.7 %copy-start.7 = (s32[4,1]{0,1:T(1,128)S(1)}, s32[4,1]{0,1:T(1,128)}, u32[]{:S(2)}) copy-start(s32[4,1]{0,1:T(1,128)} %param.12) | copy-start | bytes 52
  10.6 1.2 %copy-start = (bf16[4,2,256,256]{3,2,1,0:T(8,128)(2,1)S(1)}, bf16[4,2,256,256]{3,2,1,0:T(8,128)(2,1)}, u32[]{:S(2)}) copy-start(bf16[4,2,256,256]{3,2,1,0:T(8,128)(2,1)} %refs_7_.7) | copy-start | bytes 3145732
  11.8 5.9 %copy-start.1 = (bf16[4,2,256,256]{3,2,1,0:T(8,128)(2,1)S(1)}, bf16[4,2,256,256]{3,2,1,0:T(8,128)(2,1)}, u32[]{:S(2)}) copy-start(bf16[4,2,256,256]{3,2,1,0:T(8,128)(2,1)} %refs_7_.7) | copy-start | bytes 3145732
  11.8 5.9 %copy-start.3 = (bf16[4,64,128]{2,1,0:T(8,128)(2,1)S(1)}, bf16[4,64,128]{2,1,0:T(8,128)(2,1)}, u32[]{:S(2)}) copy-start(bf16[4,64,128]{2,1,0:T(8,128)(2,1)} %refs_9_.1) | copy-start | bytes 196612

commit v4 on v3

--- a/solution.py
+++ b/solution.py
@@ -161,12 +161,13 @@
     pick_ref[...] = jnp.concatenate([g.astype(F32) for g in groups], axis=0).astype(BF16)
 
 
-def multiply(own_out, got_ref, pick_ref, near_ref, top_down_ref, coupling_ref, basis_ref):
+def multiply(own, got_ref, pick_ref, near_ref, top_down_ref, coupling_ref, basis_ref):
     leaves, rank, size = basis_ref.shape
     got = [got_ref[:, part].reshape(-1, 128) for part in range(3)]
     pick = pick_ref[...]
+    rest = dot_nn(pick[ROWS:], got[2])
     other = jnp.concatenate([dot_nn(pick[:ROWS], got[0]), dot_nn(pick[:ROWS], got[1])], axis=1)
-    rest = dot_nn(pick[ROWS:], got[2])
+    near_out = own()
     group = [rest[ROWS * g : ROWS * g + ROWS, :] for g in range(7)]
     low = iota((ROWS, 128), 1) < rank
     far_in = jnp.where(low, group[0], pltpu.roll(group[1], rank, 1)).astype(BF16)
@@ -175,10 +176,10 @@
     top_in = jnp.concatenate([top_a, top_b], axis=1)
     local = dot_nt(far_in, coupling_ref[...].reshape(leaves * rank, -1))
     local = local + dot_nt(top_in, top_down_ref[...])
+    other = other.astype(BF16)
+    near_out = near_out + by_leaf([dot_nt(other, near_ref[l, 1]) for l in range(leaves)])
     local = jnp.where(is_mine(local.shape, rank, leaves), local, 0.0).astype(BF16)
     far_out = dot_nn(local, basis_ref[...].reshape(leaves * rank, size))
-    other = other.astype(BF16)
-    near_out = own_out + by_leaf([dot_nt(other, near_ref[l, 1]) for l in range(leaves)])
     dots = [group[6][:, rank + 16 * i : rank + 16 * i + 1] for i in range(4)]
     return near_out + far_out, dots
 
@@ -192,7 +193,8 @@
     remain = square
     for head in heads:
         remain = remain - head * head
-    return jnp.sqrt(jnp.maximum(remain, 0.01 * square))
+    remain = jnp.maximum(remain, 0.01 * square)
+    return jnp.sqrt(remain), lax.rsqrt(remain)
 
 
 def second_kernel(
@@ -212,9 +214,9 @@
 ):
     start = twice(start_ref[...])
     image, dots = multiply(
-        own_ref[...], got_ref, pick_ref, near_ref, top_down_ref, coupling_ref, basis_ref
-    )
-    scale = lax.rsqrt(dots[0] / total + 1e-06)
+        lambda: own_ref[...], got_ref, pick_ref, near_ref, top_down_ref, coupling_ref, basis_ref
+    )
+    scale = lax.rsqrt(dots[0] * (1.0 / total) + 1e-06)
     b0 = scale * start
     k1 = scale * image
     w0 = 0.5 * b0 + k1
@@ -242,7 +244,7 @@
 ):
     k1 = k1_ref[...]
     image, dots = multiply(
-        own_part(k1, near_ref),
+        lambda: own_part(k1, near_ref),
         got_ref,
         pick_ref,
         near_ref,
@@ -251,9 +253,8 @@
         basis_ref,
     )
     b0 = b0_ref[...]
-    h00 = dots[0] / total
-    h10 = norm_of(dots[1] / total, [h00])
-    inv = 1.0 / h10
+    h00 = dots[0] * (1.0 / total)
+    h10, inv = norm_of(dots[1] * (1.0 / total), [h00])
     shift = 0.5 - h00
     b1 = (shift * b0 + k1) * inv
     k2 = (shift * k1 + image) * inv
@@ -287,7 +288,7 @@
 ):
     k2 = k2_ref[...]
     image, dots = multiply(
-        own_part(k2, near_ref),
+        lambda: own_part(k2, near_ref),
         got_ref,
         pick_ref,
         near_ref,
@@ -296,10 +297,9 @@
         basis_ref,
     )
     b0, k1, b1 = b0_ref[...], k1_ref[...], b1_ref[...]
-    h01 = dots[0] / total
-    h11 = dots[1] / total
-    h21 = norm_of(dots[2] / total, [h01, h11])
-    inv = 1.0 / h21
+    h01 = dots[0] * (1.0 / total)
+    h11 = dots[1] * (1.0 / total)
+    h21, inv = norm_of(dots[2] * (1.0 / total), [h01, h11])
     shift = 0.5 - h11
     b2 = (shift * b1 + k2 - h01 * b0) * inv
     k3 = (shift * k2 + image - h01 * k1) * inv
@@ -317,15 +317,15 @@
     total, b0_ref, b1_ref, b2_ref, w2_ref, table_ref, dots_ref, out_ref, hessen_ref
 ):
     leaves = out_ref.shape[1]
-    sums = jnp.sum(dots_ref[...], axis=0)
-    dots = [sums[:, 32 * i : 32 * i + 1] / total for i in range(4)]
+    sums = jnp.sum(dots_ref[...], axis=0) * (1.0 / total)
+    dots = [sums[:, 32 * i : 32 * i + 1] for i in range(4)]
     b0, b1, b2 = b0_ref[:leaves, :], b1_ref[:leaves, :], b2_ref[:leaves, :]
-    scale = norm_of(dots[3], dots[:3])
+    scale, inv = norm_of(dots[3], dots[:3])
     update = w2_ref[:leaves, :] - dots[0] * b0 - dots[1] * b1 - dots[2] * b2
     out_ref[0] = b0
     out_ref[1] = b1
     out_ref[2] = b2
-    out_ref[3] = update * (1.0 / scale)
+    out_ref[3] = update * inv
     table = table_ref[...]
     for i in range(3):
         table = entry(table, i, 2, dots[i])

time: 49.5 us -> 48.8 us (0.986)
  Pallas kernels: 5.81 us -> 5.11 us
where the time goes in v4:
time: 48.8 us; the launch traced here: 48.5 us
  blocking collectives  27.9 us (57%)
  starting transfers between devices  7.3 us (15%)
  waiting for transfers between devices  5.54 us (11%)
  Pallas kernels  5.11 us (10%)
  local copies, waits for them, and re-layouts  1.92 us (4%)
  between operations  0.75 us (2%)
    all_to_all x3, blocking collectives, exchange(): return lax.all_to_all(out, axes, 0, 0, tiled=True)  27.9 us
    all_to_all x1, starting transfers between devices, exchange(): return lax.all_to_all(out, axes, 0, 0, tiled=True)  7.3 us
    all_to_all x1, waiting for transfers between devices, exchange(): return lax.all_to_all(out, axes, 0, 0, tiled=True)  5.54 us
    unnamed x18, local copies, waits for them, and re-layouts  1.92 us
    pallas_call x1, Pallas kernels, per_device(): call(first_kernel, [HBM] * 4, [blocks, shaped((2 * rank, leaves * rank),...  1.9 us
  transfers between devices with their start and end apart: 1, of which 1 were waited for; matrix products, arithmetic and copies ran while one was open for 0% of the time, Pallas kernels for 1%

profile of v4, /device:TPU:0, one launch (start us, length us, event | category | flops | bytes accessed | tf_op | source)
XLA Modules:
  0.0 48.5 jit_solution(6821466217116260236)
XLA Ops:
  0.6 1.9 %shard_map.113 = (bf16[32,3,4,128]{3,2,1,0:T(4,128)(2,1)}, bf16[128,256]{1,0:T(8,128)(2,1)S(1)}) custom-call(f32[4,256]{1,0:T(4,128)} %refs_0_.1, bf16[4,64,256]{2,1,0:T(8,128)(2,1)} %refs_10_.1, bf16[1,64,256]{2,1,0:T(8,128)(2,1)} %node_hbm.1, bf16[1,64,64]{2,1,0:T(8,128)(2,1)} %upper_hbm.1), custom_call_target="tpu_custom_call" | custom-call | tf_op jit(solution)/shard_map/pallas_call | solution.py:377
  2.5 0.0 copy-start.5
  2.6 0.0 copy-start.2
  2.6 7.3 %all-to-all-start = ((bf16[32,3,4,128]{3,2,1,0:T(4,128)(2,1)}), bf16[32,3,4,128]{3,2,1,0:T(4,128)(2,1)S(1)}, u32[]{:S(2)}, u32[]{:S(2)}) async-start(bf16[32,3,4,128]{3,2,1,0:T(4,128)(2,1)} %get-tuple-element.20), calls=%async_computation | async-start | bytes 196608 | tf_op jit(solution)/shard_map/all_to_all | solution.py:374
  9.9 0.0 copy-start.4
  9.9 0.0 copy-start.8
  9.9 0.0 copy-start.6
  9.9 0.0 copy-start.7
  9.9 0.0 copy-done.5
  9.9 0.6 %copy-done.4 = f32[4,256]{1,0:T(4,128)S(1)} copy-done((f32[4,256]{1,0:T(4,128)S(1)}, f32[4,256]{1,0:T(4,128)}, u32[]{:S(2)}) %copy-start.4) | copy-done | bytes 4120
  10.6 0.0 copy-done.8
  10.6 0.0 copy-done.6
  10.6 0.0 copy-done.7
  10.6 0.0 copy-start
  10.6 1.2 %copy-done = bf16[4,2,256,256]{3,2,1,0:T(8,128)(2,1)S(1)} copy-done((bf16[4,2,256,256]{3,2,1,0:T(8,128)(2,1)S(1)}, bf16[4,2,256,256]{3,2,1,0:T(8,128)(2,1)}, u32[]{:S(2)}) %copy-start) | copy-done | bytes 1048600
  11.8 0.0 copy-start.1
  11.8 0.0 copy-start.3
  11.8 0.3 shard_map.114
  12.1 5.5 %all-to-all-done.refs_2_ = bf16[32,3,4,128]{3,2,1,0:T(4,128)(2,1)S(1)} async-done(((bf16[32,3,4,128]{3,2,1,0:T(4,128)(2,1)}), bf16[32,3,4,128]{3,2,1,0:T(4,128)(2,1)S(1)}, u32[]{:S(2)}, u32[]{:S(2)}) %all-to-all-start) | async-done | bytes 98336 | tf_op jit(solution)/shard_map/all_to_all | solution.py:374
  17.7 0.0 copy-done.2
  17.7 0.0 copy-done.1
  17.7 0.0 copy-done.3
  17.7 0.7 %shard_map.115 = (bf16[32,3,4,128]{3,2,1,0:T(4,128)(2,1)S(1)}, f32[8,256]{1,0:T(8,128)S(1)}, f32[8,256]{1,0:T(8,128)S(1)}) custom-call(f32[4,256]{1,0:T(4,128)S(1)} %copy-done.4, f32[8,256]{1,0:T(8,128)S(1)} %get-tuple-element.19.refs_1_, bf16[32,3,4,128]{3,2,1,0:T(4,128)(2,1)S(1)} %all-to-all-done.refs_2_, ...), custom_call_target="tpu_custom_call" | custom-call | tf_op jit(solution)/shard_map/pallas_call | solution.py:395
  18.4 9.5 %all_to_all.20.refs_2_ = bf16[32,3,4,128]{3,2,1,0:T(4,128)(2,1)S(1)} all-to-all(bf16[32,3,4,128]{3,2,1,0:T(4,128)(2,1)S(1)} %get-tuple-element.25), channel_id=1, replica_groups=mesh['leaf'=8,'sub'=4] {'leaf','sub'}, dimensions={0} | all-to-all | bytes 196608 | tf_op jit(solution)/shard_map/all_to_all | solution.py:374
  27.9 0.7 %shard_map.116 = (bf16[32,3,4,128]{3,2,1,0:T(4,128)(2,1)S(1)}, f32[8,256]{1,0:T(8,128)S(1)}, f32[8,256]{1,0:T(8,128)S(1)}, f32[8,128]{1,0:T(8,128)S(1)}) custom-call(f32[8,256]{1,0:T(8,128)S(1)} %get-tuple-element.23.refs_0_, f32[8,256]{1,0:T(8,128)S(1)} %get-tuple-element.24.refs_1_, bf16[32,3,4,128]{3,2,1,0:T(4,128)(2,1)S(1)} %all_to_all.20.refs_2_, ...), custom_call_target="tpu_custom_call" | custom-call | tf_op jit(solution)/shard_map/pallas_call | solution.py:398
  28.7 9.5 %all_to_all.21.refs_5_ = bf16[32,3,4,128]{3,2,1,0:T(4,128)(2,1)S(1)} all-to-all(bf16[32,3,4,128]{3,2,1,0:T(4,128)(2,1)S(1)} %get-tuple-element.29), channel_id=1, replica_groups=mesh['leaf'=8,'sub'=4] {'leaf','sub'}, dimensions={0} | all-to-all | bytes 196608 | tf_op jit(solution)/shard_map/all_to_all | solution.py:374
  38.2 0.6 %shard_map.117 = (f32[32,1,128]{2,1,0:T(1,128)S(1)}, f32[8,256]{1,0:T(8,128)S(1)}, f32[8,256]{1,0:T(8,128)S(1)}, f32[8,128]{1,0:T(8,128)S(1)}) custom-call(f32[8,256]{1,0:T(8,128)S(1)} %get-tuple-element.23.refs_0_, f32[8,256]{1,0:T(8,128)S(1)} %get-tuple-element.24.refs_1_, f32[8,256]{1,0:T(8,128)S(1)} %get-tuple-element.26.refs_2_.refs_1_, ...), custom_call_target="tpu_custom_call" | custom-call | tf_op jit(solution)/shard_map/pallas_call | solution.py:401
  38.8 8.8 %all_to_all.22.refs_5_ = f32[32,1,128]{2,1,0:T(1,128)S(1)} all-to-all(f32[32,1,128]{2,1,0:T(1,128)S(1)} %get-tuple-element.33), channel_id=1, replica_groups=mesh['leaf'=8,'sub'=4] {'leaf','sub'}, dimensions={0} | all-to-all | bytes 32768 | tf_op jit(solution)/shard_map/all_to_all | solution.py:374
  47.6 0.8 %shard_map.118 = (f32[4,4,256]{2,1,0:T(4,128)}, f32[4,3]{1,0:T(4,128)}) custom-call(f32[8,256]{1,0:T(8,128)S(1)} %get-tuple-element.23.refs_0_, f32[8,256]{1,0:T(8,128)S(1)} %get-tuple-element.26.refs_2_.refs_1_, f32[8,256]{1,0:T(8,128)S(1)} %get-tuple-element.30.refs_2_, f32[8,256]{1,0:T(8,128)S(1)} %get-tuple-element.31.refs_3_, ...), custom_call_target="tpu_custom_call" | custom-call | tf_op jit(solution)/shard_map/pallas_call | solution.py:406
Async XLA Ops:
  2.5 7.4 %copy-start.5 = (bf16[1,64,256]{2,1,0:T(8,128)(2,1)S(1)}, bf16[1,64,256]{2,1,0:T(8,128)(2,1)}, u32[]{:S(2)}) copy-start(bf16[1,64,256]{2,1,0:T(8,128)(2,1)} %refs_5_.1) | copy-start | bytes 98308
  2.6 15.1 %copy-start.2 = (bf16[4,64,256]{2,1,0:T(8,128)(2,1)S(1)}, bf16[4,64,256]{2,1,0:T(8,128)(2,1)}, u32[]{:S(2)}) copy-start(bf16[4,64,256]{2,1,0:T(8,128)(2,1)} %refs_10_.1) | copy-start | bytes 393220
  2.6 15.1 %all-to-all-start = ((bf16[32,3,4,128]{3,2,1,0:T(4,128)(2,1)}), bf16[32,3,4,128]{3,2,1,0:T(4,128)(2,1)S(1)}, u32[]{:S(2)}, u32[]{:S(2)}) async-start(bf16[32,3,4,128]{3,2,1,0:T(4,128)(2,1)} %get-tuple-element.20), calls=%async_computation | async-start | bytes 196608 | tf_op jit(solution)/shard_map/all_to_all | solution.py:374
  9.9 0.7 %copy-start.4 = (f32[4,256]{1,0:T(4,128)S(1)}, f32[4,256]{1,0:T(4,128)}, u32[]{:S(2)}) copy-start(f32[4,256]{1,0:T(4,128)} %refs_0_.1) | copy-start | bytes 12292
  9.9 0.7 %copy-start.8 = (s32[1,4]{1,0:T(1,128)S(1)}, s32[1,4]{1,0:T(1,128)}, u32[]{:S(2)}) copy-start(s32[1,4]{1,0:T(1,128)} %refs_2_.1) | copy-start | bytes 52
  9.9 0.7 %copy-start.6 = (s32[4,2]{0,1:T(2,128)S(1)}, s32[4,2]{0,1:T(2,128)}, u32[]{:S(2)}) copy-start(s32[4,2]{0,1:T(2,128)} %param.13) | copy-start | bytes 100
  9.9 0.7 %copy-start.7 = (s32[4,1]{0,1:T(1,128)S(1)}, s32[4,1]{0,1:T(1,128)}, u32[]{:S(2)}) copy-start(s32[4,1]{0,1:T(1,128)} %param.12) | copy-start | bytes 52
  10.6 1.2 %copy-start = (bf16[4,2,256,256]{3,2,1,0:T(8,128)(2,1)S(1)}, bf16[4,2,256,256]{3,2,1,0:T(8,128)(2,1)}, u32[]{:S(2)}) copy-start(bf16[4,2,256,256]{3,2,1,0:T(8,128)(2,1)} %refs_7_.7) | copy-start | bytes 3145732
  11.8 5.9 %copy-start.1 = (bf16[4,2,256,256]{3,2,1,0:T(8,128)(2,1)S(1)}, bf16[4,2,256,256]{3,2,1,0:T(8,128)(2,1)}, u32[]{:S(2)}) copy-start(bf16[4,2,256,256]{3,2,1,0:T(8,128)(2,1)} %refs_7_.7) | copy-start | bytes 3145732
  11.8 5.9 %copy-start.3 = (bf16[4,64,128]{2,1,0:T(8,128)(2,1)S(1)}, bf16[4,64,128]{2,1,0:T(8,128)(2,1)}, u32[]{:S(2)}) copy-start(bf16[4,64,128]{2,1,0:T(8,128)(2,1)} %refs_9_.1) | copy-start | bytes 196612

commit v5 on v4

--- a/solution.py
+++ b/solution.py
@@ -150,13 +150,20 @@
         kept = jnp.where(lane4 == row4, ids, 0).astype(F32)
         return jnp.sum(kept, axis=1, keepdims=True).astype(jnp.int32)
 
-    branch_leaves = subs * leaves
-    index = (branch - 1) * branch_leaves + by_row(near_ids)
-    groups = [col == index]
+    branches = width // (subs * leaves)
+
+    def column(at, index):
+        return ((index // leaves) * branches + at) * leaves + index % leaves
+
+    ids = by_row(near_ids)
+    at = branch - 1 + ids // (subs * leaves)
+    inside = (at >= 0) & (at < branches)
+    groups = [col == jnp.where(inside, column(at, ids % (subs * leaves)), -1)]
     for s in range(2):
-        groups.append(col == branch * branch_leaves + by_row(far_ids[s : s + 1, :]))
+        groups.append(col == column(branch, by_row(far_ids[s : s + 1, :])))
     for s in range(4):
-        groups.append((col % leaves == 0) & (col // branch_leaves == top_ids[0:1, s : s + 1]))
+        at = (col // leaves) % branches
+        groups.append((col % leaves == 0) & (at == top_ids[0:1, s : s + 1]))
     groups.append(col % leaves > 0)
     pick_ref[...] = jnp.concatenate([g.astype(F32) for g in groups], axis=0).astype(BF16)
 
@@ -360,7 +367,6 @@
     top_ids,
     top_coupling,
 ):
-    axes = ("leaf", "sub")
     subs = lax.axis_size("sub")
     devices = lax.axis_size("leaf") * subs
     leaves, size = start_vec.shape
@@ -371,7 +377,7 @@
     table = shaped((ROWS, 128))
 
     def exchange(out):
-        return lax.all_to_all(out, axes, 0, 0, tiled=True)
+        return lax.all_to_all(out, ("sub", "leaf"), 0, 0, tiled=True)
 
     sources = (start_vec, leaf_basis, node_transfer, branch_transfer)
     out, reach2 = call(

time: 48.8 us -> 48.1 us (0.986)
  no operation moved by 1% of the time
where the time goes in v5:
time: 48.1 us; the launch traced here: 47.8 us
  blocking collectives  27.5 us (57%)
  starting transfers between devices  7.3 us (15%)
  waiting for transfers between devices  5.3 us (11%)
  Pallas kernels  5.1 us (11%)
  local copies, waits for them, and re-layouts  1.92 us (4%)
  between operations  0.74 us (2%)
    all_to_all x3, blocking collectives, exchange(): return lax.all_to_all(out, ('sub', 'leaf'), 0, 0, tiled=True)  27.5 us
    all_to_all x1, starting transfers between devices, exchange(): return lax.all_to_all(out, ('sub', 'leaf'), 0, 0, tiled=True)  7.3 us
    all_to_all x1, waiting for transfers between devices, exchange(): return lax.all_to_all(out, ('sub', 'leaf'), 0, 0, tiled=True)  5.3 us
    unnamed x18, local copies, waits for them, and re-layouts  1.92 us
    pallas_call x1, Pallas kernels, per_device(): call(first_kernel, [HBM] * 4, [blocks, shaped((2 * rank, leaves * rank),...  1.9 us
  transfers between devices with their start and end apart: 1, of which 1 were waited for; matrix products, arithmetic and copies ran while one was open for 0% of the time, Pallas kernels for 1%

profile of v5, /device:TPU:0, one launch (start us, length us, event | category | flops | bytes accessed | tf_op | source)
XLA Modules:
  0.0 47.8 jit_solution(12595904169794071386)
XLA Ops:
  0.6 1.9 %shard_map.113 = (bf16[32,3,4,128]{3,2,1,0:T(4,128)(2,1)}, bf16[128,256]{1,0:T(8,128)(2,1)S(1)}) custom-call(f32[4,256]{1,0:T(4,128)} %refs_0_.1, bf16[4,64,256]{2,1,0:T(8,128)(2,1)} %refs_10_.1, bf16[1,64,256]{2,1,0:T(8,128)(2,1)} %node_hbm.1, bf16[1,64,64]{2,1,0:T(8,128)(2,1)} %upper_hbm.1), custom_call_target="tpu_custom_call" | custom-call | tf_op jit(solution)/shard_map/pallas_call | solution.py:383
  2.5 0.0 copy-start.5
  2.6 0.0 copy-start.2
  2.6 7.3 %all-to-all-start = ((bf16[32,3,4,128]{3,2,1,0:T(4,128)(2,1)}), bf16[32,3,4,128]{3,2,1,0:T(4,128)(2,1)S(1)}, u32[]{:S(2)}, u32[]{:S(2)}) async-start(bf16[32,3,4,128]{3,2,1,0:T(4,128)(2,1)} %get-tuple-element.20), calls=%async_computation | async-start | bytes 196608 | tf_op jit(solution)/shard_map/all_to_all | solution.py:380
  9.9 0.0 copy-start.4
  9.9 0.0 copy-start.8
  9.9 0.0 copy-start.6
  9.9 0.0 copy-start.7
  9.9 0.0 copy-done.5
  9.9 0.6 %copy-done.4 = f32[4,256]{1,0:T(4,128)S(1)} copy-done((f32[4,256]{1,0:T(4,128)S(1)}, f32[4,256]{1,0:T(4,128)}, u32[]{:S(2)}) %copy-start.4) | copy-done | bytes 4120
  10.6 0.0 copy-done.8
  10.6 0.0 copy-done.6
  10.6 0.0 copy-done.7
  10.6 0.0 copy-start
  10.6 1.2 %copy-done = bf16[4,2,256,256]{3,2,1,0:T(8,128)(2,1)S(1)} copy-done((bf16[4,2,256,256]{3,2,1,0:T(8,128)(2,1)S(1)}, bf16[4,2,256,256]{3,2,1,0:T(8,128)(2,1)}, u32[]{:S(2)}) %copy-start) | copy-done | bytes 1048600
  11.8 0.0 copy-start.1
  11.8 0.0 copy-start.3
  11.8 0.3 shard_map.114
  12.1 5.3 %all-to-all-done.refs_2_ = bf16[32,3,4,128]{3,2,1,0:T(4,128)(2,1)S(1)} async-done(((bf16[32,3,4,128]{3,2,1,0:T(4,128)(2,1)}), bf16[32,3,4,128]{3,2,1,0:T(4,128)(2,1)S(1)}, u32[]{:S(2)}, u32[]{:S(2)}) %all-to-all-start) | async-done | bytes 98336 | tf_op jit(solution)/shard_map/all_to_all | solution.py:380
  17.4 0.0 copy-done.2
  17.4 0.0 copy-done.1
  17.4 0.0 copy-done.3
  17.4 0.7 %shard_map.115 = (bf16[32,3,4,128]{3,2,1,0:T(4,128)(2,1)S(1)}, f32[8,256]{1,0:T(8,128)S(1)}, f32[8,256]{1,0:T(8,128)S(1)}) custom-call(f32[4,256]{1,0:T(4,128)S(1)} %copy-done.4, f32[8,256]{1,0:T(8,128)S(1)} %get-tuple-element.19.refs_1_, bf16[32,3,4,128]{3,2,1,0:T(4,128)(2,1)S(1)} %all-to-all-done.refs_2_, ...), custom_call_target="tpu_custom_call" | custom-call | tf_op jit(solution)/shard_map/pallas_call | solution.py:401
  18.2 9.3 %all_to_all.20.refs_2_ = bf16[32,3,4,128]{3,2,1,0:T(4,128)(2,1)S(1)} all-to-all(bf16[32,3,4,128]{3,2,1,0:T(4,128)(2,1)S(1)} %get-tuple-element.25), channel_id=1, replica_groups=mesh['leaf'=8,'sub'=4] {'sub','leaf'}, dimensions={0} | all-to-all | bytes 196608 | tf_op jit(solution)/shard_map/all_to_all | solution.py:380
  27.5 0.7 %shard_map.116 = (bf16[32,3,4,128]{3,2,1,0:T(4,128)(2,1)S(1)}, f32[8,256]{1,0:T(8,128)S(1)}, f32[8,256]{1,0:T(8,128)S(1)}, f32[8,128]{1,0:T(8,128)S(1)}) custom-call(f32[8,256]{1,0:T(8,128)S(1)} %get-tuple-element.23.refs_0_, f32[8,256]{1,0:T(8,128)S(1)} %get-tuple-element.24.refs_1_, bf16[32,3,4,128]{3,2,1,0:T(4,128)(2,1)S(1)} %all_to_all.20.refs_2_, ...), custom_call_target="tpu_custom_call" | custom-call | tf_op jit(solution)/shard_map/pallas_call | solution.py:404
  28.2 9.3 %all_to_all.21.refs_5_ = bf16[32,3,4,128]{3,2,1,0:T(4,128)(2,1)S(1)} all-to-all(bf16[32,3,4,128]{3,2,1,0:T(4,128)(2,1)S(1)} %get-tuple-element.29), channel_id=1, replica_groups=mesh['leaf'=8,'sub'=4] {'sub','leaf'}, dimensions={0} | all-to-all | bytes 196608 | tf_op jit(solution)/shard_map/all_to_all | solution.py:380
  37.5 0.6 %shard_map.117 = (f32[32,1,128]{2,1,0:T(1,128)S(1)}, f32[8,256]{1,0:T(8,128)S(1)}, f32[8,256]{1,0:T(8,128)S(1)}, f32[8,128]{1,0:T(8,128)S(1)}) custom-call(f32[8,256]{1,0:T(8,128)S(1)} %get-tuple-element.23.refs_0_, f32[8,256]{1,0:T(8,128)S(1)} %get-tuple-element.24.refs_1_, f32[8,256]{1,0:T(8,128)S(1)} %get-tuple-element.26.refs_2_.refs_1_, ...), custom_call_target="tpu_custom_call" | custom-call | tf_op jit(solution)/shard_map/pallas_call | solution.py:407
  38.1 8.9 %all_to_all.22.refs_5_ = f32[32,1,128]{2,1,0:T(1,128)S(1)} all-to-all(f32[32,1,128]{2,1,0:T(1,128)S(1)} %get-tuple-element.33), channel_id=1, replica_groups=mesh['leaf'=8,'sub'=4] {'sub','leaf'}, dimensions={0} | all-to-all | bytes 32768 | tf_op jit(solution)/shard_map/all_to_all | solution.py:380
  47.0 0.8 %shard_map.118 = (f32[4,4,256]{2,1,0:T(4,128)}, f32[4,3]{1,0:T(4,128)}) custom-call(f32[8,256]{1,0:T(8,128)S(1)} %get-tuple-element.23.refs_0_, f32[8,256]{1,0:T(8,128)S(1)} %get-tuple-element.26.refs_2_.refs_1_, f32[8,256]{1,0:T(8,128)S(1)} %get-tuple-element.30.refs_2_, f32[8,256]{1,0:T(8,128)S(1)} %get-tuple-element.31.refs_3_, ...), custom_call_target="tpu_custom_call" | custom-call | tf_op jit(solution)/shard_map/pallas_call | solution.py:412
Async XLA Ops:
  2.5 7.4 %copy-start.5 = (bf16[1,64,256]{2,1,0:T(8,128)(2,1)S(1)}, bf16[1,64,256]{2,1,0:T(8,128)(2,1)}, u32[]{:S(2)}) copy-start(bf16[1,64,256]{2,1,0:T(8,128)(2,1)} %refs_5_.1) | copy-start | bytes 98308
  2.6 14.9 %copy-start.2 = (bf16[4,64,256]{2,1,0:T(8,128)(2,1)S(1)}, bf16[4,64,256]{2,1,0:T(8,128)(2,1)}, u32[]{:S(2)}) copy-start(bf16[4,64,256]{2,1,0:T(8,128)(2,1)} %refs_10_.1) | copy-start | bytes 393220
  2.6 14.9 %all-to-all-start = ((bf16[32,3,4,128]{3,2,1,0:T(4,128)(2,1)}), bf16[32,3,4,128]{3,2,1,0:T(4,128)(2,1)S(1)}, u32[]{:S(2)}, u32[]{:S(2)}) async-start(bf16[32,3,4,128]{3,2,1,0:T(4,128)(2,1)} %get-tuple-element.20), calls=%async_computation | async-start | bytes 196608 | tf_op jit(solution)/shard_map/all_to_all | solution.py:380
  9.9 0.7 %copy-start.4 = (f32[4,256]{1,0:T(4,128)S(1)}, f32[4,256]{1,0:T(4,128)}, u32[]{:S(2)}) copy-start(f32[4,256]{1,0:T(4,128)} %refs_0_.1) | copy-start | bytes 12292
  9.9 0.7 %copy-start.8 = (s32[1,4]{1,0:T(1,128)S(1)}, s32[1,4]{1,0:T(1,128)}, u32[]{:S(2)}) copy-start(s32[1,4]{1,0:T(1,128)} %refs_2_.1) | copy-start | bytes 52
  9.9 0.7 %copy-start.6 = (s32[4,2]{0,1:T(2,128)S(1)}, s32[4,2]{0,1:T(2,128)}, u32[]{:S(2)}) copy-start(s32[4,2]{0,1:T(2,128)} %param.13) | copy-start | bytes 100
  9.9 0.7 %copy-start.7 = (s32[4,1]{0,1:T(1,128)S(1)}, s32[4,1]{0,1:T(1,128)}, u32[]{:S(2)}) copy-start(s32[4,1]{0,1:T(1,128)} %param.12) | copy-start | bytes 52
  10.6 1.2 %copy-start = (bf16[4,2,256,256]{3,2,1,0:T(8,128)(2,1)S(1)}, bf16[4,2,256,256]{3,2,1,0:T(8,128)(2,1)}, u32[]{:S(2)}) copy-start(bf16[4,2,256,256]{3,2,1,0:T(8,128)(2,1)} %refs_7_.7) | copy-start | bytes 3145732
  11.8 5.6 %copy-start.1 = (bf16[4,2,256,256]{3,2,1,0:T(8,128)(2,1)S(1)}, bf16[4,2,256,256]{3,2,1,0:T(8,128)(2,1)}, u32[]{:S(2)}) copy-start(bf16[4,2,256,256]{3,2,1,0:T(8,128)(2,1)} %refs_7_.7) | copy-start | bytes 3145732
  11.8 5.6 %copy-start.3 = (bf16[4,64,128]{2,1,0:T(8,128)(2,1)S(1)}, bf16[4,64,128]{2,1,0:T(8,128)(2,1)}, u32[]{:S(2)}) copy-start(bf16[4,64,128]{2,1,0:T(8,128)(2,1)} %refs_9_.1) | copy-start | bytes 196612

commit v6 on v5

--- a/solution.py
+++ b/solution.py
@@ -89,32 +89,56 @@
 
 
 def first_kernel(
+    subs,
     start_hbm,
     basis_hbm,
     node_hbm,
     upper_hbm,
+    top_hbm,
+    near_ids_hbm,
+    far_ids_hbm,
+    top_ids_hbm,
     block_ref,
     reach2_ref,
+    start2_ref,
+    pick_ref,
+    top_down_ref,
     start_ref,
     basis_ref,
     node_ref,
     upper_ref,
+    top_ref,
+    near_ids_ref,
+    far_ids_ref,
+    top_ids_ref,
     sems,
 ):
-    sources = (basis_hbm, node_hbm, upper_hbm, start_hbm)
-    targets = (basis_ref, node_ref, upper_ref, start_ref)
+    pairs = (
+        (basis_hbm, basis_ref),
+        (near_ids_hbm, near_ids_ref),
+        (far_ids_hbm, far_ids_ref),
+        (top_ids_hbm, top_ids_ref),
+        (node_hbm, node_ref),
+        (upper_hbm, upper_ref),
+        (top_hbm, top_ref),
+        (start_hbm, start_ref),
+    )
     copies = [
         pltpu.make_async_copy(source, target, sems.at[i])
-        for i, (source, target) in enumerate(zip(sources, targets))
+        for i, (source, target) in enumerate(pairs)
     ]
     for copy in copies:
         copy.start()
     for copy in copies:
         copy.wait()
-    reach2 = twice(dot_nn(upper_ref[0], node_ref[0])).astype(BF16)
+    set_picks(subs, near_ids_ref[...], far_ids_ref[...], top_ids_ref[...], pick_ref)
+    reach = dot_nn(upper_ref[0], node_ref[0])
+    reach2 = twice(reach).astype(BF16)
     reach2_ref[...] = reach2
     start = twice(start_ref[...])
+    start2_ref[...] = start
     store_all(make_block(start, [inner(start, start)], basis_ref[...], reach2), block_ref)
+    top_down_ref[...] = dot_tn(reach.astype(BF16), top_ref[0]).astype(BF16)
 
 
 def own_part(vec, near_ref):
@@ -122,26 +146,9 @@
     return by_leaf([dot_nt(vec_bf, near_ref[l, 0]) for l in range(near_ref.shape[0])])
 
 
-def setup_kernel(
-    subs,
-    near_ids_ref,
-    far_ids_ref,
-    top_ids_ref,
-    branch_ref,
-    reach2_ref,
-    top_ref,
-    start_ref,
-    near_ref,
-    pick_ref,
-    top_down_ref,
-    own_ref,
-):
-    own_ref[...] = own_part(twice(start_ref[...]), near_ref)
-    near_ids, far_ids, top_ids = near_ids_ref[...], far_ids_ref[...], top_ids_ref[...]
-    branch = branch_ref[...]
+def set_picks(subs, near_ids, far_ids, top_ids, pick_ref):
+    branch = lax.axis_index("leaf").astype(jnp.int32)
     leaves = near_ids.shape[1]
-    rank = top_ref.shape[1]
-    top_down_ref[...] = dot_tn(reach2_ref[:rank, :], top_ref[0]).astype(BF16)
     width = pick_ref.shape[1]
     col = iota((ROWS, width), 1)
     lane4, row4 = iota((ROWS, leaves), 1), iota((ROWS, leaves), 0) % leaves
@@ -206,8 +213,7 @@
 
 def second_kernel(
     total,
-    start_ref,
-    own_ref,
+    start2_ref,
     got_ref,
     pick_ref,
     near_ref,
@@ -219,9 +225,9 @@
     b0_ref,
     k1_ref,
 ):
-    start = twice(start_ref[...])
+    start = start2_ref[...]
     image, dots = multiply(
-        lambda: own_ref[...], got_ref, pick_ref, near_ref, top_down_ref, coupling_ref, basis_ref
+        lambda: own_part(start, near_ref), got_ref, pick_ref, near_ref, top_down_ref, coupling_ref, basis_ref
     )
     scale = lax.rsqrt(dots[0] * (1.0 / total) + 1e-06)
     b0 = scale * start
@@ -344,13 +350,14 @@
     return jax.ShapeDtypeStruct(shape, dtype)
 
 
-def call(kernel, ins, outs, scratch=()):
+def call(kernel, ins, outs, scratch=(), cost=None):
     return pl.pallas_call(
         kernel,
         in_specs=ins,
         out_specs=[VMEM] * len(outs),
         out_shape=outs,
         scratch_shapes=scratch,
+        cost_estimate=cost,
         compiler_params=pltpu.CompilerParams(vmem_limit_bytes=16 * 1024 * 1024),
     )
 
@@ -379,28 +386,34 @@
     def exchange(out):
         return lax.all_to_all(out, ("sub", "leaf"), 0, 0, tiled=True)
 
-    sources = (start_vec, leaf_basis, node_transfer, branch_transfer)
-    out, reach2 = call(
-        first_kernel,
-        [HBM] * 4,
-        [blocks, shaped((2 * rank, leaves * rank), BF16)],
-        [pltpu.VMEM(a.shape, a.dtype) for a in sources] + [pltpu.SemaphoreType.DMA((4,))],
-    )(*[pltpu.with_memory_space_constraint(a, pltpu.HBM) for a in sources])
-    got = exchange(out)
-    branch = lax.axis_index("leaf").astype(jnp.int32).reshape(1, 1)
-    pick, top_down, own = call(
-        lambda *refs: setup_kernel(subs, *refs),
-        [VMEM] * 8,
+    sources = (
+        start_vec,
+        leaf_basis,
+        node_transfer,
+        branch_transfer,
+        top_coupling,
+        near_ids.T,
+        far_ids.T,
+        top_ids,
+    )
+    out, reach2, start2, pick, top_down = call(
+        lambda *refs: first_kernel(subs, *refs),
+        [HBM] * len(sources),
         [
+            blocks,
+            shaped((2 * rank, leaves * rank), BF16),
+            vec,
             shaped((8 * ROWS, devices * leaves), BF16),
             shaped((leaves * rank, top_coupling.shape[2]), BF16),
-            vec,
         ],
-    )(near_ids.T, far_ids.T, top_ids, branch, reach2, top_coupling, start_vec, near_blocks)
+        [pltpu.VMEM(a.shape, a.dtype) for a in sources]
+        + [pltpu.SemaphoreType.DMA((len(sources),))],
+        pl.CostEstimate(flops=10000000, bytes_accessed=20000000, transcendentals=0),
+    )(*[pltpu.with_memory_space_constraint(a, pltpu.HBM) for a in sources])
     fixed = (pick, near_blocks, top_down, leaf_coupling, leaf_basis)
     out, b0, k1 = call(
-        lambda *refs: second_kernel(total, *refs), [VMEM] * 9, [blocks, vec, vec]
-    )(start_vec, own, got, *fixed, reach2)
+        lambda *refs: second_kernel(total, *refs), [VMEM] * 8, [blocks, vec, vec]
+    )(start2, exchange(out), *fixed, reach2)
     out, b1, k2, heads = call(
         lambda *refs: third_kernel(total, *refs), [VMEM] * 9, [blocks, vec, vec, table]
     )(b0, k1, exchange(out), *fixed, reach2)

time: 48.1 us -> 48.6 us (1.010)
  blocking collectives: 27.5 us -> 42.1 us
  starting transfers between devices: 7.3 us -> 0 us
  waiting for transfers between devices: 5.3 us -> 0 us
  Pallas kernels: 5.1 us -> 4.27 us
  local copies, waits for them, and re-layouts: 1.92 us -> 1.24 us
    all_to_all x3 -> x4, blocking collectives: 27.5 us -> 42.1 us  [exchange(): return lax.all_to_all(out, ('sub', 'leaf'), 0, 0, tiled=True)]
    all_to_all x1 -> x0, starting transfers between devices: 7.3 us -> none  [exchange(): return lax.all_to_all(out, ('sub', 'leaf'), 0, 0, tiled=True)]
    all_to_all x1 -> x0, waiting for transfers between devices: 5.3 us -> none  [exchange(): return lax.all_to_all(out, ('sub', 'leaf'), 0, 0, tiled=True)]
    pallas_call x3 -> x2, Pallas kernels: 2.93 us -> 2.1 us  [the longest x1 1.36 us: per_device(): call(lambda *refs: first_kernel(subs, *refs), [HBM] * len(sources), [bloc...]
    unnamed x18 -> x8, local copies, waits for them, and re-layouts: 1.92 us -> 1.24 us
  transfers between devices with their start and end apart: 1 -> 0, of which waited for: 1 -> 0; matrix products, arithmetic and copies ran while one was open for 0% -> 0% of each run, Pallas kernels for 1% -> 0%
where the time goes in v6:
time: 48.6 us; the launch traced here: 48.3 us
  blocking collectives  42.1 us (87%)
  Pallas kernels  4.27 us (9%)
  local copies, waits for them, and re-layouts  1.24 us (3%)
  between operations  0.68 us (1%)
    all_to_all x4, blocking collectives, exchange(): return lax.all_to_all(out, ('sub', 'leaf'), 0, 0, tiled=True)  42.1 us
    pallas_call x1, Pallas kernels, per_device(): call(lambda *refs: first_kernel(subs, *refs), [HBM] * len(sources), [bloc...  1.36 us
    unnamed x8, local copies, waits for them, and re-layouts  1.24 us

profile of v6, /device:TPU:0, one launch (start us, length us, event | category | flops | bytes accessed | tf_op | source)
XLA Modules:
  0.0 48.3 jit_solution(13877404275876525223)
XLA Ops:
  0.6 1.4 %shard_map.113 = (bf16[32,3,4,128]{3,2,1,0:T(4,128)(2,1)S(1)}, bf16[128,256]{1,0:T(8,128)(2,1)S(1)}, f32[8,256]{1,0:T(8,128)S(1)}, bf16[64,128]{1,0:T(8,128)(2,1)S(1)}, bf16[256,256]{1,0:T(8,128)(2,1)S(1)}) custom-call(f32[4,256]{1,0:T(4,128)} %refs_0_.1, bf16[4,64,256]{2,1,0:T(8,128)(2,1)} %refs_10_.1, bf16[1,64,256]{2,1,0:T(8,128)(2,1)} %refs_2_.1, ...), custom_call_target="tpu_custom_call" | custom-call | flops 10000000 | bytes 20000000 | tf_op jit(solution)/shard_map/pallas_call | solution.py:399
  2.0 0.0 copy-start.2
  2.0 0.0 copy-start.3
  2.0 14.7 %all_to_all.20.refs_1_ = bf16[32,3,4,128]{3,2,1,0:T(4,128)(2,1)S(1)} all-to-all(bf16[32,3,4,128]{3,2,1,0:T(4,128)(2,1)S(1)} %get-tuple-element.19), channel_id=1, replica_groups=mesh['leaf'=8,'sub'=4] {'sub','leaf'}, dimensions={0} | all-to-all | bytes 196608 | tf_op jit(solution)/shard_map/all_to_all | solution.py:387
  16.7 0.0 copy-done.2
  16.7 0.0 copy-done.3
  16.7 0.0 copy-start
  16.7 1.2 %copy-done = bf16[4,2,256,256]{3,2,1,0:T(8,128)(2,1)S(1)} copy-done((bf16[4,2,256,256]{3,2,1,0:T(8,128)(2,1)S(1)}, bf16[4,2,256,256]{3,2,1,0:T(8,128)(2,1)}, u32[]{:S(2)}) %copy-start) | copy-done | bytes 1048600
  17.9 0.0 copy-start.1
  17.9 0.7 %shard_map.114 = (bf16[32,3,4,128]{3,2,1,0:T(4,128)(2,1)S(1)}, f32[8,256]{1,0:T(8,128)S(1)}, f32[8,256]{1,0:T(8,128)S(1)}) custom-call(f32[8,256]{1,0:T(8,128)S(1)} %get-tuple-element.18.refs_0_, bf16[32,3,4,128]{3,2,1,0:T(4,128)(2,1)S(1)} %all_to_all.20.refs_1_, bf16[64,128]{1,0:T(8,128)(2,1)S(1)} %get-tuple-element.20.refs_2_.refs_3_.refs_6_, ...), custom_call_target="tpu_custom_call" | custom-call | tf_op jit(solution)/shard_map/pallas_call | solution.py:414
  18.7 9.3 %all_to_all.21.refs_2_ = bf16[32,3,4,128]{3,2,1,0:T(4,128)(2,1)S(1)} all-to-all(bf16[32,3,4,128]{3,2,1,0:T(4,128)(2,1)S(1)} %get-tuple-element.25), channel_id=1, replica_groups=mesh['leaf'=8,'sub'=4] {'sub','leaf'}, dimensions={0} | all-to-all | bytes 196608 | tf_op jit(solution)/shard_map/all_to_all | solution.py:387
  28.0 0.0 copy-done.1
  28.0 0.7 %shard_map.115 = (bf16[32,3,4,128]{3,2,1,0:T(4,128)(2,1)S(1)}, f32[8,256]{1,0:T(8,128)S(1)}, f32[8,256]{1,0:T(8,128)S(1)}, f32[8,128]{1,0:T(8,128)S(1)}) custom-call(f32[8,256]{1,0:T(8,128)S(1)} %get-tuple-element.23.refs_0_, f32[8,256]{1,0:T(8,128)S(1)} %get-tuple-element.24.refs_1_, bf16[32,3,4,128]{3,2,1,0:T(4,128)(2,1)S(1)} %all_to_all.21.refs_2_, ...), custom_call_target="tpu_custom_call" | custom-call | tf_op jit(solution)/shard_map/pallas_call | solution.py:417
  28.7 9.3 %all_to_all.22.refs_5_ = bf16[32,3,4,128]{3,2,1,0:T(4,128)(2,1)S(1)} all-to-all(bf16[32,3,4,128]{3,2,1,0:T(4,128)(2,1)S(1)} %get-tuple-element.29), channel_id=1, replica_groups=mesh['leaf'=8,'sub'=4] {'sub','leaf'}, dimensions={0} | all-to-all | bytes 196608 | tf_op jit(solution)/shard_map/all_to_all | solution.py:387
  38.0 0.6 %shard_map.116 = (f32[32,1,128]{2,1,0:T(1,128)S(1)}, f32[8,256]{1,0:T(8,128)S(1)}, f32[8,256]{1,0:T(8,128)S(1)}, f32[8,128]{1,0:T(8,128)S(1)}) custom-call(f32[8,256]{1,0:T(8,128)S(1)} %get-tuple-element.23.refs_0_, f32[8,256]{1,0:T(8,128)S(1)} %get-tuple-element.24.refs_1_, f32[8,256]{1,0:T(8,128)S(1)} %get-tuple-element.26.refs_2_.refs_1_, ...), custom_call_target="tpu_custom_call" | custom-call | tf_op jit(solution)/shard_map/pallas_call | solution.py:420
  38.6 8.9 %all_to_all.23.refs_5_ = f32[32,1,128]{2,1,0:T(1,128)S(1)} all-to-all(f32[32,1,128]{2,1,0:T(1,128)S(1)} %get-tuple-element.33), channel_id=1, replica_groups=mesh['leaf'=8,'sub'=4] {'sub','leaf'}, dimensions={0} | all-to-all | bytes 32768 | tf_op jit(solution)/shard_map/all_to_all | solution.py:387
  47.5 0.8 %shard_map.117 = (f32[4,4,256]{2,1,0:T(4,128)}, f32[4,3]{1,0:T(4,128)}) custom-call(f32[8,256]{1,0:T(8,128)S(1)} %get-tuple-element.23.refs_0_, f32[8,256]{1,0:T(8,128)S(1)} %get-tuple-element.26.refs_2_.refs_1_, f32[8,256]{1,0:T(8,128)S(1)} %get-tuple-element.30.refs_2_, f32[8,256]{1,0:T(8,128)S(1)} %get-tuple-element.31.refs_3_, ...), custom_call_target="tpu_custom_call" | custom-call | tf_op jit(solution)/shard_map/pallas_call | solution.py:425
Async XLA Ops:
  2.0 14.7 %copy-start.2 = (bf16[4,64,256]{2,1,0:T(8,128)(2,1)S(1)}, bf16[4,64,256]{2,1,0:T(8,128)(2,1)}, u32[]{:S(2)}) copy-start(bf16[4,64,256]{2,1,0:T(8,128)(2,1)} %refs_10_.1) | copy-start | bytes 393220
  2.0 14.7 %copy-start.3 = (bf16[4,64,128]{2,1,0:T(8,128)(2,1)S(1)}, bf16[4,64,128]{2,1,0:T(8,128)(2,1)}, u32[]{:S(2)}) copy-start(bf16[4,64,128]{2,1,0:T(8,128)(2,1)} %refs_9_.1) | copy-start | bytes 196612
  16.7 1.2 %copy-start = (bf16[4,2,256,256]{3,2,1,0:T(8,128)(2,1)S(1)}, bf16[4,2,256,256]{3,2,1,0:T(8,128)(2,1)}, u32[]{:S(2)}) copy-start(bf16[4,2,256,256]{3,2,1,0:T(8,128)(2,1)} %refs_7_.5) | copy-start | bytes 3145732
  17.9 10.1 %copy-start.1 = (bf16[4,2,256,256]{3,2,1,0:T(8,128)(2,1)S(1)}, bf16[4,2,256,256]{3,2,1,0:T(8,128)(2,1)}, u32[]{:S(2)}) copy-start(bf16[4,2,256,256]{3,2,1,0:T(8,128)(2,1)} %refs_7_.5) | copy-start | bytes 3145732

commit v7 on v6

--- a/solution.py
+++ b/solution.py
@@ -408,7 +408,7 @@
         ],
         [pltpu.VMEM(a.shape, a.dtype) for a in sources]
         + [pltpu.SemaphoreType.DMA((len(sources),))],
-        pl.CostEstimate(flops=10000000, bytes_accessed=20000000, transcendentals=0),
+        pl.CostEstimate(flops=2000000000, bytes_accessed=20000000, transcendentals=0),
     )(*[pltpu.with_memory_space_constraint(a, pltpu.HBM) for a in sources])
     fixed = (pick, near_blocks, top_down, leaf_coupling, leaf_basis)
     out, b0, k1 = call(

time: 48.6 us -> 47.4 us (0.975)
  local copies, waits for them, and re-layouts: 1.24 us -> 0.02 us
    unnamed x8 -> x6, local copies, waits for them, and re-layouts: 1.24 us -> 0.02 us
where the time goes in v7:
time: 47.4 us; the launch traced here: 47.2 us
  blocking collectives  42.1 us (89%)
  Pallas kernels  4.36 us (9%)
  between operations  0.69 us (1%)
    all_to_all x4, blocking collectives, exchange(): return lax.all_to_all(out, ('sub', 'leaf'), 0, 0, tiled=True)  42.1 us
    pallas_call x1, Pallas kernels, per_device(): call(lambda *refs: first_kernel(subs, *refs), [HBM] * len(sources), [bloc...  1.44 us

profile of v7, /device:TPU:0, one launch (start us, length us, event | category | flops | bytes accessed | tf_op | source)
XLA Modules:
  0.0 47.2 jit_solution(7497082338071432261)
XLA Ops:
  0.6 0.0 copy-start
  0.6 1.4 %shard_map.113 = (bf16[32,3,4,128]{3,2,1,0:T(4,128)(2,1)S(1)}, bf16[128,256]{1,0:T(8,128)(2,1)S(1)}, f32[8,256]{1,0:T(8,128)S(1)}, bf16[64,128]{1,0:T(8,128)(2,1)S(1)}, bf16[256,256]{1,0:T(8,128)(2,1)S(1)}) custom-call(f32[4,256]{1,0:T(4,128)} %refs_0_.1, bf16[4,64,256]{2,1,0:T(8,128)(2,1)} %refs_10_.1, bf16[1,64,256]{2,1,0:T(8,128)(2,1)} %refs_2_.1, ...), custom_call_target="tpu_custom_call" | custom-call | flops 2000000000 | bytes 20000000 | tf_op jit(solution)/shard_map/pallas_call | solution.py:399
  2.1 0.0 copy-start.1
  2.1 0.0 copy-start.2
  2.1 14.7 %all_to_all.20.refs_1_ = bf16[32,3,4,128]{3,2,1,0:T(4,128)(2,1)S(1)} all-to-all(bf16[32,3,4,128]{3,2,1,0:T(4,128)(2,1)S(1)} %get-tuple-element.19), channel_id=1, replica_groups=mesh['leaf'=8,'sub'=4] {'sub','leaf'}, dimensions={0} | all-to-all | bytes 196608 | tf_op jit(solution)/shard_map/all_to_all | solution.py:387
  16.8 0.0 copy-done
  16.8 0.0 copy-done.1
  16.8 0.0 copy-done.2
  16.8 0.8 %shard_map.114 = (bf16[32,3,4,128]{3,2,1,0:T(4,128)(2,1)S(1)}, f32[8,256]{1,0:T(8,128)S(1)}, f32[8,256]{1,0:T(8,128)S(1)}) custom-call(f32[8,256]{1,0:T(8,128)S(1)} %get-tuple-element.18.refs_0_, bf16[32,3,4,128]{3,2,1,0:T(4,128)(2,1)S(1)} %all_to_all.20.refs_1_, bf16[64,128]{1,0:T(8,128)(2,1)S(1)} %get-tuple-element.20.refs_2_.refs_3_.refs_6_, ...), custom_call_target="tpu_custom_call" | custom-call | tf_op jit(solution)/shard_map/pallas_call | solution.py:414
  17.5 9.3 %all_to_all.21.refs_2_ = bf16[32,3,4,128]{3,2,1,0:T(4,128)(2,1)S(1)} all-to-all(bf16[32,3,4,128]{3,2,1,0:T(4,128)(2,1)S(1)} %get-tuple-element.25), channel_id=1, replica_groups=mesh['leaf'=8,'sub'=4] {'sub','leaf'}, dimensions={0} | all-to-all | bytes 196608 | tf_op jit(solution)/shard_map/all_to_all | solution.py:387
  26.8 0.7 %shard_map.115 = (bf16[32,3,4,128]{3,2,1,0:T(4,128)(2,1)S(1)}, f32[8,256]{1,0:T(8,128)S(1)}, f32[8,256]{1,0:T(8,128)S(1)}, f32[8,128]{1,0:T(8,128)S(1)}) custom-call(f32[8,256]{1,0:T(8,128)S(1)} %get-tuple-element.23.refs_0_, f32[8,256]{1,0:T(8,128)S(1)} %get-tuple-element.24.refs_1_, bf16[32,3,4,128]{3,2,1,0:T(4,128)(2,1)S(1)} %all_to_all.21.refs_2_, ...), custom_call_target="tpu_custom_call" | custom-call | tf_op jit(solution)/shard_map/pallas_call | solution.py:417
  27.6 9.3 %all_to_all.22.refs_5_ = bf16[32,3,4,128]{3,2,1,0:T(4,128)(2,1)S(1)} all-to-all(bf16[32,3,4,128]{3,2,1,0:T(4,128)(2,1)S(1)} %get-tuple-element.29), channel_id=1, replica_groups=mesh['leaf'=8,'sub'=4] {'sub','leaf'}, dimensions={0} | all-to-all | bytes 196608 | tf_op jit(solution)/shard_map/all_to_all | solution.py:387
  36.9 0.6 %shard_map.116 = (f32[32,1,128]{2,1,0:T(1,128)S(1)}, f32[8,256]{1,0:T(8,128)S(1)}, f32[8,256]{1,0:T(8,128)S(1)}, f32[8,128]{1,0:T(8,128)S(1)}) custom-call(f32[8,256]{1,0:T(8,128)S(1)} %get-tuple-element.23.refs_0_, f32[8,256]{1,0:T(8,128)S(1)} %get-tuple-element.24.refs_1_, f32[8,256]{1,0:T(8,128)S(1)} %get-tuple-element.26.refs_2_.refs_1_, ...), custom_call_target="tpu_custom_call" | custom-call | tf_op jit(solution)/shard_map/pallas_call | solution.py:420
  37.5 8.9 %all_to_all.23.refs_5_ = f32[32,1,128]{2,1,0:T(1,128)S(1)} all-to-all(f32[32,1,128]{2,1,0:T(1,128)S(1)} %get-tuple-element.33), channel_id=1, replica_groups=mesh['leaf'=8,'sub'=4] {'sub','leaf'}, dimensions={0} | all-to-all | bytes 32768 | tf_op jit(solution)/shard_map/all_to_all | solution.py:387
  46.4 0.8 %shard_map.117 = (f32[4,4,256]{2,1,0:T(4,128)}, f32[4,3]{1,0:T(4,128)}) custom-call(f32[8,256]{1,0:T(8,128)S(1)} %get-tuple-element.23.refs_0_, f32[8,256]{1,0:T(8,128)S(1)} %get-tuple-element.26.refs_2_.refs_1_, f32[8,256]{1,0:T(8,128)S(1)} %get-tuple-element.30.refs_2_, f32[8,256]{1,0:T(8,128)S(1)} %get-tuple-element.31.refs_3_, ...), custom_call_target="tpu_custom_call" | custom-call | tf_op jit(solution)/shard_map/pallas_call | solution.py:425
Async XLA Ops:
  0.6 16.1 %copy-start = (bf16[4,2,256,256]{3,2,1,0:T(8,128)(2,1)S(1)}, bf16[4,2,256,256]{3,2,1,0:T(8,128)(2,1)}, u32[]{:S(2)}) copy-start(bf16[4,2,256,256]{3,2,1,0:T(8,128)(2,1)} %refs_7_.5) | copy-start | bytes 3145732
  2.1 14.7 %copy-start.1 = (bf16[4,64,256]{2,1,0:T(8,128)(2,1)S(1)}, bf16[4,64,256]{2,1,0:T(8,128)(2,1)}, u32[]{:S(2)}) copy-start(bf16[4,64,256]{2,1,0:T(8,128)(2,1)} %refs_10_.1) | copy-start | bytes 393220
  2.1 14.7 %copy-start.2 = (bf16[4,64,128]{2,1,0:T(8,128)(2,1)S(1)}, bf16[4,64,128]{2,1,0:T(8,128)(2,1)}, u32[]{:S(2)}) copy-start(bf16[4,64,128]{2,1,0:T(8,128)(2,1)} %refs_9_.1) | copy-start | bytes 196612

commit v8 on v7

--- a/solution.py
+++ b/solution.py
@@ -9,7 +9,6 @@
 BF16 = jnp.bfloat16
 ROWS = 8
 VMEM = pl.BlockSpec(memory_space=pltpu.VMEM)
-HBM = pl.BlockSpec(memory_space=pltpu.HBM)
 
 
 def dot_nt(a, b):
@@ -88,21 +87,12 @@
         pl.loop(0, devices)(store)
 
 
+def early_kernel(table_ref):
+    table_ref[...] = jnp.zeros(table_ref.shape, F32)
+
+
 def first_kernel(
     subs,
-    start_hbm,
-    basis_hbm,
-    node_hbm,
-    upper_hbm,
-    top_hbm,
-    near_ids_hbm,
-    far_ids_hbm,
-    top_ids_hbm,
-    block_ref,
-    reach2_ref,
-    start2_ref,
-    pick_ref,
-    top_down_ref,
     start_ref,
     basis_ref,
     node_ref,
@@ -111,26 +101,13 @@
     near_ids_ref,
     far_ids_ref,
     top_ids_ref,
-    sems,
-):
-    pairs = (
-        (basis_hbm, basis_ref),
-        (near_ids_hbm, near_ids_ref),
-        (far_ids_hbm, far_ids_ref),
-        (top_ids_hbm, top_ids_ref),
-        (node_hbm, node_ref),
-        (upper_hbm, upper_ref),
-        (top_hbm, top_ref),
-        (start_hbm, start_ref),
-    )
-    copies = [
-        pltpu.make_async_copy(source, target, sems.at[i])
-        for i, (source, target) in enumerate(pairs)
-    ]
-    for copy in copies:
-        copy.start()
-    for copy in copies:
-        copy.wait()
+    table_ref,
+    block_ref,
+    reach2_ref,
+    start2_ref,
+    pick_ref,
+    top_down_ref,
+):
     set_picks(subs, near_ids_ref[...], far_ids_ref[...], top_ids_ref[...], pick_ref)
     reach = dot_nn(upper_ref[0], node_ref[0])
     reach2 = twice(reach).astype(BF16)
@@ -243,6 +220,7 @@
     total,
     b0_ref,
     k1_ref,
+    table_in_ref,
     got_ref,
     pick_ref,
     near_ref,
@@ -274,8 +252,7 @@
     w1 = 0.5 * b1 + k2
     b1_ref[...] = b1
     k2_ref[...] = k2
-    table = jnp.zeros((ROWS, 128), F32)
-    table = entry(table, 0, 0, h00)
+    table = entry(table_in_ref[...], 0, 0, h00)
     table_ref[...] = entry(table, 1, 0, h10)
     dots = [inner(b0, w1), inner(b1, w1), inner(w1, w1)]
     store_all(make_block(k2, dots, basis_ref[...], reach2_ref[...]), block_ref)
@@ -330,7 +307,7 @@
     total, b0_ref, b1_ref, b2_ref, w2_ref, table_ref, dots_ref, out_ref, hessen_ref
 ):
     leaves = out_ref.shape[1]
-    sums = jnp.sum(dots_ref[...], axis=0) * (1.0 / total)
+    sums = jnp.sum(dots_ref[:, 0, :], axis=0, keepdims=True) * (1.0 / total)
     dots = [sums[:, 32 * i : 32 * i + 1] for i in range(4)]
     b0, b1, b2 = b0_ref[:leaves, :], b1_ref[:leaves, :], b2_ref[:leaves, :]
     scale, inv = norm_of(dots[3], dots[:3])
@@ -350,13 +327,12 @@
     return jax.ShapeDtypeStruct(shape, dtype)
 
 
-def call(kernel, ins, outs, scratch=(), cost=None):
+def call(kernel, ins, outs, cost=None):
     return pl.pallas_call(
         kernel,
         in_specs=ins,
         out_specs=[VMEM] * len(outs),
         out_shape=outs,
-        scratch_shapes=scratch,
         cost_estimate=cost,
         compiler_params=pltpu.CompilerParams(vmem_limit_bytes=16 * 1024 * 1024),
     )
@@ -396,9 +372,15 @@
         far_ids.T,
         top_ids,
     )
+    (heads,) = call(
+        early_kernel,
+        [],
+        [table],
+        pl.CostEstimate(flops=5000000000, bytes_accessed=20000000, transcendentals=0),
+    )()
     out, reach2, start2, pick, top_down = call(
         lambda *refs: first_kernel(subs, *refs),
-        [HBM] * len(sources),
+        [VMEM] * (len(sources) + 1),
         [
             blocks,
             shaped((2 * rank, leaves * rank), BF16),
@@ -406,17 +388,15 @@
             shaped((8 * ROWS, devices * leaves), BF16),
             shaped((leaves * rank, top_coupling.shape[2]), BF16),
         ],
-        [pltpu.VMEM(a.shape, a.dtype) for a in sources]
-        + [pltpu.SemaphoreType.DMA((len(sources),))],
         pl.CostEstimate(flops=2000000000, bytes_accessed=20000000, transcendentals=0),
-    )(*[pltpu.with_memory_space_constraint(a, pltpu.HBM) for a in sources])
+    )(*sources, heads)
     fixed = (pick, near_blocks, top_down, leaf_coupling, leaf_basis)
     out, b0, k1 = call(
         lambda *refs: second_kernel(total, *refs), [VMEM] * 8, [blocks, vec, vec]
     )(start2, exchange(out), *fixed, reach2)
     out, b1, k2, heads = call(
-        lambda *refs: third_kernel(total, *refs), [VMEM] * 9, [blocks, vec, vec, table]
-    )(b0, k1, exchange(out), *fixed, reach2)
+        lambda *refs: third_kernel(total, *refs), [VMEM] * 10, [blocks, vec, vec, table]
+    )(b0, k1, heads, exchange(out), *fixed, reach2)
     dots, b2, w2, heads = call(
         lambda *refs: fourth_kernel(total, *refs),
         [VMEM] * 11,

time: 47.4 us -> 47.3 us (level)
  Pallas kernels: 4.36 us -> 3.27 us
  local copies, waits for them, and re-layouts: 0.02 us -> 0.86 us
    pallas_call x2 -> x3, Pallas kernels: 2.19 us -> 1.11 us  [the longest x1 0.75 us: per_device(): call(lambda *refs: third_kernel(total, *refs), [VMEM] * 10, [blocks, vec,...]
    unnamed x6 -> x20, local copies, waits for them, and re-layouts: 0.02 us -> 0.86 us
where the time goes in v8:
time: 47.3 us; the launch traced here: 47 us
  blocking collectives  42.1 us (89%)
  Pallas kernels  3.27 us (7%)
  local copies, waits for them, and re-layouts  0.86 us (2%)
  between operations  0.78 us (2%)
    all_to_all x4, blocking collectives, exchange(): return lax.all_to_all(out, ('sub', 'leaf'), 0, 0, tiled=True)  42.1 us

profile of v8, /device:TPU:0, one launch (start us, length us, event | category | flops | bytes accessed | tf_op | source)
XLA Modules:
  0.0 47.0 jit_solution(4928132473633963948)
XLA Ops:
  0.6 0.0 copy-start.1
  0.6 0.0 copy-start.4
  0.7 0.0 copy-start.5
  0.7 0.0 copy-start.3
  0.7 0.0 copy-start.6
  0.7 0.0 copy-start.9
  0.7 0.0 copy-start.7
  0.7 0.0 copy-start.8
  0.7 0.8 %copy-done.1 = bf16[4,64,256]{2,1,0:T(8,128)(2,1)S(1)} copy-done((bf16[4,64,256]{2,1,0:T(8,128)(2,1)S(1)}, bf16[4,64,256]{2,1,0:T(8,128)(2,1)}, u32[]{:S(2)}) %copy-start.1) | copy-done | bytes 131096
  1.5 0.0 copy-done.4
  1.5 0.0 copy-done.5
  1.5 0.0 copy-done.3
  1.5 0.0 copy-done.6
  1.6 0.0 copy-done.9
  1.6 0.0 copy-done.7
  1.6 0.0 copy-done.8
  1.6 0.0 copy-start
  1.6 0.4 shard_map.114
  2.0 0.0 copy-start.2
  2.0 14.7 %all_to_all.20.refs_1_ = bf16[32,3,4,128]{3,2,1,0:T(4,128)(2,1)S(1)} all-to-all(bf16[32,3,4,128]{3,2,1,0:T(4,128)(2,1)S(1)} %get-tuple-element.19), channel_id=1, replica_groups=mesh['leaf'=8,'sub'=4] {'sub','leaf'}, dimensions={0} | all-to-all | bytes 196608 | tf_op jit(solution)/shard_map/all_to_all | solution.py:363
  16.6 0.0 copy-done
  16.6 0.0 copy-done.2
  16.6 0.7 %shard_map.115 = (bf16[32,3,4,128]{3,2,1,0:T(4,128)(2,1)S(1)}, f32[8,256]{1,0:T(8,128)S(1)}, f32[8,256]{1,0:T(8,128)S(1)}) custom-call(f32[8,256]{1,0:T(8,128)S(1)} %get-tuple-element.18.refs_0_, bf16[32,3,4,128]{3,2,1,0:T(4,128)(2,1)S(1)} %all_to_all.20.refs_1_, bf16[64,128]{1,0:T(8,128)(2,1)S(1)} %get-tuple-element.20.refs_2_.refs_4_.refs_6_, ...), custom_call_target="tpu_custom_call" | custom-call | tf_op jit(solution)/shard_map/pallas_call | solution.py:394
  17.4 9.3 %all_to_all.21.refs_3_ = bf16[32,3,4,128]{3,2,1,0:T(4,128)(2,1)S(1)} all-to-all(bf16[32,3,4,128]{3,2,1,0:T(4,128)(2,1)S(1)} %get-tuple-element.25), channel_id=1, replica_groups=mesh['leaf'=8,'sub'=4] {'sub','leaf'}, dimensions={0} | all-to-all | bytes 196608 | tf_op jit(solution)/shard_map/all_to_all | solution.py:363
  26.7 0.7 %shard_map.116 = (bf16[32,3,4,128]{3,2,1,0:T(4,128)(2,1)S(1)}, f32[8,256]{1,0:T(8,128)S(1)}, f32[8,256]{1,0:T(8,128)S(1)}, f32[8,128]{1,0:T(8,128)S(1)}) custom-call(f32[8,256]{1,0:T(8,128)S(1)} %get-tuple-element.23.refs_0_, f32[8,256]{1,0:T(8,128)S(1)} %get-tuple-element.24.refs_1_, f32[8,128]{1,0:T(8,128)S(1)} %shard_map.113.refs_8_.refs_2_, ...), custom_call_target="tpu_custom_call" | custom-call | tf_op jit(solution)/shard_map/pallas_call | solution.py:397
  27.5 9.3 %all_to_all.22.refs_5_ = bf16[32,3,4,128]{3,2,1,0:T(4,128)(2,1)S(1)} all-to-all(bf16[32,3,4,128]{3,2,1,0:T(4,128)(2,1)S(1)} %get-tuple-element.29), channel_id=1, replica_groups=mesh['leaf'=8,'sub'=4] {'sub','leaf'}, dimensions={0} | all-to-all | bytes 196608 | tf_op jit(solution)/shard_map/all_to_all | solution.py:363
  36.8 0.6 %shard_map.117 = (f32[32,1,128]{2,1,0:T(1,128)S(1)}, f32[8,256]{1,0:T(8,128)S(1)}, f32[8,256]{1,0:T(8,128)S(1)}, f32[8,128]{1,0:T(8,128)S(1)}) custom-call(f32[8,256]{1,0:T(8,128)S(1)} %get-tuple-element.23.refs_0_, f32[8,256]{1,0:T(8,128)S(1)} %get-tuple-element.24.refs_1_, f32[8,256]{1,0:T(8,128)S(1)} %get-tuple-element.26.refs_2_.refs_1_, ...), custom_call_target="tpu_custom_call" | custom-call | tf_op jit(solution)/shard_map/pallas_call | solution.py:400
  37.4 8.9 %all_to_all.23.refs_5_ = f32[32,1,128]{2,1,0:T(1,128)S(1)} all-to-all(f32[32,1,128]{2,1,0:T(1,128)S(1)} %get-tuple-element.33), channel_id=1, replica_groups=mesh['leaf'=8,'sub'=4] {'sub','leaf'}, dimensions={0} | all-to-all | bytes 32768 | tf_op jit(solution)/shard_map/all_to_all | solution.py:363
  46.2 0.8 %shard_map.118 = (f32[4,4,256]{2,1,0:T(4,128)}, f32[4,3]{1,0:T(4,128)}) custom-call(f32[8,256]{1,0:T(8,128)S(1)} %get-tuple-element.23.refs_0_, f32[8,256]{1,0:T(8,128)S(1)} %get-tuple-element.26.refs_2_.refs_1_, f32[8,256]{1,0:T(8,128)S(1)} %get-tuple-element.30.refs_2_, f32[8,256]{1,0:T(8,128)S(1)} %get-tuple-element.31.refs_3_, ...), custom_call_target="tpu_custom_call" | custom-call | tf_op jit(solution)/shard_map/pallas_call | solution.py:405
  (1 shorter events, 0.0 us)
Async XLA Ops:
  0.6 0.9 %copy-start.1 = (bf16[4,64,256]{2,1,0:T(8,128)(2,1)S(1)}, bf16[4,64,256]{2,1,0:T(8,128)(2,1)}, u32[]{:S(2)}) copy-start(bf16[4,64,256]{2,1,0:T(8,128)(2,1)} %refs_10_.1) | copy-start | bytes 393220
  0.6 0.9 %copy-start.4 = (bf16[1,64,256]{2,1,0:T(8,128)(2,1)S(1)}, bf16[1,64,256]{2,1,0:T(8,128)(2,1)}, u32[]{:S(2)}) copy-start(bf16[1,64,256]{2,1,0:T(8,128)(2,1)} %refs_4_.1) | copy-start | bytes 98308
  0.7 0.9 %copy-start.5 = (bf16[1,64,64]{2,1,0:T(8,128)(2,1)S(1)}, bf16[1,64,64]{2,1,0:T(8,128)(2,1)}, u32[]{:S(2)}) copy-start(bf16[1,64,64]{2,1,0:T(8,128)(2,1)} %refs_3_.2) | copy-start | bytes 24580
  0.7 0.9 %copy-start.3 = (bf16[1,64,256]{2,1,0:T(8,128)(2,1)S(1)}, bf16[1,64,256]{2,1,0:T(8,128)(2,1)}, u32[]{:S(2)}) copy-start(bf16[1,64,256]{2,1,0:T(8,128)(2,1)} %refs_2_.1) | copy-start | bytes 98308
  0.7 0.9 %copy-start.6 = (f32[4,256]{1,0:T(4,128)S(1)}, f32[4,256]{1,0:T(4,128)}, u32[]{:S(2)}) copy-start(f32[4,256]{1,0:T(4,128)} %refs_0_.1) | copy-start | bytes 12292
  0.7 0.9 %copy-start.9 = (s32[1,4]{1,0:T(1,128)S(1)}, s32[1,4]{1,0:T(1,128)}, u32[]{:S(2)}) copy-start(s32[1,4]{1,0:T(1,128)} %refs_7_.3) | copy-start | bytes 52
  0.7 0.9 %copy-start.7 = (s32[4,2]{0,1:T(2,128)S(1)}, s32[4,2]{0,1:T(2,128)}, u32[]{:S(2)}) copy-start(s32[4,2]{0,1:T(2,128)} %param.13) | copy-start | bytes 100
  0.7 0.9 %copy-start.8 = (s32[4,1]{0,1:T(1,128)S(1)}, s32[4,1]{0,1:T(1,128)}, u32[]{:S(2)}) copy-start(s32[4,1]{0,1:T(1,128)} %param.12) | copy-start | bytes 52
  1.6 15.1 %copy-start = (bf16[4,2,256,256]{3,2,1,0:T(8,128)(2,1)S(1)}, bf16[4,2,256,256]{3,2,1,0:T(8,128)(2,1)}, u32[]{:S(2)}) copy-start(bf16[4,2,256,256]{3,2,1,0:T(8,128)(2,1)} %refs_7_.5) | copy-start | bytes 3145732
  2.0 14.7 %copy-start.2 = (bf16[4,64,128]{2,1,0:T(8,128)(2,1)S(1)}, bf16[4,64,128]{2,1,0:T(8,128)(2,1)}, u32[]{:S(2)}) copy-start(bf16[4,64,128]{2,1,0:T(8,128)(2,1)} %refs_9_.1) | copy-start | bytes 196612

commit v9 on v8

--- a/solution.py
+++ b/solution.py
@@ -107,8 +107,20 @@
     start2_ref,
     pick_ref,
     top_down_ref,
-):
-    set_picks(subs, near_ids_ref[...], far_ids_ref[...], top_ids_ref[...], pick_ref)
+    near_pick_ref,
+    far_pick_ref,
+    top_pick_ref,
+):
+    set_picks(
+        subs,
+        near_ids_ref[...],
+        far_ids_ref[...],
+        top_ids_ref[...],
+        pick_ref,
+        near_pick_ref,
+        far_pick_ref,
+        top_pick_ref,
+    )
     reach = dot_nn(upper_ref[0], node_ref[0])
     reach2 = twice(reach).astype(BF16)
     reach2_ref[...] = reach2
@@ -123,7 +135,9 @@
     return by_leaf([dot_nt(vec_bf, near_ref[l, 0]) for l in range(near_ref.shape[0])])
 
 
-def set_picks(subs, near_ids, far_ids, top_ids, pick_ref):
+def set_picks(
+    subs, near_ids, far_ids, top_ids, pick_ref, near_pick_ref, far_pick_ref, top_pick_ref
+):
     branch = lax.axis_index("leaf").astype(jnp.int32)
     leaves = near_ids.shape[1]
     width = pick_ref.shape[1]
@@ -134,7 +148,7 @@
         kept = jnp.where(lane4 == row4, ids, 0).astype(F32)
         return jnp.sum(kept, axis=1, keepdims=True).astype(jnp.int32)
 
-    branches = width // (subs * leaves)
+    branches = top_pick_ref.shape[1]
 
     def column(at, index):
         return ((index // leaves) * branches + at) * leaves + index % leaves
@@ -149,17 +163,87 @@
         at = (col // leaves) % branches
         groups.append((col % leaves == 0) & (at == top_ids[0:1, s : s + 1]))
     groups.append(col % leaves > 0)
-    pick_ref[...] = jnp.concatenate([g.astype(F32) for g in groups], axis=0).astype(BF16)
-
-
-def multiply(own, got_ref, pick_ref, near_ref, top_down_ref, coupling_ref, basis_ref):
+    if pick_ref.shape[0] > ROWS:
+        pick_ref[...] = jnp.concatenate([g.astype(F32) for g in groups], axis=0).astype(BF16)
+    else:
+        pick_ref[...] = jnp.zeros(pick_ref.shape, BF16)
+    row = iota(near_pick_ref.shape[1:], 0)
+    own_branch = branch * subs * leaves - subs * leaves
+    outside = (row + own_branch < 0) | (row + own_branch >= branches * subs * leaves)
+    for l in range(leaves):
+        near_pick_ref[l] = (jnp.where(outside, -1, row) == near_ids[0:1, l : l + 1]).astype(F32)
+    row = iota(far_pick_ref.shape[1:], 0)
+    for s in range(2):
+        for l in range(leaves):
+            far_pick_ref[s * leaves + l] = (row == far_ids[s : s + 1, l : l + 1]).astype(F32)
+    row = iota(top_pick_ref.shape[1:], 0)
+    for s in range(4):
+        top_pick_ref[s] = (row == top_ids[0:1, s : s + 1]).astype(F32)
+
+
+def gather_rows(got_ref, near_pick_ref, far_pick_ref, top_pick_ref):
+    branches = top_pick_ref.shape[1]
+    leaves = got_ref.shape[2]
+    subs = got_ref.shape[0] // branches
+    branch = lax.axis_index("leaf").astype(jnp.int32)
+    near_by = [got_ref[sub * branches + branch, 2].astype(F32) for sub in range(subs)]
+    near_by = jnp.concatenate(near_by, axis=0)
+
+    def chosen(masks, rows):
+        return by_leaf(
+            [
+                jnp.broadcast_to(jnp.sum(mask * rows, axis=0, keepdims=True), (ROWS, 128))
+                for mask in masks
+            ]
+        )
+
+    group = [
+        chosen([far_pick_ref[s * leaves + l] for l in range(leaves)], near_by) for s in range(2)
+    ]
+    about = [jnp.maximum(branch - 1, 0), branch, jnp.minimum(branch + 1, branches - 1)]
+    halves = []
+    for part in range(2):
+        rows = [
+            got_ref[sub * branches + at, part].astype(F32) for at in about for sub in range(subs)
+        ]
+        halves.append(
+            chosen([near_pick_ref[l] for l in range(leaves)], jnp.concatenate(rows, axis=0))
+        )
+    other = jnp.concatenate(halves, axis=1)
+    sums = [
+        sum(got_ref[sub * branches + at, 2].astype(F32) for sub in range(subs))
+        for at in range(branches)
+    ]
+    for s in range(4):
+        row = sum(top_pick_ref[s, at : at + 1, :] * sums[at][:1, :] for at in range(branches))
+        group.append(jnp.broadcast_to(row, (ROWS, 128)))
+    total = sum(sums)
+    group.append(total[1:2, :] + total[2:3, :] + total[3:4, :])
+    return other, group
+
+
+def multiply(
+    own,
+    got_ref,
+    pick_ref,
+    near_pick_ref,
+    far_pick_ref,
+    top_pick_ref,
+    near_ref,
+    top_down_ref,
+    coupling_ref,
+    basis_ref,
+):
     leaves, rank, size = basis_ref.shape
-    got = [got_ref[:, part].reshape(-1, 128) for part in range(3)]
-    pick = pick_ref[...]
-    rest = dot_nn(pick[ROWS:], got[2])
-    other = jnp.concatenate([dot_nn(pick[:ROWS], got[0]), dot_nn(pick[:ROWS], got[1])], axis=1)
+    if pick_ref.shape[0] == ROWS:
+        other, group = gather_rows(got_ref, near_pick_ref, far_pick_ref, top_pick_ref)
+    else:
+        got = [got_ref[:, part].reshape(-1, 128) for part in range(3)]
+        pick = pick_ref[...]
+        rest = dot_nn(pick[ROWS:], got[2])
+        other = jnp.concatenate([dot_nn(pick[:ROWS], half) for half in got[:2]], axis=1)
+        group = [rest[ROWS * g : ROWS * g + ROWS, :] for g in range(7)]
     near_out = own()
-    group = [rest[ROWS * g : ROWS * g + ROWS, :] for g in range(7)]
     low = iota((ROWS, 128), 1) < rank
     far_in = jnp.where(low, group[0], pltpu.roll(group[1], rank, 1)).astype(BF16)
     top_a = jnp.where(low, pltpu.roll(group[2], rank, 1), group[3]).astype(BF16)
@@ -193,6 +277,9 @@
     start2_ref,
     got_ref,
     pick_ref,
+    near_pick_ref,
+    far_pick_ref,
+    top_pick_ref,
     near_ref,
     top_down_ref,
     coupling_ref,
@@ -204,7 +291,16 @@
 ):
     start = start2_ref[...]
     image, dots = multiply(
-        lambda: own_part(start, near_ref), got_ref, pick_ref, near_ref, top_down_ref, coupling_ref, basis_ref
+        lambda: own_part(start, near_ref),
+        got_ref,
+        pick_ref,
+        near_pick_ref,
+        far_pick_ref,
+        top_pick_ref,
+        near_ref,
+        top_down_ref,
+        coupling_ref,
+        basis_ref,
     )
     scale = lax.rsqrt(dots[0] * (1.0 / total) + 1e-06)
     b0 = scale * start
@@ -223,6 +319,9 @@
     table_in_ref,
     got_ref,
     pick_ref,
+    near_pick_ref,
+    far_pick_ref,
+    top_pick_ref,
     near_ref,
     top_down_ref,
     coupling_ref,
@@ -238,6 +337,9 @@
         lambda: own_part(k1, near_ref),
         got_ref,
         pick_ref,
+        near_pick_ref,
+        far_pick_ref,
+        top_pick_ref,
         near_ref,
         top_down_ref,
         coupling_ref,
@@ -267,6 +369,9 @@
     table_in_ref,
     got_ref,
     pick_ref,
+    near_pick_ref,
+    far_pick_ref,
+    top_pick_ref,
     near_ref,
     top_down_ref,
     coupling_ref,
@@ -281,6 +386,9 @@
         lambda: own_part(k2, near_ref),
         got_ref,
         pick_ref,
+        near_pick_ref,
+        far_pick_ref,
+        top_pick_ref,
         near_ref,
         top_down_ref,
         coupling_ref,
@@ -378,28 +486,32 @@
         [table],
         pl.CostEstimate(flops=5000000000, bytes_accessed=20000000, transcendentals=0),
     )()
-    out, reach2, start2, pick, top_down = call(
+    picks = ROWS if devices <= 64 else 8 * ROWS
+    out, reach2, start2, pick, top_down, near_pick, far_pick, top_pick = call(
         lambda *refs: first_kernel(subs, *refs),
         [VMEM] * (len(sources) + 1),
         [
             blocks,
             shaped((2 * rank, leaves * rank), BF16),
             vec,
-            shaped((8 * ROWS, devices * leaves), BF16),
+            shaped((picks, devices * leaves), BF16),
             shaped((leaves * rank, top_coupling.shape[2]), BF16),
+            shaped((leaves, 3 * subs * leaves, 128)),
+            shaped((2 * leaves, subs * leaves, 128)),
+            shaped((4, devices // subs, 128)),
         ],
         pl.CostEstimate(flops=2000000000, bytes_accessed=20000000, transcendentals=0),
     )(*sources, heads)
-    fixed = (pick, near_blocks, top_down, leaf_coupling, leaf_basis)
+    fixed = (pick, near_pick, far_pick, top_pick, near_blocks, top_down, leaf_coupling, leaf_basis)
     out, b0, k1 = call(
-        lambda *refs: second_kernel(total, *refs), [VMEM] * 8, [blocks, vec, vec]
+        lambda *refs: second_kernel(total, *refs), [VMEM] * 11, [blocks, vec, vec]
     )(start2, exchange(out), *fixed, reach2)
     out, b1, k2, heads = call(
-        lambda *refs: third_kernel(total, *refs), [VMEM] * 10, [blocks, vec, vec, table]
+        lambda *refs: third_kernel(total, *refs), [VMEM] * 13, [blocks, vec, vec, table]
     )(b0, k1, heads, exchange(out), *fixed, reach2)
     dots, b2, w2, heads = call(
         lambda *refs: fourth_kernel(total, *refs),
-        [VMEM] * 11,
+        [VMEM] * 14,
         [shaped((devices, 1, 128)), vec, vec, table],
     )(b0, k1, b1, k2, heads, exchange(out), *fixed)
     basis, hessen = call(

time: 47.3 us -> 47.2 us (level)
  no operation moved by 1% of the time
where the time goes in v9:
time: 47.2 us; the launch traced here: 47 us
  blocking collectives  42.1 us (89%)
  Pallas kernels  3.2 us (7%)
  local copies, waits for them, and re-layouts  0.86 us (2%)
  between operations  0.78 us (2%)
    all_to_all x4, blocking collectives, exchange(): return lax.all_to_all(out, ('sub', 'leaf'), 0, 0, tiled=True)  42.1 us

profile of v9, /device:TPU:0, one launch (start us, length us, event | category | flops | bytes accessed | tf_op | source)
XLA Modules:
  0.0 47.0 jit_solution(9576273588967906790)
XLA Ops:
  0.6 0.0 copy-start.1
  0.6 0.0 copy-start.4
  0.7 0.0 copy-start.5
  0.7 0.0 copy-start.3
  0.7 0.0 copy-start.6
  0.7 0.0 copy-start.9
  0.7 0.0 copy-start.7
  0.7 0.0 copy-start.8
  0.7 0.8 %copy-done.1 = bf16[4,64,256]{2,1,0:T(8,128)(2,1)S(1)} copy-done((bf16[4,64,256]{2,1,0:T(8,128)(2,1)S(1)}, bf16[4,64,256]{2,1,0:T(8,128)(2,1)}, u32[]{:S(2)}) %copy-start.1) | copy-done | bytes 131096
  1.5 0.0 copy-done.4
  1.5 0.0 copy-done.5
  1.5 0.0 copy-done.3
  1.5 0.0 copy-done.6
  1.6 0.0 copy-done.9
  1.6 0.0 copy-done.7
  1.6 0.0 copy-done.8
  1.6 0.0 copy-start
  1.6 0.4 shard_map.114
  2.0 0.0 copy-start.2
  2.0 14.7 %all_to_all.20.refs_1_ = bf16[32,3,4,128]{3,2,1,0:T(4,128)(2,1)S(1)} all-to-all(bf16[32,3,4,128]{3,2,1,0:T(4,128)(2,1)S(1)} %get-tuple-element.22), channel_id=1, replica_groups=mesh['leaf'=8,'sub'=4] {'sub','leaf'}, dimensions={0} | all-to-all | bytes 196608 | tf_op jit(solution)/shard_map/all_to_all | solution.py:471
  16.6 0.0 copy-done
  16.6 0.0 copy-done.2
  16.7 0.7 %shard_map.115 = (bf16[32,3,4,128]{3,2,1,0:T(4,128)(2,1)S(1)}, f32[8,256]{1,0:T(8,128)S(1)}, f32[8,256]{1,0:T(8,128)S(1)}) custom-call(f32[8,256]{1,0:T(8,128)S(1)} %get-tuple-element.21.refs_0_, bf16[32,3,4,128]{3,2,1,0:T(4,128)(2,1)S(1)} %all_to_all.20.refs_1_, bf16[8,128]{1,0:T(8,128)(2,1)S(1)} %get-tuple-element.23.refs_2_.refs_4_.refs_6_, ...), custom_call_target="tpu_custom_call" | custom-call | tf_op jit(solution)/shard_map/pallas_call | solution.py:506
  17.4 9.3 %all_to_all.21.refs_3_ = bf16[32,3,4,128]{3,2,1,0:T(4,128)(2,1)S(1)} all-to-all(bf16[32,3,4,128]{3,2,1,0:T(4,128)(2,1)S(1)} %get-tuple-element.31), channel_id=1, replica_groups=mesh['leaf'=8,'sub'=4] {'sub','leaf'}, dimensions={0} | all-to-all | bytes 196608 | tf_op jit(solution)/shard_map/all_to_all | solution.py:471
  26.7 0.7 %shard_map.116 = (bf16[32,3,4,128]{3,2,1,0:T(4,128)(2,1)S(1)}, f32[8,256]{1,0:T(8,128)S(1)}, f32[8,256]{1,0:T(8,128)S(1)}, f32[8,128]{1,0:T(8,128)S(1)}) custom-call(f32[8,256]{1,0:T(8,128)S(1)} %get-tuple-element.29.refs_0_, f32[8,256]{1,0:T(8,128)S(1)} %get-tuple-element.30.refs_1_, f32[8,128]{1,0:T(8,128)S(1)} %shard_map.113.refs_8_.refs_2_, ...), custom_call_target="tpu_custom_call" | custom-call | tf_op jit(solution)/shard_map/pallas_call | solution.py:509
  27.4 9.3 %all_to_all.22.refs_5_ = bf16[32,3,4,128]{3,2,1,0:T(4,128)(2,1)S(1)} all-to-all(bf16[32,3,4,128]{3,2,1,0:T(4,128)(2,1)S(1)} %get-tuple-element.35), channel_id=1, replica_groups=mesh['leaf'=8,'sub'=4] {'sub','leaf'}, dimensions={0} | all-to-all | bytes 196608 | tf_op jit(solution)/shard_map/all_to_all | solution.py:471
  36.7 0.6 %shard_map.117 = (f32[32,1,128]{2,1,0:T(1,128)S(1)}, f32[8,256]{1,0:T(8,128)S(1)}, f32[8,256]{1,0:T(8,128)S(1)}, f32[8,128]{1,0:T(8,128)S(1)}) custom-call(f32[8,256]{1,0:T(8,128)S(1)} %get-tuple-element.29.refs_0_, f32[8,256]{1,0:T(8,128)S(1)} %get-tuple-element.30.refs_1_, f32[8,256]{1,0:T(8,128)S(1)} %get-tuple-element.32.refs_2_.refs_1_, ...), custom_call_target="tpu_custom_call" | custom-call | tf_op jit(solution)/shard_map/pallas_call | solution.py:512
  37.3 8.9 %all_to_all.23.refs_5_ = f32[32,1,128]{2,1,0:T(1,128)S(1)} all-to-all(f32[32,1,128]{2,1,0:T(1,128)S(1)} %get-tuple-element.39), channel_id=1, replica_groups=mesh['leaf'=8,'sub'=4] {'sub','leaf'}, dimensions={0} | all-to-all | bytes 32768 | tf_op jit(solution)/shard_map/all_to_all | solution.py:471
  46.1 0.8 %shard_map.118 = (f32[4,4,256]{2,1,0:T(4,128)}, f32[4,3]{1,0:T(4,128)}) custom-call(f32[8,256]{1,0:T(8,128)S(1)} %get-tuple-element.29.refs_0_, f32[8,256]{1,0:T(8,128)S(1)} %get-tuple-element.32.refs_2_.refs_1_, f32[8,256]{1,0:T(8,128)S(1)} %get-tuple-element.36.refs_2_, f32[8,256]{1,0:T(8,128)S(1)} %get-tuple-element.37.refs_3_, ...), custom_call_target="tpu_custom_call" | custom-call | tf_op jit(solution)/shard_map/pallas_call | solution.py:517
  (1 shorter events, 0.0 us)
Async XLA Ops:
  0.6 0.9 %copy-start.1 = (bf16[4,64,256]{2,1,0:T(8,128)(2,1)S(1)}, bf16[4,64,256]{2,1,0:T(8,128)(2,1)}, u32[]{:S(2)}) copy-start(bf16[4,64,256]{2,1,0:T(8,128)(2,1)} %refs_13_.1) | copy-start | bytes 393220
  0.6 0.9 %copy-start.4 = (bf16[1,64,256]{2,1,0:T(8,128)(2,1)S(1)}, bf16[1,64,256]{2,1,0:T(8,128)(2,1)}, u32[]{:S(2)}) copy-start(bf16[1,64,256]{2,1,0:T(8,128)(2,1)} %refs_4_.1) | copy-start | bytes 98308
  0.7 0.9 %copy-start.5 = (bf16[1,64,64]{2,1,0:T(8,128)(2,1)S(1)}, bf16[1,64,64]{2,1,0:T(8,128)(2,1)}, u32[]{:S(2)}) copy-start(bf16[1,64,64]{2,1,0:T(8,128)(2,1)} %refs_3_.1) | copy-start | bytes 24580
  0.7 0.9 %copy-start.3 = (bf16[1,64,256]{2,1,0:T(8,128)(2,1)S(1)}, bf16[1,64,256]{2,1,0:T(8,128)(2,1)}, u32[]{:S(2)}) copy-start(bf16[1,64,256]{2,1,0:T(8,128)(2,1)} %refs_2_.1) | copy-start | bytes 98308
  0.7 0.9 %copy-start.6 = (f32[4,256]{1,0:T(4,128)S(1)}, f32[4,256]{1,0:T(4,128)}, u32[]{:S(2)}) copy-start(f32[4,256]{1,0:T(4,128)} %refs_0_.1) | copy-start | bytes 12292
  0.7 0.9 %copy-start.9 = (s32[1,4]{1,0:T(1,128)S(1)}, s32[1,4]{1,0:T(1,128)}, u32[]{:S(2)}) copy-start(s32[1,4]{1,0:T(1,128)} %refs_7_.1) | copy-start | bytes 52
  0.7 0.9 %copy-start.7 = (s32[4,2]{0,1:T(2,128)S(1)}, s32[4,2]{0,1:T(2,128)}, u32[]{:S(2)}) copy-start(s32[4,2]{0,1:T(2,128)} %param.13) | copy-start | bytes 100
  0.7 0.9 %copy-start.8 = (s32[4,1]{0,1:T(1,128)S(1)}, s32[4,1]{0,1:T(1,128)}, u32[]{:S(2)}) copy-start(s32[4,1]{0,1:T(1,128)} %param.12) | copy-start | bytes 52
  1.6 15.1 %copy-start = (bf16[4,2,256,256]{3,2,1,0:T(8,128)(2,1)S(1)}, bf16[4,2,256,256]{3,2,1,0:T(8,128)(2,1)}, u32[]{:S(2)}) copy-start(bf16[4,2,256,256]{3,2,1,0:T(8,128)(2,1)} %refs_10_.3) | copy-start | bytes 3145732
  2.0 14.7 %copy-start.2 = (bf16[4,64,128]{2,1,0:T(8,128)(2,1)S(1)}, bf16[4,64,128]{2,1,0:T(8,128)(2,1)}, u32[]{:S(2)}) copy-start(bf16[4,64,128]{2,1,0:T(8,128)(2,1)} %refs_12_.1) | copy-start | bytes 196612

commit v10 on v9

--- a/solution.py
+++ b/solution.py
@@ -97,7 +97,6 @@
     basis_ref,
     node_ref,
     upper_ref,
-    top_ref,
     near_ids_ref,
     far_ids_ref,
     top_ids_ref,
@@ -106,7 +105,6 @@
     reach2_ref,
     start2_ref,
     pick_ref,
-    top_down_ref,
     near_pick_ref,
     far_pick_ref,
     top_pick_ref,
@@ -127,7 +125,6 @@
     start = twice(start_ref[...])
     start2_ref[...] = start
     store_all(make_block(start, [inner(start, start)], basis_ref[...], reach2), block_ref)
-    top_down_ref[...] = dot_tn(reach.astype(BF16), top_ref[0]).astype(BF16)
 
 
 def own_part(vec, near_ref):
@@ -281,15 +278,17 @@
     far_pick_ref,
     top_pick_ref,
     near_ref,
-    top_down_ref,
+    top_ref,
     coupling_ref,
     basis_ref,
     reach2_ref,
     block_ref,
     b0_ref,
     k1_ref,
+    top_down_ref,
 ):
     start = start2_ref[...]
+    top_down_ref[...] = dot_tn(reach2_ref[: basis_ref.shape[1], :], top_ref[0]).astype(BF16)
     image, dots = multiply(
         lambda: own_part(start, near_ref),
         got_ref,
@@ -475,7 +474,6 @@
         leaf_basis,
         node_transfer,
         branch_transfer,
-        top_coupling,
         near_ids.T,
         far_ids.T,
         top_ids,
@@ -487,7 +485,7 @@
         pl.CostEstimate(flops=5000000000, bytes_accessed=20000000, transcendentals=0),
     )()
     picks = ROWS if devices <= 64 else 8 * ROWS
-    out, reach2, start2, pick, top_down, near_pick, far_pick, top_pick = call(
+    out, reach2, start2, pick, near_pick, far_pick, top_pick = call(
         lambda *refs: first_kernel(subs, *refs),
         [VMEM] * (len(sources) + 1),
         [
@@ -495,17 +493,19 @@
             shaped((2 * rank, leaves * rank), BF16),
             vec,
             shaped((picks, devices * leaves), BF16),
-            shaped((leaves * rank, top_coupling.shape[2]), BF16),
             shaped((leaves, 3 * subs * leaves, 128)),
             shaped((2 * leaves, subs * leaves, 128)),
             shaped((4, devices // subs, 128)),
         ],
         pl.CostEstimate(flops=2000000000, bytes_accessed=20000000, transcendentals=0),
     )(*sources, heads)
-    fixed = (pick, near_pick, far_pick, top_pick, near_blocks, top_down, leaf_coupling, leaf_basis)
-    out, b0, k1 = call(
-        lambda *refs: second_kernel(total, *refs), [VMEM] * 11, [blocks, vec, vec]
-    )(start2, exchange(out), *fixed, reach2)
+    picked = (pick, near_pick, far_pick, top_pick, near_blocks)
+    out, b0, k1, top_down = call(
+        lambda *refs: second_kernel(total, *refs),
+        [VMEM] * 11,
+        [blocks, vec, vec, shaped((leaves * rank, top_coupling.shape[2]), BF16)],
+    )(start2, exchange(out), *picked, top_coupling, leaf_coupling, leaf_basis, reach2)
+    fixed = (*picked, top_down, leaf_coupling, leaf_basis)
     out, b1, k2, heads = call(
         lambda *refs: third_kernel(total, *refs), [VMEM] * 13, [blocks, vec, vec, table]
     )(b0, k1, heads, exchange(out), *fixed, reach2)

time: 47.2 us -> 47.2 us (level)
  no operation moved by 1% of the time
where the time goes in v10:
time: 47.2 us; the launch traced here: 47 us
  blocking collectives  42.1 us (89%)
  Pallas kernels  3.21 us (7%)
  local copies, waits for them, and re-layouts  0.87 us (2%)
  between operations  0.77 us (2%)
    all_to_all x4, blocking collectives, exchange(): return lax.all_to_all(out, ('sub', 'leaf'), 0, 0, tiled=True)  42.1 us

profile of v10, /device:TPU:0, one launch (start us, length us, event | category | flops | bytes accessed | tf_op | source)
XLA Modules:
  0.0 47.0 jit_solution(10333269504621109312)
XLA Ops:
  0.6 0.0 copy-start.1
  0.6 0.0 copy-start.5
  0.7 0.0 copy-start.4
  0.7 0.0 copy-start.6
  0.7 0.0 copy-start.9
  0.7 0.0 copy-start.7
  0.7 0.0 copy-start.8
  0.7 0.8 %copy-done.1 = bf16[4,64,256]{2,1,0:T(8,128)(2,1)S(1)} copy-done((bf16[4,64,256]{2,1,0:T(8,128)(2,1)S(1)}, bf16[4,64,256]{2,1,0:T(8,128)(2,1)}, u32[]{:S(2)}) %copy-start.1) | copy-done | bytes 131096
  1.5 0.0 copy-done.5
  1.5 0.0 copy-done.4
  1.5 0.0 copy-done.6
  1.5 0.0 copy-done.9
  1.5 0.0 copy-done.7
  1.6 0.0 copy-done.8
  1.6 0.0 copy-start
  1.6 0.0 copy-start.3
  1.6 0.3 shard_map.114
  1.9 0.0 copy-start.2
  1.9 14.7 %all_to_all.20.refs_1_ = bf16[32,3,4,128]{3,2,1,0:T(4,128)(2,1)S(1)} all-to-all(bf16[32,3,4,128]{3,2,1,0:T(4,128)(2,1)S(1)} %get-tuple-element.22), channel_id=1, replica_groups=mesh['leaf'=8,'sub'=4] {'sub','leaf'}, dimensions={0} | all-to-all | bytes 196608 | tf_op jit(solution)/shard_map/all_to_all | solution.py:470
  16.6 0.0 copy-done
  16.6 0.0 copy-done.3
  16.6 0.0 copy-done.2
  16.6 0.8 %shard_map.115 = (bf16[32,3,4,128]{3,2,1,0:T(4,128)(2,1)S(1)}, f32[8,256]{1,0:T(8,128)S(1)}, f32[8,256]{1,0:T(8,128)S(1)}, bf16[256,256]{1,0:T(8,128)(2,1)S(1)}) custom-call(f32[8,256]{1,0:T(8,128)S(1)} %get-tuple-element.21.refs_0_, bf16[32,3,4,128]{3,2,1,0:T(4,128)(2,1)S(1)} %all_to_all.20.refs_1_, ...), custom_call_target="tpu_custom_call" | custom-call | tf_op jit(solution)/shard_map/pallas_call | solution.py:503
  17.4 9.3 %all_to_all.21.refs_3_ = bf16[32,3,4,128]{3,2,1,0:T(4,128)(2,1)S(1)} all-to-all(bf16[32,3,4,128]{3,2,1,0:T(4,128)(2,1)S(1)} %get-tuple-element.30), channel_id=1, replica_groups=mesh['leaf'=8,'sub'=4] {'sub','leaf'}, dimensions={0} | all-to-all | bytes 196608 | tf_op jit(solution)/shard_map/all_to_all | solution.py:470
  26.7 0.7 %shard_map.116 = (bf16[32,3,4,128]{3,2,1,0:T(4,128)(2,1)S(1)}, f32[8,256]{1,0:T(8,128)S(1)}, f32[8,256]{1,0:T(8,128)S(1)}, f32[8,128]{1,0:T(8,128)S(1)}) custom-call(f32[8,256]{1,0:T(8,128)S(1)} %get-tuple-element.28.refs_0_, f32[8,256]{1,0:T(8,128)S(1)} %get-tuple-element.29.refs_1_, f32[8,128]{1,0:T(8,128)S(1)} %shard_map.113.refs_7_.refs_2_, ...), custom_call_target="tpu_custom_call" | custom-call | tf_op jit(solution)/shard_map/pallas_call | solution.py:509
  27.4 9.3 %all_to_all.22.refs_5_ = bf16[32,3,4,128]{3,2,1,0:T(4,128)(2,1)S(1)} all-to-all(bf16[32,3,4,128]{3,2,1,0:T(4,128)(2,1)S(1)} %get-tuple-element.35), channel_id=1, replica_groups=mesh['leaf'=8,'sub'=4] {'sub','leaf'}, dimensions={0} | all-to-all | bytes 196608 | tf_op jit(solution)/shard_map/all_to_all | solution.py:470
  36.7 0.6 %shard_map.117 = (f32[32,1,128]{2,1,0:T(1,128)S(1)}, f32[8,256]{1,0:T(8,128)S(1)}, f32[8,256]{1,0:T(8,128)S(1)}, f32[8,128]{1,0:T(8,128)S(1)}) custom-call(f32[8,256]{1,0:T(8,128)S(1)} %get-tuple-element.28.refs_0_, f32[8,256]{1,0:T(8,128)S(1)} %get-tuple-element.29.refs_1_, f32[8,256]{1,0:T(8,128)S(1)} %get-tuple-element.32.refs_2_.refs_1_, ...), custom_call_target="tpu_custom_call" | custom-call | tf_op jit(solution)/shard_map/pallas_call | solution.py:512
  37.3 8.9 %all_to_all.23.refs_5_ = f32[32,1,128]{2,1,0:T(1,128)S(1)} all-to-all(f32[32,1,128]{2,1,0:T(1,128)S(1)} %get-tuple-element.39), channel_id=1, replica_groups=mesh['leaf'=8,'sub'=4] {'sub','leaf'}, dimensions={0} | all-to-all | bytes 32768 | tf_op jit(solution)/shard_map/all_to_all | solution.py:470
  46.2 0.8 %shard_map.118 = (f32[4,4,256]{2,1,0:T(4,128)}, f32[4,3]{1,0:T(4,128)}) custom-call(f32[8,256]{1,0:T(8,128)S(1)} %get-tuple-element.28.refs_0_, f32[8,256]{1,0:T(8,128)S(1)} %get-tuple-element.32.refs_2_.refs_1_, f32[8,256]{1,0:T(8,128)S(1)} %get-tuple-element.36.refs_2_, f32[8,256]{1,0:T(8,128)S(1)} %get-tuple-element.37.refs_3_, ...), custom_call_target="tpu_custom_call" | custom-call | tf_op jit(solution)/shard_map/pallas_call | solution.py:517
  (1 shorter events, 0.0 us)
Async XLA Ops:
  0.6 0.9 %copy-start.1 = (bf16[4,64,256]{2,1,0:T(8,128)(2,1)S(1)}, bf16[4,64,256]{2,1,0:T(8,128)(2,1)}, u32[]{:S(2)}) copy-start(bf16[4,64,256]{2,1,0:T(8,128)(2,1)} %refs_13_.1) | copy-start | bytes 393220
  0.6 0.9 %copy-start.5 = (bf16[1,64,64]{2,1,0:T(8,128)(2,1)S(1)}, bf16[1,64,64]{2,1,0:T(8,128)(2,1)}, u32[]{:S(2)}) copy-start(bf16[1,64,64]{2,1,0:T(8,128)(2,1)} %refs_3_.1) | copy-start | bytes 24580
  0.7 0.9 %copy-start.4 = (bf16[1,64,256]{2,1,0:T(8,128)(2,1)S(1)}, bf16[1,64,256]{2,1,0:T(8,128)(2,1)}, u32[]{:S(2)}) copy-start(bf16[1,64,256]{2,1,0:T(8,128)(2,1)} %refs_2_.1) | copy-start | bytes 98308
  0.7 0.9 %copy-start.6 = (f32[4,256]{1,0:T(4,128)S(1)}, f32[4,256]{1,0:T(4,128)}, u32[]{:S(2)}) copy-start(f32[4,256]{1,0:T(4,128)} %refs_0_.1) | copy-start | bytes 12292
  0.7 0.9 %copy-start.9 = (s32[1,4]{1,0:T(1,128)S(1)}, s32[1,4]{1,0:T(1,128)}, u32[]{:S(2)}) copy-start(s32[1,4]{1,0:T(1,128)} %refs_6_.2) | copy-start | bytes 52
  0.7 0.9 %copy-start.7 = (s32[4,2]{0,1:T(2,128)S(1)}, s32[4,2]{0,1:T(2,128)}, u32[]{:S(2)}) copy-start(s32[4,2]{0,1:T(2,128)} %param.13) | copy-start | bytes 100
  0.7 0.9 %copy-start.8 = (s32[4,1]{0,1:T(1,128)S(1)}, s32[4,1]{0,1:T(1,128)}, u32[]{:S(2)}) copy-start(s32[4,1]{0,1:T(1,128)} %param.12) | copy-start | bytes 52
  1.6 15.0 %copy-start = (bf16[4,2,256,256]{3,2,1,0:T(8,128)(2,1)S(1)}, bf16[4,2,256,256]{3,2,1,0:T(8,128)(2,1)}, u32[]{:S(2)}) copy-start(bf16[4,2,256,256]{3,2,1,0:T(8,128)(2,1)} %refs_10_.3) | copy-start | bytes 3145732
  1.6 15.0 %copy-start.3 = (bf16[1,64,256]{2,1,0:T(8,128)(2,1)S(1)}, bf16[1,64,256]{2,1,0:T(8,128)(2,1)}, u32[]{:S(2)}) copy-start(bf16[1,64,256]{2,1,0:T(8,128)(2,1)} %refs_7_.1) | copy-start | bytes 98308
  1.9 14.7 %copy-start.2 = (bf16[4,64,128]{2,1,0:T(8,128)(2,1)S(1)}, bf16[4,64,128]{2,1,0:T(8,128)(2,1)}, u32[]{:S(2)}) copy-start(bf16[4,64,128]{2,1,0:T(8,128)(2,1)} %refs_12_.1) | copy-start | bytes 196612

commit v11 on v9

--- a/solution.py
+++ b/solution.py
@@ -236,14 +236,15 @@
 ):
     leaves, rank, size = basis_ref.shape
     if pick_ref.shape[0] == ROWS:
+        near_out = own()
         other, group = gather_rows(got_ref, near_pick_ref, far_pick_ref, top_pick_ref)
     else:
         got = [got_ref[:, part].reshape(-1, 128) for part in range(3)]
         pick = pick_ref[...]
         rest = dot_nn(pick[ROWS:], got[2])
         other = jnp.concatenate([dot_nn(pick[:ROWS], half) for half in got[:2]], axis=1)
+        near_out = own()
         group = [rest[ROWS * g : ROWS * g + ROWS, :] for g in range(7)]
-    near_out = own()
     low = iota((ROWS, 128), 1) < rank
     far_in = jnp.where(low, group[0], pltpu.roll(group[1], rank, 1)).astype(BF16)
     top_a = jnp.where(low, pltpu.roll(group[2], rank, 1), group[3]).astype(BF16)

time: 47.2 us -> 47.2 us (level)
  no operation moved by 1% of the time
where the time goes in v11:
time: 47.2 us; the launch traced here: 47 us
  blocking collectives  42.1 us (89%)
  Pallas kernels  3.2 us (7%)
  local copies, waits for them, and re-layouts  0.86 us (2%)
  between operations  0.78 us (2%)
    all_to_all x4, blocking collectives, exchange(): return lax.all_to_all(out, ('sub', 'leaf'), 0, 0, tiled=True)  42.1 us

profile of v11, /device:TPU:0, one launch (start us, length us, event | category | flops | bytes accessed | tf_op | source)
XLA Modules:
  0.0 47.0 jit_solution(9576273588967906790)
XLA Ops:
  0.6 0.0 copy-start.1
  0.6 0.0 copy-start.4
  0.7 0.0 copy-start.5
  0.7 0.0 copy-start.3
  0.7 0.0 copy-start.6
  0.7 0.0 copy-start.9
  0.7 0.0 copy-start.7
  0.7 0.0 copy-start.8
  0.7 0.8 %copy-done.1 = bf16[4,64,256]{2,1,0:T(8,128)(2,1)S(1)} copy-done((bf16[4,64,256]{2,1,0:T(8,128)(2,1)S(1)}, bf16[4,64,256]{2,1,0:T(8,128)(2,1)}, u32[]{:S(2)}) %copy-start.1) | copy-done | bytes 131096
  1.5 0.0 copy-done.4
  1.5 0.0 copy-done.5
  1.5 0.0 copy-done.3
  1.5 0.0 copy-done.6
  1.6 0.0 copy-done.9
  1.6 0.0 copy-done.7
  1.6 0.0 copy-done.8
  1.6 0.0 copy-start
  1.6 0.4 shard_map.114
  2.0 0.0 copy-start.2
  2.0 14.7 %all_to_all.20.refs_1_ = bf16[32,3,4,128]{3,2,1,0:T(4,128)(2,1)S(1)} all-to-all(bf16[32,3,4,128]{3,2,1,0:T(4,128)(2,1)S(1)} %get-tuple-element.22), channel_id=1, replica_groups=mesh['leaf'=8,'sub'=4] {'sub','leaf'}, dimensions={0} | all-to-all | bytes 196608 | tf_op jit(solution)/shard_map/all_to_all | solution.py:472
  16.6 0.0 copy-done
  16.6 0.0 copy-done.2
  16.7 0.7 %shard_map.115 = (bf16[32,3,4,128]{3,2,1,0:T(4,128)(2,1)S(1)}, f32[8,256]{1,0:T(8,128)S(1)}, f32[8,256]{1,0:T(8,128)S(1)}) custom-call(f32[8,256]{1,0:T(8,128)S(1)} %get-tuple-element.21.refs_0_, bf16[32,3,4,128]{3,2,1,0:T(4,128)(2,1)S(1)} %all_to_all.20.refs_1_, bf16[8,128]{1,0:T(8,128)(2,1)S(1)} %get-tuple-element.23.refs_2_.refs_4_.refs_6_, ...), custom_call_target="tpu_custom_call" | custom-call | tf_op jit(solution)/shard_map/pallas_call | solution.py:507
  17.4 9.3 %all_to_all.21.refs_3_ = bf16[32,3,4,128]{3,2,1,0:T(4,128)(2,1)S(1)} all-to-all(bf16[32,3,4,128]{3,2,1,0:T(4,128)(2,1)S(1)} %get-tuple-element.31), channel_id=1, replica_groups=mesh['leaf'=8,'sub'=4] {'sub','leaf'}, dimensions={0} | all-to-all | bytes 196608 | tf_op jit(solution)/shard_map/all_to_all | solution.py:472
  26.7 0.7 %shard_map.116 = (bf16[32,3,4,128]{3,2,1,0:T(4,128)(2,1)S(1)}, f32[8,256]{1,0:T(8,128)S(1)}, f32[8,256]{1,0:T(8,128)S(1)}, f32[8,128]{1,0:T(8,128)S(1)}) custom-call(f32[8,256]{1,0:T(8,128)S(1)} %get-tuple-element.29.refs_0_, f32[8,256]{1,0:T(8,128)S(1)} %get-tuple-element.30.refs_1_, f32[8,128]{1,0:T(8,128)S(1)} %shard_map.113.refs_8_.refs_2_, ...), custom_call_target="tpu_custom_call" | custom-call | tf_op jit(solution)/shard_map/pallas_call | solution.py:510
  27.4 9.3 %all_to_all.22.refs_5_ = bf16[32,3,4,128]{3,2,1,0:T(4,128)(2,1)S(1)} all-to-all(bf16[32,3,4,128]{3,2,1,0:T(4,128)(2,1)S(1)} %get-tuple-element.35), channel_id=1, replica_groups=mesh['leaf'=8,'sub'=4] {'sub','leaf'}, dimensions={0} | all-to-all | bytes 196608 | tf_op jit(solution)/shard_map/all_to_all | solution.py:472
  36.7 0.6 %shard_map.117 = (f32[32,1,128]{2,1,0:T(1,128)S(1)}, f32[8,256]{1,0:T(8,128)S(1)}, f32[8,256]{1,0:T(8,128)S(1)}, f32[8,128]{1,0:T(8,128)S(1)}) custom-call(f32[8,256]{1,0:T(8,128)S(1)} %get-tuple-element.29.refs_0_, f32[8,256]{1,0:T(8,128)S(1)} %get-tuple-element.30.refs_1_, f32[8,256]{1,0:T(8,128)S(1)} %get-tuple-element.32.refs_2_.refs_1_, ...), custom_call_target="tpu_custom_call" | custom-call | tf_op jit(solution)/shard_map/pallas_call | solution.py:513
  37.3 8.9 %all_to_all.23.refs_5_ = f32[32,1,128]{2,1,0:T(1,128)S(1)} all-to-all(f32[32,1,128]{2,1,0:T(1,128)S(1)} %get-tuple-element.39), channel_id=1, replica_groups=mesh['leaf'=8,'sub'=4] {'sub','leaf'}, dimensions={0} | all-to-all | bytes 32768 | tf_op jit(solution)/shard_map/all_to_all | solution.py:472
  46.1 0.8 %shard_map.118 = (f32[4,4,256]{2,1,0:T(4,128)}, f32[4,3]{1,0:T(4,128)}) custom-call(f32[8,256]{1,0:T(8,128)S(1)} %get-tuple-element.29.refs_0_, f32[8,256]{1,0:T(8,128)S(1)} %get-tuple-element.32.refs_2_.refs_1_, f32[8,256]{1,0:T(8,128)S(1)} %get-tuple-element.36.refs_2_, f32[8,256]{1,0:T(8,128)S(1)} %get-tuple-element.37.refs_3_, ...), custom_call_target="tpu_custom_call" | custom-call | tf_op jit(solution)/shard_map/pallas_call | solution.py:518
  (1 shorter events, 0.0 us)
Async XLA Ops:
  0.6 0.9 %copy-start.1 = (bf16[4,64,256]{2,1,0:T(8,128)(2,1)S(1)}, bf16[4,64,256]{2,1,0:T(8,128)(2,1)}, u32[]{:S(2)}) copy-start(bf16[4,64,256]{2,1,0:T(8,128)(2,1)} %refs_13_.1) | copy-start | bytes 393220
  0.6 0.9 %copy-start.4 = (bf16[1,64,256]{2,1,0:T(8,128)(2,1)S(1)}, bf16[1,64,256]{2,1,0:T(8,128)(2,1)}, u32[]{:S(2)}) copy-start(bf16[1,64,256]{2,1,0:T(8,128)(2,1)} %refs_4_.1) | copy-start | bytes 98308
  0.7 0.9 %copy-start.5 = (bf16[1,64,64]{2,1,0:T(8,128)(2,1)S(1)}, bf16[1,64,64]{2,1,0:T(8,128)(2,1)}, u32[]{:S(2)}) copy-start(bf16[1,64,64]{2,1,0:T(8,128)(2,1)} %refs_3_.1) | copy-start | bytes 24580
  0.7 0.9 %copy-start.3 = (bf16[1,64,256]{2,1,0:T(8,128)(2,1)S(1)}, bf16[1,64,256]{2,1,0:T(8,128)(2,1)}, u32[]{:S(2)}) copy-start(bf16[1,64,256]{2,1,0:T(8,128)(2,1)} %refs_2_.1) | copy-start | bytes 98308
  0.7 0.9 %copy-start.6 = (f32[4,256]{1,0:T(4,128)S(1)}, f32[4,256]{1,0:T(4,128)}, u32[]{:S(2)}) copy-start(f32[4,256]{1,0:T(4,128)} %refs_0_.1) | copy-start | bytes 12292
  0.7 0.9 %copy-start.9 = (s32[1,4]{1,0:T(1,128)S(1)}, s32[1,4]{1,0:T(1,128)}, u32[]{:S(2)}) copy-start(s32[1,4]{1,0:T(1,128)} %refs_7_.1) | copy-start | bytes 52
  0.7 0.9 %copy-start.7 = (s32[4,2]{0,1:T(2,128)S(1)}, s32[4,2]{0,1:T(2,128)}, u32[]{:S(2)}) copy-start(s32[4,2]{0,1:T(2,128)} %param.13) | copy-start | bytes 100
  0.7 0.9 %copy-start.8 = (s32[4,1]{0,1:T(1,128)S(1)}, s32[4,1]{0,1:T(1,128)}, u32[]{:S(2)}) copy-start(s32[4,1]{0,1:T(1,128)} %param.12) | copy-start | bytes 52
  1.6 15.1 %copy-start = (bf16[4,2,256,256]{3,2,1,0:T(8,128)(2,1)S(1)}, bf16[4,2,256,256]{3,2,1,0:T(8,128)(2,1)}, u32[]{:S(2)}) copy-start(bf16[4,2,256,256]{3,2,1,0:T(8,128)(2,1)} %refs_10_.3) | copy-start | bytes 3145732
  2.0 14.7 %copy-start.2 = (bf16[4,64,128]{2,1,0:T(8,128)(2,1)S(1)}, bf16[4,64,128]{2,1,0:T(8,128)(2,1)}, u32[]{:S(2)}) copy-start(bf16[4,64,128]{2,1,0:T(8,128)(2,1)} %refs_12_.1) | copy-start | bytes 196612
